TPU v7x, 32 devices: a whole 2x2x4 slice. The times are simulated.
32 devices in a mesh: section: 2 (over x), expert: 16 (over z, y, core).
Axes of the slice: x: 2, y: 2, z: 4, core: 2. Of those that a mesh axis runs over, the one named last changes fastest.
Arguments:
- fwd_act: bfloat16 [2, 128, 2048], P('section', 'expert'), may hold values from -6 to 6
- fwd_routes: int32 [2, 128, 8], P('section', 'expert'), may hold values from 0 to 15, all different within a row; in each aligned block of 8 rows (0 to 7, 8 to 15, ..., all dimensions but the last counted through in order) at most 8 rows name the same one
- bwd_saved: bfloat16 [2, 128, 2048], P('section', 'expert'), may hold values from -6 to 6
- bwd_grad: bfloat16 [2, 128, 2048], P('section', 'expert'), may hold values from -6 to 6
- bwd_routes: int32 [2, 128, 8], P('section', 'expert'), may hold values from 0 to 15, all different within a row; in each aligned block of 8 rows (0 to 7, 8 to 15, ..., all dimensions but the last counted through in order) at most 8 rows name the same one
- norm_gain: float32 [2, 2048], P('section'), may hold values from 0.1 to 1.9
- router: bfloat16 [2048, 16], replicated, may hold values from -0.125 to 0.125
- w_gate: bfloat16 [16, 2048, 768], P('expert'), may hold values from -0.125 to 0.125
- w_up: bfloat16 [16, 2048, 768], P('expert'), may hold values from -0.125 to 0.125
- w_down: bfloat16 [16, 768, 2048], P('expert'), may hold values from -0.875 to 0.875
Outputs:
- fwd_next: bfloat16 [2, 128, 2048], P('section', 'expert')
- grad_prev: bfloat16 [2, 128, 2048], P('section', 'expert')
Inputs may be any that keep to these rules, and one draw needn't show every extreme that they name: `fwd_routes`: each token names 8 different experts. Within one section, the 8 tokens of one expert-axis device (aligned blocks of rows) name any one expert at most 8 times, and in every draw some block names some expert exactly 8 times. `bwd_routes`: as for fwd_routes, drawn independently.
All inputs are finite; a program needn't handle non-finite values.
Results may differ from a plain program's by a relative error of at most 0.01.
Values may be sent and summed in bfloat16 or wider, within the bound.
No kernel may reach another device: no remote copies, remote signals or barrier semaphores. Data moves between devices by JAX's collectives and lax.ppermute only.
A program may use at most 64 MiB of HBM per device.

v0:
```python
import jax
import jax.numpy as jnp
from jax import lax
from jax.sharding import PartitionSpec as P

EPSILON = 1e-06


def shifted(block, axis, distance):
    devices = range(lax.axis_size(axis))
    route = [(i - distance, i) for i in devices if i - distance in devices]
    return lax.ppermute(block, axis, route)


def normalize(acts_in, gain_row):
    values = acts_in.astype(jnp.float32)
    factor = lax.rsqrt(jnp.mean(values * values, axis=-1, keepdims=True) + EPSILON)
    unit_rows = values * factor
    return ((unit_rows * gain_row).astype(jnp.bfloat16), unit_rows, factor)


def gate_values(normed, router, routes):
    logits = jnp.dot(normed, router, preferred_element_type=jnp.float32)
    chosen = jnp.take_along_axis(logits, routes, axis=1)
    raised = jnp.exp(chosen)
    return raised / jnp.sum(raised, axis=-1, keepdims=True)


def expert_forward(rows_in, gate_mat, up_mat, down_mat):
    pre_gate = jnp.dot(rows_in, gate_mat, preferred_element_type=jnp.float32)
    pre_up = jnp.dot(rows_in, up_mat, preferred_element_type=jnp.float32)
    sigma = jax.nn.sigmoid(pre_gate)
    hidden = (pre_gate * sigma * pre_up).astype(jnp.bfloat16)
    return jnp.dot(hidden, down_mat, preferred_element_type=jnp.float32).astype(jnp.bfloat16)


def expert_backward(rows_in, grads_in, gate_mat, up_mat, down_mat):
    pre_gate = jnp.dot(rows_in, gate_mat, preferred_element_type=jnp.float32)
    pre_up = jnp.dot(rows_in, up_mat, preferred_element_type=jnp.float32)
    sigma = jax.nn.sigmoid(pre_gate)
    silu_val = pre_gate * sigma
    hidden = (silu_val * pre_up).astype(jnp.bfloat16)
    expert_out = jnp.dot(hidden, down_mat, preferred_element_type=jnp.float32).astype(jnp.bfloat16)
    dgate = jnp.sum(grads_in.astype(jnp.float32) * expert_out.astype(jnp.float32), axis=-1).astype(
        jnp.bfloat16
    )
    contract = (((1,), (1,)), ((), ()))
    d_hidden = lax.dot_general(grads_in, down_mat, contract, preferred_element_type=jnp.float32)
    d_up = (d_hidden * silu_val).astype(jnp.bfloat16)
    d_pre = (d_hidden * pre_up * sigma * (1.0 + pre_gate * (1.0 - sigma))).astype(jnp.bfloat16)
    d_rows = lax.dot_general(d_pre, gate_mat, contract, preferred_element_type=jnp.float32)
    d_rows = d_rows + lax.dot_general(d_up, up_mat, contract, preferred_element_type=jnp.float32)
    return (d_rows.astype(jnp.bfloat16), dgate)


def input_gradient(gates, dgate, pair_grads, routes, router, unit_rows, factor, gain_row, grads_in):
    d_normed = jnp.sum(gates[:, :, None] * pair_grads, axis=1)
    d_chosen = gates * (dgate - jnp.sum(gates * dgate, axis=-1, keepdims=True))
    labels = jnp.arange(router.shape[1], dtype=jnp.int32)
    hits = (routes[:, :, None] == labels[None, None, :]).astype(jnp.float32)
    d_logits = jnp.sum(hits * d_chosen[:, :, None], axis=1)
    d_normed = d_normed + lax.dot_general(
        d_logits,
        router.astype(jnp.float32),
        (((1,), (1,)), ((), ())),
        precision=lax.Precision.HIGHEST,
    )
    d_unit = d_normed * gain_row
    result = factor * (d_unit - unit_rows * jnp.mean(d_unit * unit_rows, axis=-1, keepdims=True))
    return (result + grads_in.astype(jnp.float32)).astype(jnp.bfloat16)


def placement(routes, expert_count, capacity):
    flat_ids = routes.reshape(-1)
    labels = jnp.arange(expert_count, dtype=jnp.int32)
    onehot = (flat_ids[:, None] == labels[None, :]).astype(jnp.int32)
    before = jnp.cumsum(onehot, axis=0) - onehot
    slot_ids = jnp.sum(before * onehot, axis=1)
    target = flat_ids * capacity + slot_ids
    slot_labels = jnp.arange(expert_count * capacity, dtype=jnp.int32)
    select = (slot_labels[:, None] == target[None, :]).astype(jnp.bfloat16)
    spread = jnp.sum(
        select.reshape(expert_count * capacity, routes.shape[0], routes.shape[1]), axis=2
    )
    return (target, spread)


def dispatch(spread, rows_in, expert_count, capacity):
    placed = jnp.dot(spread, rows_in, preferred_element_type=jnp.float32).astype(jnp.bfloat16)
    return placed.reshape(expert_count, capacity, rows_in.shape[1])


def per_device(
    fwd_act, fwd_routes, bwd_saved, bwd_grad, bwd_routes, norm_gain, router, w_gate, w_up, w_down
):
    tok_count = fwd_act.shape[1]
    top_count = fwd_routes.shape[2]
    model_width = fwd_act.shape[2]
    expert_count = router.shape[1]
    capacity = min(tok_count, max(2, 2 * tok_count * top_count // expert_count))
    gain_row = norm_gain[0]
    gate_mat = w_gate[0]
    up_mat = w_up[0]
    down_mat = w_down[0]
    acts_f = fwd_act[0]
    routes_f = fwd_routes[0]
    normed_f, unused_unit, unused_factor = normalize(acts_f, gain_row)
    gates_f = gate_values(normed_f, router, routes_f)
    target_f, spread_f = placement(routes_f, expert_count, capacity)
    send_f = dispatch(spread_f, normed_f, expert_count, capacity)
    saved_b = bwd_saved[0]
    grads_b = bwd_grad[0]
    routes_b = bwd_routes[0]
    normed_b, unit_b, factor_b = normalize(saved_b, gain_row)
    gates_b = gate_values(normed_b, router, routes_b)
    target_b, spread_b = placement(routes_b, expert_count, capacity)
    send_x = dispatch(spread_b, normed_b, expert_count, capacity)
    send_g = dispatch(spread_b, grads_b, expert_count, capacity)
    rows_in = lax.all_to_all(send_f, "expert", split_axis=0, concat_axis=0, tiled=True)
    sources = rows_in.shape[0]
    slots = rows_in.shape[1]
    result = expert_forward(rows_in.reshape(-1, model_width), gate_mat, up_mat, down_mat)
    back_f = lax.all_to_all(
        result.reshape(sources, slots, model_width),
        "expert",
        split_axis=0,
        concat_axis=0,
        tiled=True,
    )
    rows_in = lax.all_to_all(send_x, "expert", split_axis=0, concat_axis=0, tiled=True)
    grads_in = lax.all_to_all(send_g, "expert", split_axis=0, concat_axis=0, tiled=True)
    sources = rows_in.shape[0]
    slots = rows_in.shape[1]
    d_rows, d_gates = expert_backward(
        rows_in.reshape(-1, model_width),
        grads_in.reshape(-1, model_width),
        gate_mat,
        up_mat,
        down_mat,
    )
    back_rows = lax.all_to_all(
        d_rows.reshape(sources, slots, model_width),
        "expert",
        split_axis=0,
        concat_axis=0,
        tiled=True,
    )
    back_gates = lax.all_to_all(
        d_gates.reshape(sources, slots), "expert", split_axis=0, concat_axis=0, tiled=True
    )
    picked_f = jnp.take(back_f.reshape(expert_count * capacity, model_width), target_f, axis=0)
    picked_f = picked_f.reshape(tok_count, top_count, model_width).astype(jnp.float32)
    layer_out = (
        acts_f.astype(jnp.float32) + jnp.sum(gates_f[:, :, None] * picked_f, axis=1)
    ).astype(jnp.bfloat16)
    fwd_next = shifted(layer_out[None], "section", 1)
    pair_grads = jnp.take(back_rows.reshape(expert_count * capacity, model_width), target_b, axis=0)
    pair_grads = pair_grads.reshape(tok_count, top_count, model_width).astype(jnp.float32)
    dgate = (
        jnp.take(back_gates.reshape(-1), target_b, axis=0)
        .reshape(tok_count, top_count)
        .astype(jnp.float32)
    )
    d_input = input_gradient(
        gates_b, dgate, pair_grads, routes_b, router, unit_b, factor_b, gain_row, grads_b
    )
    grad_prev = shifted(d_input[None], "section", -1)
    return (fwd_next, grad_prev)


def solution(mesh):
    in_specs = (
        P("section", "expert", None),
        P("section", "expert", None),
        P("section", "expert", None),
        P("section", "expert", None),
        P("section", "expert", None),
        P("section", None),
        P(),
        P("expert", None, None),
        P("expert", None, None),
        P("expert", None, None),
    )
    out_specs = (P("section", "expert", None), P("section", "expert", None))
    return jax.shard_map(
        per_device, mesh=mesh, in_specs=in_specs, out_specs=out_specs, check_vma=False
    )
```

profile of v0, /device:TPU:0, one launch (start us, length us, event | category | flops | bytes accessed | tf_op | source)
XLA Modules:
  0.0 122.3 jit_solution(11826197045238805441)
XLA Ops:
  3.7 1.9 %fusion.44 = bf16[16,8,2048]{2,1,0:T(8,128)(2,1)} fusion(bf16[128,8]{0,1:T(8,128)(2,1)S(1)} %fusion.97, bf16[1,8,2048]{2,1,0:T(8,128)(2,1)} %param.16, f32[8]{0:T(128)S(1)} %add_rsqrt_fusion, f32[2048]{0:T(1024)} %bitcast.150), kind=kOutput, calls=%fused_computation.36 | convolution fusion | flops 4521984 | bytes 567328 | tf_op jit(solution)/shard_map/dot_general | solution.py:89
  5.7 7.4 %all-to-all-start.3 = ((bf16[16,8,2048]{2,1,0:T(8,128)(2,1)}), bf16[16,8,2048]{2,1,0:T(8,128)(2,1)}, u32[]{:S(2)}, u32[]{:S(2)}) async-start(bf16[16,8,2048]{2,1,0:T(8,128)(2,1)} %fusion.44), calls=%async_computation.3 | async-start | bytes 1048576 | tf_op jit(solution)/shard_map/all_to_all | solution.py:130
  17.2 1.1 fusion.100
  22.4 1.2 fusion.43
  23.6 1.1 fusion.42
  25.3 2.4 %all-to-all-done.3 = bf16[16,8,2048]{2,1,0:T(8,128)(2,1)} async-done(((bf16[16,8,2048]{2,1,0:T(8,128)(2,1)}), bf16[16,8,2048]{2,1,0:T(8,128)(2,1)}, u32[]{:S(2)}, u32[]{:S(2)}) %all-to-all-start.3) | async-done | bytes 524320 | tf_op jit(solution)/shard_map/all_to_all | solution.py:130
  27.6 4.2 %all-to-all-start.2 = ((bf16[16,8,2048]{2,1,0:T(8,128)(2,1)}), bf16[16,8,2048]{2,1,0:T(8,128)(2,1)}, u32[]{:S(2)}, u32[]{:S(2)}) async-start(bf16[16,8,2048]{2,1,0:T(8,128)(2,1)} %fusion.43), calls=%async_computation.2 | async-start | bytes 1048576 | tf_op jit(solution)/shard_map/all_to_all | solution.py:131
  33.2 2.6 %fusion.14 = f32[128,768]{1,0:T(8,128)S(1)} fusion(bf16[1,2048,768]{2,1,0:T(8,128)(2,1)} %param.21, bf16[16,8,2048]{2,1,0:T(8,128)(2,1)} %all-to-all-done.3), kind=kOutput, calls=%fused_computation.19 | convolution fusion | flops 402653184 | bytes 4063232 | tf_op jit(solution)/shard_map/dot_general | solution.py:38
  35.8 2.4 %fusion.8 = f32[128,768]{1,0:T(8,128)} fusion(bf16[1,2048,768]{2,1,0:T(8,128)(2,1)S(1)} %copy-done, bf16[16,8,2048]{2,1,0:T(8,128)(2,1)} %all-to-all-done.3), kind=kOutput, calls=%fused_computation.13 | convolution fusion | flops 402653184 | bytes 4063232 | tf_op jit(solution)/shard_map/dot_general | solution.py:39
  38.2 8.2 %all-to-all-done.2 = bf16[16,8,2048]{2,1,0:T(8,128)(2,1)} async-done(((bf16[16,8,2048]{2,1,0:T(8,128)(2,1)}), bf16[16,8,2048]{2,1,0:T(8,128)(2,1)}, u32[]{:S(2)}, u32[]{:S(2)}) %all-to-all-start.2) | async-done | bytes 524320 | tf_op jit(solution)/shard_map/all_to_all | solution.py:131
  46.4 4.2 %all-to-all-start = ((bf16[16,8,2048]{2,1,0:T(8,128)(2,1)}), bf16[16,8,2048]{2,1,0:T(8,128)(2,1)}, u32[]{:S(2)}, u32[]{:S(2)}) async-start(bf16[16,8,2048]{2,1,0:T(8,128)(2,1)} %fusion.42), calls=%async_computation | async-start | bytes 1048576 | tf_op jit(solution)/shard_map/all_to_all | solution.py:119
  50.6 3.3 %fusion.46 = bf16[128]{0:T(256)(128)(2,1)} fusion(bf16[1,768,2048]{2,1,0:T(8,128)(2,1)} %param.23, bf16[16,8,2048]{2,1,0:T(8,128)(2,1)} %all-to-all-done.2, f32[128,768]{1,0:T(8,128)} %fusion.8, f32[128,768]{1,0:T(8,128)S(1)} %fusion.14), kind=kOutput, calls=%fused_computation.39 | convolution fusion | flops 404553600 | bytes 4456704 | tf_op jit(solution)/shard_map/dot_general | solution.py:43
  53.9 1.3 %convert_element_type.154 = bf16[16,1,8]{2,1,0:T(2,128)(2,1)} reshape(bf16[128]{0:T(256)(128)(2,1)} %fusion.46) | data formatting | bytes 512 | tf_op jit(solution)/shard_map/convert_element_type | solution.py:44
  55.3 3.2 %fusion.2 = f32[128,768]{1,0:T(8,128)S(1)} fusion(bf16[1,768,2048]{2,1,0:T(8,128)(2,1)} %param.23, bf16[16,8,2048]{2,1,0:T(8,128)(2,1)} %all-to-all-done.2), kind=kOutput, calls=%fused_computation.7 | convolution fusion | flops 402653184 | bytes 4063232 | tf_op jit(solution)/shard_map/dot_general | solution.py:48
  58.5 1.2 fusion.6
  60.5 2.0 %fusion.39 = bf16[16,8,2048]{2,1,0:T(8,128)(2,1)} fusion(f32[128,2048]{1,0:T(8,128)S(1)} %fusion.6, bf16[1,2048,768]{2,1,0:T(8,128)(2,1)S(1)} %copy-done.1, f32[128,768]{1,0:T(8,128)S(1)} %fusion.14, f32[128,768]{1,0:T(8,128)S(1)} %fusion.2, f32[128,768]{1,0:T(8,128)S(1)} %copy-done.2), kind=kOutput, calls=%fused_computation.33 | convolution fusion | flops 404160512 | bytes 5898240 | tf_op jit(solution)/shard_map/dot_general | solution.py:51
  62.4 2.6 %all-to-all-done = bf16[16,8,2048]{2,1,0:T(8,128)(2,1)} async-done(((bf16[16,8,2048]{2,1,0:T(8,128)(2,1)}), bf16[16,8,2048]{2,1,0:T(8,128)(2,1)}, u32[]{:S(2)}, u32[]{:S(2)}) %all-to-all-start) | async-done | bytes 524320 | tf_op jit(solution)/shard_map/all_to_all | solution.py:119
  65.1 4.1 %all-to-all-start.5 = ((bf16[16,1,8]{2,1,0:T(2,128)(2,1)}), bf16[16,1,8]{2,1,0:T(2,128)(2,1)}, u32[]{:S(2)}, u32[]{:S(2)}) async-start(bf16[16,1,8]{2,1,0:T(2,128)(2,1)} %convert_element_type.154), calls=%async_computation.5 | async-start | bytes 16384 | tf_op jit(solution)/shard_map/all_to_all | solution.py:148
  69.2 2.6 %fusion.16 = f32[128,768]{1,0:T(8,128)S(1)} fusion(bf16[1,2048,768]{2,1,0:T(8,128)(2,1)} %param.21, bf16[16,8,2048]{2,1,0:T(8,128)(2,1)} %all-to-all-done), kind=kOutput, calls=%fused_computation.21 | convolution fusion | flops 402653184 | bytes 4063232 | tf_op jit(solution)/shard_map/dot_general | solution.py:30
  71.8 3.6 %all-to-all-done.5 = bf16[16,1,8]{2,1,0:T(2,128)(2,1)} async-done(((bf16[16,1,8]{2,1,0:T(2,128)(2,1)}), bf16[16,1,8]{2,1,0:T(2,128)(2,1)}, u32[]{:S(2)}, u32[]{:S(2)}) %all-to-all-start.5) | async-done | bytes 288 | tf_op jit(solution)/shard_map/all_to_all | solution.py:148
  75.4 4.2 %all-to-all-start.4 = ((bf16[16,8,2048]{2,1,0:T(8,128)(2,1)}), bf16[16,8,2048]{2,1,0:T(8,128)(2,1)}, u32[]{:S(2)}, u32[]{:S(2)}) async-start(bf16[16,8,2048]{2,1,0:T(8,128)(2,1)} %fusion.39), calls=%async_computation.4 | async-start | bytes 1048576 | tf_op jit(solution)/shard_map/all_to_all | solution.py:141
  79.6 4.1 %fusion.36 = bf16[16,8,2048]{2,1,0:T(8,128)(2,1)} fusion(bf16[1,768,2048]{2,1,0:T(8,128)(2,1)} %param.23, bf16[1,2048,768]{2,1,0:T(8,128)(2,1)S(1)} %copy-done, bf16[16,8,2048]{2,1,0:T(8,128)(2,1)} %all-to-all-done, f32[128,768]{1,0:T(8,128)S(1)} %fusion.16), kind=kOutput, calls=%fused_computation.32 | convolution fusion | flops 806158336 | bytes 7733248 | tf_op jit(solution)/shard_map/dot_general | solution.py:34
  86.7 7.4 %all-to-all-done.4 = bf16[16,8,2048]{2,1,0:T(8,128)(2,1)} async-done(((bf16[16,8,2048]{2,1,0:T(8,128)(2,1)}), bf16[16,8,2048]{2,1,0:T(8,128)(2,1)}, u32[]{:S(2)}, u32[]{:S(2)}) %all-to-all-start.4) | async-done | bytes 524320 | tf_op jit(solution)/shard_map/all_to_all | solution.py:141
  94.1 4.2 %all-to-all-start.1 = ((bf16[16,8,2048]{2,1,0:T(8,128)(2,1)}), bf16[16,8,2048]{2,1,0:T(8,128)(2,1)}, u32[]{:S(2)}, u32[]{:S(2)}) async-start(bf16[16,8,2048]{2,1,0:T(8,128)(2,1)} %fusion.36), calls=%async_computation.1 | async-start | bytes 1048576 | tf_op jit(solution)/shard_map/all_to_all | solution.py:123
  98.4 2.2 %gather_fusion.4 = bf16[64,2048]{1,0:T(8,128)(2,1)S(1)} fusion(bf16[128,2048]{1,0:T(8,128)(2,1)} %bitcast.23, s32[1024]{0:T(1024)} %pad_clamp_fusion.1), kind=kCustom, calls=%fused_computation.3.clone | custom fusion | bytes 524544 | tf_op jit(solution)/shard_map/jit(_take)/gather | solution.py:157
  101.0 1.1 fusion.85
  102.3 1.3 %collective-permute-start.1 = (bf16[1,8,2048]{2,1,0:T(8,128)(2,1)S(1)}, bf16[1,8,2048]{2,1,0:T(8,128)(2,1)S(1)}, u32[]{:S(2)}, u32[]{:S(2)}) collective-permute-start(bf16[1,8,2048]{2,1,0:T(8,128)(2,1)S(1)} %fusion.91), channel_id=1, source_target_pairs={{16,0},{17,1},{18,2},{19,3},{20,4},{21,5},{22,6},{23,7},{24,8},{25... | collective-permute-start | bytes 98312 | tf_op jit(solution)/shard_map/ppermute | solution.py:12
  103.6 9.2 %all-to-all-done.1 = bf16[16,8,2048]{2,1,0:T(8,128)(2,1)} async-done(((bf16[16,8,2048]{2,1,0:T(8,128)(2,1)}), bf16[16,8,2048]{2,1,0:T(8,128)(2,1)}, u32[]{:S(2)}, u32[]{:S(2)}) %all-to-all-start.1) | async-done | bytes 524320 | tf_op jit(solution)/shard_map/all_to_all | solution.py:123
  112.8 2.2 %gather_fusion.2 = bf16[64,2048]{1,0:T(8,128)(2,1)S(1)} fusion(bf16[128,2048]{1,0:T(8,128)(2,1)} %bitcast.10, s32[1024]{0:T(1024)} %pad_clamp_fusion.2), kind=kCustom, calls=%fused_computation.1.clone | custom fusion | bytes 524544 | tf_op jit(solution)/shard_map/jit(_take)/gather | solution.py:151
  115.0 1.0 fusion.58
  116.1 3.4 %collective-permute-start = (bf16[1,8,2048]{2,1,0:T(8,128)(2,1)S(1)}, bf16[1,8,2048]{2,1,0:T(8,128)(2,1)S(1)}, u32[]{:S(2)}, u32[]{:S(2)}) collective-permute-start(bf16[1,8,2048]{2,1,0:T(8,128)(2,1)S(1)} %fusion.83), channel_id=1, source_target_pairs={{0,16},{1,17},{2,18},{3,19},{4,20},{5,21},{6,22},{7,23},{8,24},{9,... | collective-permute-start | bytes 98312 | tf_op jit(solution)/shard_map/ppermute | solution.py:12
  119.5 1.6 %collective-permute-done = bf16[1,8,2048]{2,1,0:T(8,128)(2,1)S(1)} collective-permute-done((bf16[1,8,2048]{2,1,0:T(8,128)(2,1)S(1)}, bf16[1,8,2048]{2,1,0:T(8,128)(2,1)S(1)}, u32[]{:S(2)}, u32[]{:S(2)}) %collective-permute-start) | collective-permute-done | bytes 32800 | tf_op jit(solution)/shard_map/ppermute | solution.py:12
  (88 shorter events, 18.4 us)
Async XLA Ops:
  0.6 35.2 %copy-start = (bf16[1,2048,768]{2,1,0:T(8,128)(2,1)S(1)}, bf16[1,2048,768]{2,1,0:T(8,128)(2,1)}, u32[]{:S(2)}) copy-start(bf16[1,2048,768]{2,1,0:T(8,128)(2,1)} %param.22) | copy-start | bytes 9437188
  0.6 18.5 %copy-start.6 = (s32[1,8,8]{2,1,0:T(8,128)S(1)}, s32[1,8,8]{2,1,0:T(8,128)}, u32[]{:S(2)}) copy-start(s32[1,8,8]{2,1,0:T(8,128)} %param.18) | copy-start | bytes 772
  1.8 18.6 %copy-start.4 = (bf16[1,8,2048]{2,1,0:T(8,128)(2,1)S(1)}, bf16[1,8,2048]{2,1,0:T(8,128)(2,1)}, u32[]{:S(2)}) copy-start(bf16[1,8,2048]{2,1,0:T(8,128)(2,1)} %param.14) | copy-start | bytes 98308
  1.8 18.7 %copy-start.10 = (f32[1,2048]{1,0:T(1,128)S(1)}, f32[1,2048]{1,0:T(1,128)}, u32[]{:S(2)}) copy-start(f32[1,2048]{1,0:T(1,128)} %param.19) | copy-start | bytes 24580
  1.8 18.7 %copy-start.11 = (bf16[2048,16]{0,1:T(8,128)(2,1)S(1)}, bf16[2048,16]{0,1:T(8,128)(2,1)}, u32[]{:S(2)}) copy-start(bf16[2048,16]{0,1:T(8,128)(2,1)} %param.20) | copy-start | bytes 196612
  3.7 14.6 %copy-start.14 = (f32[8]{0:T(128)}, f32[8]{0:T(128)S(1)}, u32[]{:S(2)}) copy-start(f32[8]{0:T(128)S(1)} %add_rsqrt_fusion) | copy-start | bytes 100
  5.7 22.0 %all-to-all-start.3 = ((bf16[16,8,2048]{2,1,0:T(8,128)(2,1)}), bf16[16,8,2048]{2,1,0:T(8,128)(2,1)}, u32[]{:S(2)}, u32[]{:S(2)}) async-start(bf16[16,8,2048]{2,1,0:T(8,128)(2,1)} %fusion.44), calls=%async_computation.3 | async-start | bytes 1048576 | tf_op jit(solution)/shard_map/all_to_all | solution.py:130
  19.1 3.1 %copy-start.9 = (s32[1,8,8]{2,1,0:T(8,128)S(1)}, s32[1,8,8]{2,1,0:T(8,128)}, u32[]{:S(2)}) copy-start(s32[1,8,8]{2,1,0:T(8,128)} %param.15) | copy-start | bytes 772
  19.1 3.4 %copy-start.7 = (bf16[1,8,2048]{2,1,0:T(8,128)(2,1)S(1)}, bf16[1,8,2048]{2,1,0:T(8,128)(2,1)}, u32[]{:S(2)}) copy-start(bf16[1,8,2048]{2,1,0:T(8,128)(2,1)} %param.17) | copy-start | bytes 98308
  19.2 1.3 %copy-start.12 = (f32[8,8]{1,0:T(8,128)}, f32[8,8]{1,0:T(8,128)S(1)}, u32[]{:S(2)}) copy-start(f32[8,8]{1,0:T(8,128)S(1)} %reshape.256) | copy-start | bytes 772
  27.6 18.7 %all-to-all-start.2 = ((bf16[16,8,2048]{2,1,0:T(8,128)(2,1)}), bf16[16,8,2048]{2,1,0:T(8,128)(2,1)}, u32[]{:S(2)}, u32[]{:S(2)}) async-start(bf16[16,8,2048]{2,1,0:T(8,128)(2,1)} %fusion.43), calls=%async_computation.2 | async-start | bytes 1048576 | tf_op jit(solution)/shard_map/all_to_all | solution.py:131
  46.4 18.7 %all-to-all-start = ((bf16[16,8,2048]{2,1,0:T(8,128)(2,1)}), bf16[16,8,2048]{2,1,0:T(8,128)(2,1)}, u32[]{:S(2)}, u32[]{:S(2)}) async-start(bf16[16,8,2048]{2,1,0:T(8,128)(2,1)} %fusion.42), calls=%async_computation | async-start | bytes 1048576 | tf_op jit(solution)/shard_map/all_to_all | solution.py:119
  58.5 1.9 %copy-start.1 = (bf16[1,2048,768]{2,1,0:T(8,128)(2,1)S(1)}, bf16[1,2048,768]{2,1,0:T(8,128)(2,1)}, u32[]{:S(2)}) copy-start(bf16[1,2048,768]{2,1,0:T(8,128)(2,1)} %param.21) | copy-start | bytes 9437188
  58.5 1.9 %copy-start.2 = (f32[128,768]{1,0:T(8,128)S(1)}, f32[128,768]{1,0:T(8,128)}, u32[]{:S(2)}) copy-start(f32[128,768]{1,0:T(8,128)} %fusion.8) | copy-start | bytes 1179652
  65.1 10.3 %all-to-all-start.5 = ((bf16[16,1,8]{2,1,0:T(2,128)(2,1)}), bf16[16,1,8]{2,1,0:T(2,128)(2,1)}, u32[]{:S(2)}, u32[]{:S(2)}) async-start(bf16[16,1,8]{2,1,0:T(2,128)(2,1)} %convert_element_type.154), calls=%async_computation.5 | async-start | bytes 16384 | tf_op jit(solution)/shard_map/all_to_all | solution.py:148
  75.4 18.7 %all-to-all-start.4 = ((bf16[16,8,2048]{2,1,0:T(8,128)(2,1)}), bf16[16,8,2048]{2,1,0:T(8,128)(2,1)}, u32[]{:S(2)}, u32[]{:S(2)}) async-start(bf16[16,8,2048]{2,1,0:T(8,128)(2,1)} %fusion.39), calls=%async_computation.4 | async-start | bytes 1048576 | tf_op jit(solution)/shard_map/all_to_all | solution.py:141
  83.8 16.8 %copy-start.17 = (pred[64]{0:T(512)(128)(4,1)S(1)}, pred[64]{0:T(512)(128)(4,1)}, u32[]{:S(2)}) copy-start(pred[64]{0:T(512)(128)(4,1)} %get-tuple-element.6) | copy-start | bytes 196
  83.8 17.3 %copy-start.3 = (bf16[1,8,2048]{2,1,0:T(8,128)(2,1)S(1)}, bf16[1,8,2048]{2,1,0:T(8,128)(2,1)}, u32[]{:S(2)}) copy-start(bf16[1,8,2048]{2,1,0:T(8,128)(2,1)} %param.16) | copy-start | bytes 98308
  83.8 17.3 %copy-start.15 = (f32[8]{0:T(128)S(1)}, f32[8]{0:T(128)}, u32[]{:S(2)}) copy-start(f32[8]{0:T(128)} %copy-done.14) | copy-start | bytes 100
  83.8 18.4 %copy-start.8 = (bf16[1,8,2048]{2,1,0:T(8,128)(2,1)S(1)}, bf16[1,8,2048]{2,1,0:T(8,128)(2,1)}, u32[]{:S(2)}) copy-start(bf16[1,8,2048]{2,1,0:T(8,128)(2,1)} %param.17) | copy-start | bytes 98308
  86.6 15.6 %copy-start.16 = (f32[8]{0:T(128)S(1)}, f32[8]{0:T(128)}, u32[]{:S(2)}) copy-start(f32[8]{0:T(128)} %copy-done.14) | copy-start | bytes 100
  86.7 28.4 %copy-start.13 = (f32[8,8]{1,0:T(8,128)S(1)}, f32[8,8]{1,0:T(8,128)}, u32[]{:S(2)}) copy-start(f32[8,8]{1,0:T(8,128)} %broadcast_divide_fusion.1) | copy-start | bytes 772
  94.1 18.7 %all-to-all-start.1 = ((bf16[16,8,2048]{2,1,0:T(8,128)(2,1)}), bf16[16,8,2048]{2,1,0:T(8,128)(2,1)}, u32[]{:S(2)}, u32[]{:S(2)}) async-start(bf16[16,8,2048]{2,1,0:T(8,128)(2,1)} %fusion.36), calls=%async_computation.1 | async-start | bytes 1048576 | tf_op jit(solution)/shard_map/all_to_all | solution.py:123
  98.3 17.7 %copy-start.5 = (bf16[1,8,2048]{2,1,0:T(8,128)(2,1)S(1)}, bf16[1,8,2048]{2,1,0:T(8,128)(2,1)}, u32[]{:S(2)}) copy-start(bf16[1,8,2048]{2,1,0:T(8,128)(2,1)} %param.14) | copy-start | bytes 98308
  102.3 17.2 %collective-permute-start.1 = (bf16[1,8,2048]{2,1,0:T(8,128)(2,1)S(1)}, bf16[1,8,2048]{2,1,0:T(8,128)(2,1)S(1)}, u32[]{:S(2)}, u32[]{:S(2)}) collective-permute-start(bf16[1,8,2048]{2,1,0:T(8,128)(2,1)S(1)} %fusion.91), channel_id=1, source_target_pairs={{16,0},{17,1},{18,2},{19,3},{20,4},{21,5},{22,6},{23,7},{24,8},{25... | collective-permute-start | bytes 98312 | tf_op jit(solution)/shard_map/ppermute | solution.py:12
  116.1 5.0 %collective-permute-start = (bf16[1,8,2048]{2,1,0:T(8,128)(2,1)S(1)}, bf16[1,8,2048]{2,1,0:T(8,128)(2,1)S(1)}, u32[]{:S(2)}, u32[]{:S(2)}) collective-permute-start(bf16[1,8,2048]{2,1,0:T(8,128)(2,1)S(1)} %fusion.83), channel_id=1, source_target_pairs={{0,16},{1,17},{2,18},{3,19},{4,20},{5,21},{6,22},{7,23},{8,24},{9,... | collective-permute-start | bytes 98312 | tf_op jit(solution)/shard_map/ppermute | solution.py:12
where the time goes:
time: 124 us; the launch traced here: 122 us
  waiting for transfers between devices  35 us (28%)
  starting transfers between devices  33.1 us (27%)
  matrix products  28.1 us (23%)
  local copies, waits for them, and re-layouts  12.6 us (10%)
  other arithmetic  12.4 us (10%)
    all_to_all x1, waiting for transfers between devices, per_device(): lax.all_to_all(result.reshape(sources, slots, model_width), 'expert', spl...  9.23 us
    all_to_all x1, waiting for transfers between devices, per_device(): lax.all_to_all(send_g, 'expert', split_axis=0, concat_axis=0, tiled=True)  8.16 us
    all_to_all x1, starting transfers between devices, per_device(): lax.all_to_all(send_x, 'expert', split_axis=0, concat_axis=0, tiled=True)  7.44 us
    all_to_all x1, waiting for transfers between devices, per_device(): lax.all_to_all(d_rows.reshape(sources, slots, model_width), 'expert', spl...  7.43 us
    ppermute x2, starting transfers between devices, shifted(): return lax.ppermute(block, axis, route)  4.69 us
    dot_general x3, matrix products, dispatch(): jnp.dot(spread, rows_in, preferred_element_type=jnp.float32)  4.24 us
    all_to_all x1, starting transfers between devices, per_device(): lax.all_to_all(send_f, 'expert', split_axis=0, concat_axis=0, tiled=True)  4.24 us
    all_to_all x1, starting transfers between devices, per_device(): lax.all_to_all(result.reshape(sources, slots, model_width), 'expert', spl...  4.24 us
  transfers between devices with their start and end apart: 8, of which 7 were waited for; matrix products, arithmetic and copies ran while one was open for 38% of the time, Pallas kernels for 0%

commit v1 on v0

--- a/solution.py
+++ b/solution.py
@@ -1,6 +1,8 @@
 import jax
 import jax.numpy as jnp
 from jax import lax
+from jax.experimental import pallas as pl
+from jax.experimental.pallas import tpu as pltpu
 from jax.sharding import PartitionSpec as P
 
 EPSILON = 1e-06
@@ -90,7 +92,7 @@
     return placed.reshape(expert_count, capacity, rows_in.shape[1])
 
 
-def per_device(
+def routed_plan(
     fwd_act, fwd_routes, bwd_saved, bwd_grad, bwd_routes, norm_gain, router, w_gate, w_up, w_down
 ):
     tok_count = fwd_act.shape[1]
@@ -168,6 +170,202 @@
     return (fwd_next, grad_prev)
 
 
+AXES = ("section", "expert")
+SQUARE = 8
+CORE, HALF, SECTION = 1, 8, 16
+LANES = 128
+
+
+def swapped(block, distance):
+    count = lax.axis_size(AXES)
+    return lax.ppermute(block, AXES, [(i, i ^ distance) for i in range(count)])
+
+
+def expert_kernel(
+    where_ref, near_ref, far_ref, gain_ref, gain_far_ref, router_ref,
+    gate_hbm, up_hbm, down_hbm, kept_ref, sent_ref,
+    gate_ref, up_ref, down_ref, sems,
+):
+    width = gain_ref.shape[1]
+    hidden_count = gate_ref.shape[1]
+    step = 256 if hidden_count % 256 == 0 else hidden_count
+    pieces = hidden_count // step
+    copies = []
+    for piece in range(pieces):
+        cols = pl.ds(piece * step, step)
+        copies.append((
+            pltpu.make_async_copy(gate_hbm.at[:, cols], gate_ref.at[:, cols], sems.at[0, piece]),
+            pltpu.make_async_copy(up_hbm.at[:, cols], up_ref.at[:, cols], sems.at[1, piece]),
+            pltpu.make_async_copy(down_hbm.at[cols, :], down_ref.at[cols, :], sems.at[2, piece]),
+        ))
+        for copy in copies[-1]:
+            copy.start()
+
+    first_section = where_ref[0] == 0
+    own_expert = where_ref[1]
+    gain_here = gain_ref[...]
+    gain_there = gain_far_ref[...]
+    gain_f = jnp.where(first_section, gain_here, gain_there)
+    gain_b = jnp.where(first_section, gain_there, gain_here)
+
+    chunks = []
+    for ref in (near_ref, far_ref):
+        rows = ref[...].astype(jnp.float32)
+        chunks += [rows[24 * k : 24 * k + 24] for k in range(SQUARE // 2)]
+    acts = jnp.concatenate([c[0:8] for c in chunks] + [c[8:16] for c in chunks], axis=0)
+    grads = jnp.concatenate([c[16:24, :width] for c in chunks], axis=0)
+    routes = acts[:, width:]
+    acts = acts[:, :width]
+    half = acts.shape[0] // 2
+
+    factor = lax.rsqrt(jnp.mean(acts * acts, axis=-1, keepdims=True) + EPSILON)
+    unit = acts * factor
+    normed = jnp.concatenate([unit[:half] * gain_f, unit[half:] * gain_b], axis=0)
+    normed = normed.astype(jnp.bfloat16)
+    grads_low = grads.astype(jnp.bfloat16)
+
+    router = router_ref[...]
+    experts = router.shape[1]
+    logits = jnp.dot(normed, router, preferred_element_type=jnp.float32)
+    labels = lax.broadcasted_iota(jnp.int32, logits.shape, 1)
+    labels_real = labels.astype(jnp.float32)
+    chosen = routes[:, 0:1] == labels_real
+    for k in range(1, TOP_COUNT):
+        chosen = jnp.logical_or(chosen, routes[:, k : k + 1] == labels_real)
+    raised = jnp.where(chosen, jnp.exp(logits), 0.0)
+    gates = raised / jnp.sum(raised, axis=-1, keepdims=True)
+    own = labels == own_expert
+    gate_own = jnp.sum(jnp.where(own, gates, 0.0), axis=-1, keepdims=True)
+
+    contract = (((1,), (1,)), ((), ()))
+    expert_out = None
+    pair_grad = None
+    for piece in range(pieces):
+        cols = slice(piece * step, piece * step + step)
+        for copy in copies[piece]:
+            copy.wait()
+        gate_mat = gate_ref[:, cols]
+        up_mat = up_ref[:, cols]
+        down_mat = down_ref[cols, :]
+        pre_gate = jnp.dot(normed, gate_mat, preferred_element_type=jnp.float32)
+        pre_up = jnp.dot(normed, up_mat, preferred_element_type=jnp.float32)
+        sigma = jax.nn.sigmoid(pre_gate)
+        silu_val = pre_gate * sigma
+        hidden = (silu_val * pre_up).astype(jnp.bfloat16)
+        part = jnp.dot(hidden, down_mat, preferred_element_type=jnp.float32)
+        expert_out = part if expert_out is None else expert_out + part
+        d_hidden = lax.dot_general(
+            grads_low, down_mat, contract, preferred_element_type=jnp.float32
+        )
+        d_up = (d_hidden * silu_val[half:]).astype(jnp.bfloat16)
+        sigma_b = sigma[half:]
+        slope = sigma_b * (1.0 + pre_gate[half:] * (1.0 - sigma_b))
+        d_pre = (d_hidden * pre_up[half:] * slope).astype(jnp.bfloat16)
+        part = lax.dot_general(d_pre, gate_mat, contract, preferred_element_type=jnp.float32)
+        part = part + lax.dot_general(d_up, up_mat, contract, preferred_element_type=jnp.float32)
+        pair_grad = part if pair_grad is None else pair_grad + part
+
+    out_f = gate_own[:half] * expert_out[:half]
+    dgate = jnp.sum(grads * expert_out[half:], axis=-1, keepdims=True)
+    gate_b = gate_own[half:]
+    spread = gate_b * dgate * (jnp.where(own[half:], 1.0, 0.0) - gates[half:])
+    spread_high = spread.astype(jnp.bfloat16)
+    spread_low = (spread - spread_high.astype(jnp.float32)).astype(jnp.bfloat16)
+    d_normed = gate_b * pair_grad
+    d_normed = d_normed + lax.dot_general(
+        spread_high, router, contract, preferred_element_type=jnp.float32
+    )
+    d_normed = d_normed + lax.dot_general(
+        spread_low, router, contract, preferred_element_type=jnp.float32
+    )
+    d_unit = d_normed * gain_b
+    unit_b = unit[half:]
+    out_b = factor[half:] * (
+        d_unit - unit_b * jnp.mean(d_unit * unit_b, axis=-1, keepdims=True)
+    )
+
+    head_f = out_f[0:8] + jnp.where(first_section, 0.0, acts[0:8])
+    head_b = out_b[0:8] + jnp.where(first_section, grads[0:8], 0.0)
+    parts = []
+    for k in range(SQUARE):
+        parts.append(head_f if k == 0 else out_f[8 * k : 8 * k + 8])
+        parts.append(head_b if k == 0 else out_b[8 * k : 8 * k + 8])
+    kept_ref[...] = jnp.concatenate(parts[:SQUARE], axis=0).astype(jnp.bfloat16)
+    sent_ref[...] = jnp.concatenate(parts[SQUARE:], axis=0).astype(jnp.bfloat16)
+
+
+TOP_COUNT = 8
+
+
+def run_experts(where, near, far, gain_row, gain_far, router, gate_mat, up_mat, down_mat):
+    width, hidden_count = gate_mat.shape
+    rows = SQUARE // 2 * 16
+    vmem = pl.BlockSpec(memory_space=pltpu.VMEM)
+    hbm = pl.BlockSpec(memory_space=pl.ANY)
+    return pl.pallas_call(
+        expert_kernel,
+        out_shape=[jax.ShapeDtypeStruct((rows, width), jnp.bfloat16)] * 2,
+        in_specs=[pl.BlockSpec(memory_space=pltpu.SMEM)] + [vmem] * 5 + [hbm] * 3,
+        out_specs=[vmem] * 2,
+        scratch_shapes=[
+            pltpu.VMEM((width, hidden_count), jnp.bfloat16),
+            pltpu.VMEM((width, hidden_count), jnp.bfloat16),
+            pltpu.VMEM((hidden_count, width), jnp.bfloat16),
+            pltpu.SemaphoreType.DMA((3, max(1, hidden_count // 256))),
+        ],
+        compiler_params=pltpu.CompilerParams(vmem_limit_bytes=40 * 1024 * 1024),
+        name="experts",
+    )(where, near, far, gain_row, gain_far, router, gate_mat, up_mat, down_mat)
+
+
+def added(*blocks):
+    return sum(block.astype(jnp.float32) for block in blocks)
+
+
+def paired_plan(
+    fwd_act, fwd_routes, bwd_saved, bwd_grad, bwd_routes, norm_gain, router, w_gate, w_up, w_down
+):
+    section = lax.axis_index("section")
+    first = section == 0
+    where = jnp.stack([section, lax.axis_index("expert")]).astype(jnp.int32)
+
+    acts = jnp.where(first, fwd_act[0], bwd_saved[0])
+    routes = jnp.where(first, fwd_routes[0], bwd_routes[0]).astype(jnp.bfloat16)
+    tail = jnp.pad(routes, ((0, 0), (0, LANES - routes.shape[1])))
+    own_rows = jnp.concatenate(
+        [
+            jnp.concatenate([acts, tail], axis=1),
+            jnp.pad(bwd_grad[0], ((0, 0), (0, LANES))),
+        ],
+        axis=0,
+    )
+    across = swapped(own_rows, SECTION)
+    along = swapped(own_rows, HALF)
+    gain_far = swapped(norm_gain, SECTION)
+    forward = jnp.where(first, along[:8], across[:8])
+    backward = jnp.where(first, across, along)
+    mine = jnp.concatenate([forward, backward], axis=0)
+    near = jnp.concatenate([mine] + [swapped(mine, k) for k in (2, 4, 6)], axis=0)
+    far = swapped(near, CORE)
+
+    kept, sent = run_experts(
+        where, near, far, norm_gain, gain_far, router, w_gate[0], w_up[0], w_down[0]
+    )
+
+    chip = added(kept, swapped(sent, CORE)).astype(jnp.bfloat16)
+    total = added(
+        chip[0:16], swapped(chip[16:32], 2), swapped(chip[32:48], 4), swapped(chip[48:64], 6)
+    )
+    total = total.astype(jnp.bfloat16)
+    leaving = jnp.where(first, total[:8], total[8:])
+    staying = jnp.where(first, total[8:], total[:8])
+    result = added(staying, swapped(leaving, SECTION + HALF)).astype(jnp.bfloat16)
+    nothing = jnp.zeros_like(result)
+    fwd_next = jnp.where(first, nothing, result)[None]
+    grad_prev = jnp.where(first, result, nothing)[None]
+    return (fwd_next, grad_prev)
+
+
 def solution(mesh):
     in_specs = (
         P("section", "expert", None),
@@ -182,6 +380,8 @@
         P("expert", None, None),
     )
     out_specs = (P("section", "expert", None), P("section", "expert", None))
+    shape = dict(mesh.shape)
+    paired = shape["section"] == 2 and shape["expert"] == 2 * SQUARE
     return jax.shard_map(
-        per_device, mesh=mesh, in_specs=in_specs, out_specs=out_specs, check_vma=False
-    )
+        paired_plan if paired else routed_plan, mesh=mesh, in_specs=in_specs, out_specs=out_specs, check_vma=False
+    )

time: 124 us -> 54.5 us (0.44)
  matrix products: 28.1 us -> 0 us
  waiting for transfers between devices: 35 us -> 16.7 us
  starting transfers between devices: 33.1 us -> 16.6 us
  Pallas kernels: 0 us -> 9.3 us
  other arithmetic: 12.4 us -> 3.12 us
  local copies, waits for them, and re-layouts: 12.6 us -> 7.53 us
    all_to_all x6 -> x0, waiting for transfers between devices: 33.4 us -> none  [the longest x1 9.23 us: per_device(): lax.all_to_all(result.reshape(sources, slots, model_width), 'expert', spl...]
    all_to_all x6 -> x0, starting transfers between devices: 28.5 us -> none  [the longest x1 7.44 us: per_device(): lax.all_to_all(send_x, 'expert', split_axis=0, concat_axis=0, tiled=True)]
    dot_general x14 -> x0, matrix products: 28.1 us -> none  [the longest x3 4.24 us: dispatch(): jnp.dot(spread, rows_in, preferred_element_type=jnp.float32)]
    ppermute x2 -> x12, waiting for transfers between devices: 1.57 us -> 16.7 us  [swapped(): return lax.ppermute(block, AXES, [(i, i ^ distance) for i in range(count)])]
    ppermute x2 -> x12, starting transfers between devices: 4.69 us -> 16.6 us  [swapped(): return lax.ppermute(block, AXES, [(i, i ^ distance) for i in range(count)])]
    pallas_call x0 -> x1, Pallas kernels: none -> 9.3 us  [run_experts(): pl.pallas_call(expert_kernel, out_shape=[jax.ShapeDtypeStruct((rows, widt...]
    gather x10 -> x0, local copies, waits for them, and re-layouts: 7.22 us -> none  [the longest x1 2.22 us: per_device(): jnp.take(back_rows.reshape(expert_count * capacity, model_width), target_...]
    unnamed x38 -> x11, local copies, waits for them, and re-layouts: 2.08 us -> 7.5 us
  transfers between devices with their start and end apart: 8 -> 12, of which waited for: 7 -> 8; matrix products, arithmetic and copies ran while one was open for 38% -> 2% of each run, Pallas kernels for 0% -> 0%
where the time goes in v1:
time: 54.5 us; the launch traced here: 54 us
  waiting for transfers between devices  16.7 us (31%)
  starting transfers between devices  16.6 us (30%)
  Pallas kernels  9.3 us (17%)
  local copies, waits for them, and re-layouts  7.53 us (14%)
  other arithmetic  3.12 us (6%)
  between operations  0.73 us (1%)
    ppermute x12, waiting for transfers between devices, swapped(): return lax.ppermute(block, AXES, [(i, i ^ distance) for i in range(count)])  16.7 us
    ppermute x12, starting transfers between devices, swapped(): return lax.ppermute(block, AXES, [(i, i ^ distance) for i in range(count)])  16.6 us
    pallas_call x1, Pallas kernels, run_experts(): pl.pallas_call(expert_kernel, out_shape=[jax.ShapeDtypeStruct((rows, widt...  9.3 us
    unnamed x11, local copies, waits for them, and re-layouts  7.5 us
  transfers between devices with their start and end apart: 12, of which 8 were waited for; matrix products, arithmetic and copies ran while one was open for 2% of the time, Pallas kernels for 0%

profile of v1, /device:TPU:0, one launch (start us, length us, event | category | flops | bytes accessed | tf_op | source)
XLA Modules:
  0.0 54.0 jit_solution(6044322879080820186)
XLA Ops:
  0.6 0.7 %fusion.6 = bf16[8,8]{1,0:T(8,128)(2,1)S(1)} fusion(s32[1,8,8]{2,1,0:T(8,128)} %param.11, s32[1,8,8]{2,1,0:T(8,128)} %param.14, pred[]{:T(512)S(6)} %eq.3), kind=kLoop, calls=%fused_computation.25 | loop fusion | flops 128 | bytes 641 | tf_op jit(solution)/shard_map/convert_element_type | solution.py:333
  1.3 0.8 %select_bitcast_fusion.2 = bf16[8,2048]{1,0:T(8,128)(2,1)S(1)} fusion(bf16[1,8,2048]{2,1,0:T(8,128)(2,1)} %param.10, bf16[1,8,2048]{2,1,0:T(8,128)(2,1)} %param.12, pred[]{:T(512)S(6)} %eq.3), kind=kLoop, calls=%fused_computation.17 | loop fusion | flops 16384 | bytes 98305 | tf_op jit(solution)/shard_map/jit(_where)/select_n | solution.py:332
  2.1 0.8 %fusion.4 = bf16[16,2176]{1,0:T(8,128)(2,1)S(1)} fusion(bf16[8,2048]{1,0:T(8,128)(2,1)} %bitcast.17, bf16[8,8]{1,0:T(8,128)(2,1)S(1)} %fusion.6, bf16[8,2048]{1,0:T(8,128)(2,1)S(1)} %select_bitcast_fusion.2), kind=kLoop, calls=%fused_computation.10 | loop fusion | flops 452608 | bytes 135296 | tf_op jit(solution)/shard_map/concatenate | solution.py:335
  2.9 2.9 %collective-permute-start.1 = (bf16[16,2176]{1,0:T(8,128)(2,1)S(1)}, bf16[16,2176]{1,0:T(8,128)(2,1)S(1)}, u32[]{:S(2)}, u32[]{:S(2)}) collective-permute-start(bf16[16,2176]{1,0:T(8,128)(2,1)S(1)} %fusion.4), channel_id=1, source_target_pairs={{0,16},{1,17},{2,18},{3,19},{4,20},{5,21},{6,22},{7,23},{8,24},{9,... | collective-permute-start | bytes 208904 | tf_op jit(solution)/shard_map/ppermute | solution.py:181
  5.8 2.6 %collective-permute-start = (bf16[16,2176]{1,0:T(8,128)(2,1)S(1)}, bf16[16,2176]{1,0:T(8,128)(2,1)S(1)}, u32[]{:S(2)}, u32[]{:S(2)}) collective-permute-start(bf16[16,2176]{1,0:T(8,128)(2,1)S(1)} %fusion.4), channel_id=1, source_target_pairs={{0,8},{1,9},{2,10},{3,11},{4,12},{5,13},{6,14},{7,15},{8,0},{9,1},... | collective-permute-start | bytes 208904 | tf_op jit(solution)/shard_map/ppermute | solution.py:181
  8.4 3.0 %collective-permute-done = bf16[16,2176]{1,0:T(8,128)(2,1)S(1)} collective-permute-done((bf16[16,2176]{1,0:T(8,128)(2,1)S(1)}, bf16[16,2176]{1,0:T(8,128)(2,1)S(1)}, u32[]{:S(2)}, u32[]{:S(2)}) %collective-permute-start) | collective-permute-done | bytes 69664 | tf_op jit(solution)/shard_map/ppermute | solution.py:181
  11.4 1.6 %collective-permute-start.2 = (bf16[24,2176]{1,0:T(8,128)(2,1)S(1)}, bf16[24,2176]{1,0:T(8,128)(2,1)S(1)}, u32[]{:S(2)}, u32[]{:S(2)}) collective-permute-start(bf16[24,2176]{1,0:T(8,128)(2,1)S(1)} %pad_maximum_fusion), channel_id=1, source_target_pairs={{0,2},{1,3},{2,0},{3,1},{4,6},{5,7},{6,4},{7,5},{8,10},{9,11},{10,... | collective-permute-start | bytes 313352 | tf_op jit(solution)/shard_map/ppermute | solution.py:181
  13.0 1.2 %collective-permute-start.4 = (bf16[24,2176]{1,0:T(8,128)(2,1)S(1)}, bf16[24,2176]{1,0:T(8,128)(2,1)S(1)}, u32[]{:S(2)}, u32[]{:S(2)}) collective-permute-start(bf16[24,2176]{1,0:T(8,128)(2,1)S(1)} %pad_maximum_fusion), channel_id=1, source_target_pairs={{0,6},{1,7},{2,4},{3,5},{4,2},{5,3},{6,0},{7,1},{8,14},{9,15},{10,... | collective-permute-start | bytes 313352 | tf_op jit(solution)/shard_map/ppermute | solution.py:181
  14.3 0.7 %collective-permute-start.3 = (bf16[24,2176]{1,0:T(8,128)(2,1)S(1)}, bf16[24,2176]{1,0:T(8,128)(2,1)S(1)}, u32[]{:S(2)}, u32[]{:S(2)}) collective-permute-start(bf16[24,2176]{1,0:T(8,128)(2,1)S(1)} %pad_maximum_fusion), channel_id=1, source_target_pairs={{0,4},{1,5},{2,6},{3,7},{4,0},{5,1},{6,2},{7,3},{8,12},{9,13},{10,... | collective-permute-start | bytes 313352 | tf_op jit(solution)/shard_map/ppermute | solution.py:181
  15.0 1.5 %collective-permute-done.2 = bf16[24,2176]{1,0:T(8,128)(2,1)S(1)} collective-permute-done((bf16[24,2176]{1,0:T(8,128)(2,1)S(1)}, bf16[24,2176]{1,0:T(8,128)(2,1)S(1)}, u32[]{:S(2)}, u32[]{:S(2)}) %collective-permute-start.2) | collective-permute-done | bytes 104480 | tf_op jit(solution)/shard_map/ppermute | solution.py:181
  16.5 2.4 %collective-permute-done.3 = bf16[24,2176]{1,0:T(8,128)(2,1)S(1)} collective-permute-done((bf16[24,2176]{1,0:T(8,128)(2,1)S(1)}, bf16[24,2176]{1,0:T(8,128)(2,1)S(1)}, u32[]{:S(2)}, u32[]{:S(2)}) %collective-permute-start.3) | collective-permute-done | bytes 104480 | tf_op jit(solution)/shard_map/ppermute | solution.py:181
  19.0 0.1 collective-permute-start.5
  19.1 0.6 %collective-permute-start.6 = (f32[1,2048]{1,0:T(1,128)}, f32[1,2048]{1,0:T(1,128)S(1)}, u32[]{:S(2)}, u32[]{:S(2)}) collective-permute-start(f32[1,2048]{1,0:T(1,128)} %gain_ref.1), channel_id=1, source_target_pairs={{0,16},{1,17},{2,18},{3,19},{4,20},{5,21},{6,22},{7,23},{8,24},{9,... | collective-permute-start | bytes 24584 | tf_op jit(solution)/shard_map/ppermute | solution.py:181
  19.7 0.1 pad_add_fusion.where_ref
  19.7 1.1 %copy.12.router_ref = bf16[2048,16]{1,0:T(8,128)(2,1)S(1)} copy(bf16[2048,16]{0,1:T(8,128)(2,1)} %param.16) | data formatting | bytes 131072 | tf_op args[6]
  20.9 2.1 %collective-permute-done.6.gain_far_ref = f32[1,2048]{1,0:T(1,128)S(1)} collective-permute-done((f32[1,2048]{1,0:T(1,128)}, f32[1,2048]{1,0:T(1,128)S(1)}, u32[]{:S(2)}, u32[]{:S(2)}) %collective-permute-start.6) | collective-permute-done | bytes 8224 | tf_op jit(solution)/shard_map/ppermute | solution.py:181
  23.0 1.9 %copy-done = bf16[1,2048,768]{2,1,0:T(8,128)(2,1)S(1)} copy-done((bf16[1,2048,768]{2,1,0:T(8,128)(2,1)S(1)}, bf16[1,2048,768]{2,1,0:T(8,128)(2,1)}, u32[]{:S(2)}) %copy-start) | copy-done | bytes 3145752
  24.9 1.9 %copy-done.1 = bf16[1,2048,768]{2,1,0:T(8,128)(2,1)S(1)} copy-done((bf16[1,2048,768]{2,1,0:T(8,128)(2,1)S(1)}, bf16[1,2048,768]{2,1,0:T(8,128)(2,1)}, u32[]{:S(2)}) %copy-start.1) | copy-done | bytes 3145752
  26.8 1.9 %copy-done.2 = bf16[1,768,2048]{2,1,0:T(8,128)(2,1)S(1)} copy-done((bf16[1,768,2048]{2,1,0:T(8,128)(2,1)S(1)}, bf16[1,768,2048]{2,1,0:T(8,128)(2,1)}, u32[]{:S(2)}) %copy-start.2) | copy-done | bytes 3145752
  28.7 0.7 %copy-done.3 = f32[1,2048]{1,0:T(1,128)S(1)} copy-done((f32[1,2048]{1,0:T(1,128)S(1)}, f32[1,2048]{1,0:T(1,128)}, u32[]{:S(2)}) %copy-start.3) | copy-done | bytes 8216
  29.4 9.3 %experts.1 = (bf16[64,2048]{1,0:T(8,128)(2,1)S(1)}, bf16[64,2048]{1,0:T(8,128)(2,1)S(1)}) custom-call(s32[2]{0:T(128)S(1)} %pad_add_fusion.where_ref, bf16[96,2176]{1,0:T(8,128)(2,1)S(1)} %constant_dynamic-update-slice_fusion.near_ref, bf16[96,2176]{1,0:T(8,128)(2,1)S(1)} %collective-permute-done.5.far_ref, f32[1,2048]{1,0:T(1,128)S(1)} %copy-done.3, ...), custom_call_target="tpu_custom_call" | custom-call | tf_op jit(solution)/shard_map/experts/pallas_call | solution.py:305
  38.7 0.1 collective-permute-start.7
  38.8 1.5 %collective-permute-done.7 = bf16[64,2048]{1,0:T(8,128)(2,1)S(1)} collective-permute-done((bf16[64,2048]{1,0:T(8,128)(2,1)S(1)}, bf16[64,2048]{1,0:T(8,128)(2,1)S(1)}, u32[]{:S(2)}, u32[]{:S(2)}) %collective-permute-start.7) | collective-permute-done | bytes 262176 | tf_op jit(solution)/shard_map/ppermute | solution.py:181
  40.3 0.1 add_convert_fusion
  40.4 1.6 %collective-permute-start.8 = (bf16[16,2048]{1,0:T(8,128)(2,1)S(1)}, bf16[16,2048]{1,0:T(8,128)(2,1)S(1)}, u32[]{:S(2)}, u32[]{:S(2)}) collective-permute-start(bf16[16,2048]{1,0:T(8,128)(2,1)S(1)} %get-tuple-element.10), channel_id=1, source_target_pairs={{0,2},{1,3},{2,0},{3,1},{4,6},{5,7},{6,4},{7,5},{8,10},{9,11},{10,... | collective-permute-start | bytes 196616 | tf_op jit(solution)/shard_map/ppermute | solution.py:181
  41.9 1.1 %collective-permute-start.10 = (bf16[16,2048]{1,0:T(8,128)(2,1)S(1)}, bf16[16,2048]{1,0:T(8,128)(2,1)S(1)}, u32[]{:S(2)}, u32[]{:S(2)}) collective-permute-start(bf16[16,2048]{1,0:T(8,128)(2,1)S(1)} %get-tuple-element.11), channel_id=1, source_target_pairs={{0,6},{1,7},{2,4},{3,5},{4,2},{5,3},{6,0},{7,1},{8,14},{9,15},{10,... | collective-permute-start | bytes 196616 | tf_op jit(solution)/shard_map/ppermute | solution.py:181
  43.0 0.9 %collective-permute-start.9 = (bf16[16,2048]{1,0:T(8,128)(2,1)S(1)}, bf16[16,2048]{1,0:T(8,128)(2,1)S(1)}, u32[]{:S(2)}, u32[]{:S(2)}) collective-permute-start(bf16[16,2048]{1,0:T(8,128)(2,1)S(1)} %get-tuple-element.12), channel_id=1, source_target_pairs={{0,4},{1,5},{2,6},{3,7},{4,0},{5,1},{6,2},{7,3},{8,12},{9,13},{10,... | collective-permute-start | bytes 196616 | tf_op jit(solution)/shard_map/ppermute | solution.py:181
  43.9 0.8 %collective-permute-done.8 = bf16[16,2048]{1,0:T(8,128)(2,1)S(1)} collective-permute-done((bf16[16,2048]{1,0:T(8,128)(2,1)S(1)}, bf16[16,2048]{1,0:T(8,128)(2,1)S(1)}, u32[]{:S(2)}, u32[]{:S(2)}) %collective-permute-start.8) | collective-permute-done | bytes 65568 | tf_op jit(solution)/shard_map/ppermute | solution.py:181
  44.7 2.8 %collective-permute-done.10 = bf16[16,2048]{1,0:T(8,128)(2,1)S(1)} collective-permute-done((bf16[16,2048]{1,0:T(8,128)(2,1)S(1)}, bf16[16,2048]{1,0:T(8,128)(2,1)S(1)}, u32[]{:S(2)}, u32[]{:S(2)}) %collective-permute-start.10) | collective-permute-done | bytes 65568 | tf_op jit(solution)/shard_map/ppermute | solution.py:181
  47.6 3.3 %collective-permute-start.11 = (bf16[8,2048]{1,0:T(8,128)(2,1)S(1)}, bf16[8,2048]{1,0:T(8,128)(2,1)S(1)}, u32[]{:S(2)}, u32[]{:S(2)}) collective-permute-start(bf16[8,2048]{1,0:T(8,128)(2,1)S(1)} %broadcast_select_fusion.1), channel_id=1, source_target_pairs={{0,24},{1,25},{2,26},{3,27},{4,28},{5,29},{6,30},{7,31},{8,16},{9,... | collective-permute-start | bytes 98312 | tf_op jit(solution)/shard_map/ppermute | solution.py:181
  50.9 2.5 %collective-permute-done.11 = bf16[8,2048]{1,0:T(8,128)(2,1)S(1)} collective-permute-done((bf16[8,2048]{1,0:T(8,128)(2,1)S(1)}, bf16[8,2048]{1,0:T(8,128)(2,1)S(1)}, u32[]{:S(2)}, u32[]{:S(2)}) %collective-permute-start.11) | collective-permute-done | bytes 32800 | tf_op jit(solution)/shard_map/ppermute | solution.py:181
  53.4 0.6 %select_bitcast_fusion = (bf16[1,8,2048]{2,1,0:T(8,128)(2,1)}, bf16[1,8,2048]{2,1,0:T(8,128)(2,1)}) fusion(pred[]{:T(512)S(6)} %eq.3, bf16[8,2048]{1,0:T(8,128)(2,1)S(1)} %collective-permute-done.11, bf16[16,2048]{1,0:T(8,128)(2,1)S(1)} %add_convert_fusion.1), kind=kLoop, calls=%fused_computation.15 | loop fusion | flops 114688 | bytes 163841 | tf_op jit(solution)/shard_map/broadcast_in_dim | solution.py:365
  (17 shorter events, 0.2 us)
Async XLA Ops:
  2.9 5.5 %collective-permute-start.1 = (bf16[16,2176]{1,0:T(8,128)(2,1)S(1)}, bf16[16,2176]{1,0:T(8,128)(2,1)S(1)}, u32[]{:S(2)}, u32[]{:S(2)}) collective-permute-start(bf16[16,2176]{1,0:T(8,128)(2,1)S(1)} %fusion.4), channel_id=1, source_target_pairs={{0,16},{1,17},{2,18},{3,19},{4,20},{5,21},{6,22},{7,23},{8,24},{9,... | collective-permute-start | bytes 208904 | tf_op jit(solution)/shard_map/ppermute | solution.py:181
  5.8 5.6 %collective-permute-start = (bf16[16,2176]{1,0:T(8,128)(2,1)S(1)}, bf16[16,2176]{1,0:T(8,128)(2,1)S(1)}, u32[]{:S(2)}, u32[]{:S(2)}) collective-permute-start(bf16[16,2176]{1,0:T(8,128)(2,1)S(1)} %fusion.4), channel_id=1, source_target_pairs={{0,8},{1,9},{2,10},{3,11},{4,12},{5,13},{6,14},{7,15},{8,0},{9,1},... | collective-permute-start | bytes 208904 | tf_op jit(solution)/shard_map/ppermute | solution.py:181
  11.4 5.1 %collective-permute-start.2 = (bf16[24,2176]{1,0:T(8,128)(2,1)S(1)}, bf16[24,2176]{1,0:T(8,128)(2,1)S(1)}, u32[]{:S(2)}, u32[]{:S(2)}) collective-permute-start(bf16[24,2176]{1,0:T(8,128)(2,1)S(1)} %pad_maximum_fusion), channel_id=1, source_target_pairs={{0,2},{1,3},{2,0},{3,1},{4,6},{5,7},{6,4},{7,5},{8,10},{9,11},{10,... | collective-permute-start | bytes 313352 | tf_op jit(solution)/shard_map/ppermute | solution.py:181
  13.0 5.9 %collective-permute-start.4 = (bf16[24,2176]{1,0:T(8,128)(2,1)S(1)}, bf16[24,2176]{1,0:T(8,128)(2,1)S(1)}, u32[]{:S(2)}, u32[]{:S(2)}) collective-permute-start(bf16[24,2176]{1,0:T(8,128)(2,1)S(1)} %pad_maximum_fusion), channel_id=1, source_target_pairs={{0,6},{1,7},{2,4},{3,5},{4,2},{5,3},{6,0},{7,1},{8,14},{9,15},{10,... | collective-permute-start | bytes 313352 | tf_op jit(solution)/shard_map/ppermute | solution.py:181
  14.3 4.7 %collective-permute-start.3 = (bf16[24,2176]{1,0:T(8,128)(2,1)S(1)}, bf16[24,2176]{1,0:T(8,128)(2,1)S(1)}, u32[]{:S(2)}, u32[]{:S(2)}) collective-permute-start(bf16[24,2176]{1,0:T(8,128)(2,1)S(1)} %pad_maximum_fusion), channel_id=1, source_target_pairs={{0,4},{1,5},{2,6},{3,7},{4,0},{5,1},{6,2},{7,3},{8,12},{9,13},{10,... | collective-permute-start | bytes 313352 | tf_op jit(solution)/shard_map/ppermute | solution.py:181
  19.0 4.0 %collective-permute-start.5 = (bf16[96,2176]{1,0:T(8,128)(2,1)S(1)}, bf16[96,2176]{1,0:T(8,128)(2,1)S(1)}, u32[]{:S(2)}, u32[]{:S(2)}) collective-permute-start(bf16[96,2176]{1,0:T(8,128)(2,1)S(1)} %constant_dynamic-update-slice_fusion.near_ref), channel_id=1, source_target_pairs={{0,1},{1,0},{2,3},{3,2},{4,5},{5,4},{6,7},{7,6},{8,9},{9,8},{10,11... | collective-permute-start | bytes 1253384 | tf_op jit(solution)/shard_map/ppermute | solution.py:181
  19.1 3.9 %collective-permute-start.6 = (f32[1,2048]{1,0:T(1,128)}, f32[1,2048]{1,0:T(1,128)S(1)}, u32[]{:S(2)}, u32[]{:S(2)}) collective-permute-start(f32[1,2048]{1,0:T(1,128)} %gain_ref.1), channel_id=1, source_target_pairs={{0,16},{1,17},{2,18},{3,19},{4,20},{5,21},{6,22},{7,23},{8,24},{9,... | collective-permute-start | bytes 24584 | tf_op jit(solution)/shard_map/ppermute | solution.py:181
  23.0 1.9 %copy-start = (bf16[1,2048,768]{2,1,0:T(8,128)(2,1)S(1)}, bf16[1,2048,768]{2,1,0:T(8,128)(2,1)}, u32[]{:S(2)}) copy-start(bf16[1,2048,768]{2,1,0:T(8,128)(2,1)} %param.17) | copy-start | bytes 9437188
  24.9 1.9 %copy-start.1 = (bf16[1,2048,768]{2,1,0:T(8,128)(2,1)S(1)}, bf16[1,2048,768]{2,1,0:T(8,128)(2,1)}, u32[]{:S(2)}) copy-start(bf16[1,2048,768]{2,1,0:T(8,128)(2,1)} %param.18) | copy-start | bytes 9437188
  26.8 1.9 %copy-start.2 = (bf16[1,768,2048]{2,1,0:T(8,128)(2,1)S(1)}, bf16[1,768,2048]{2,1,0:T(8,128)(2,1)}, u32[]{:S(2)}) copy-start(bf16[1,768,2048]{2,1,0:T(8,128)(2,1)} %param.19) | copy-start | bytes 9437188
  28.7 0.7 %copy-start.3 = (f32[1,2048]{1,0:T(1,128)S(1)}, f32[1,2048]{1,0:T(1,128)}, u32[]{:S(2)}) copy-start(f32[1,2048]{1,0:T(1,128)} %gain_ref.1) | copy-start | bytes 24580
  38.7 1.6 %collective-permute-start.7 = (bf16[64,2048]{1,0:T(8,128)(2,1)S(1)}, bf16[64,2048]{1,0:T(8,128)(2,1)S(1)}, u32[]{:S(2)}, u32[]{:S(2)}) collective-permute-start(bf16[64,2048]{1,0:T(8,128)(2,1)S(1)} %get-tuple-element.5), channel_id=1, source_target_pairs={{0,1},{1,0},{2,3},{3,2},{4,5},{5,4},{6,7},{7,6},{8,9},{9,8},{10,11... | collective-permute-start | bytes 786440 | tf_op jit(solution)/shard_map/ppermute | solution.py:181
  40.4 4.3 %collective-permute-start.8 = (bf16[16,2048]{1,0:T(8,128)(2,1)S(1)}, bf16[16,2048]{1,0:T(8,128)(2,1)S(1)}, u32[]{:S(2)}, u32[]{:S(2)}) collective-permute-start(bf16[16,2048]{1,0:T(8,128)(2,1)S(1)} %get-tuple-element.10), channel_id=1, source_target_pairs={{0,2},{1,3},{2,0},{3,1},{4,6},{5,7},{6,4},{7,5},{8,10},{9,11},{10,... | collective-permute-start | bytes 196616 | tf_op jit(solution)/shard_map/ppermute | solution.py:181
  41.9 5.6 %collective-permute-start.10 = (bf16[16,2048]{1,0:T(8,128)(2,1)S(1)}, bf16[16,2048]{1,0:T(8,128)(2,1)S(1)}, u32[]{:S(2)}, u32[]{:S(2)}) collective-permute-start(bf16[16,2048]{1,0:T(8,128)(2,1)S(1)} %get-tuple-element.11), channel_id=1, source_target_pairs={{0,6},{1,7},{2,4},{3,5},{4,2},{5,3},{6,0},{7,1},{8,14},{9,15},{10,... | collective-permute-start | bytes 196616 | tf_op jit(solution)/shard_map/ppermute | solution.py:181
  43.0 4.5 %collective-permute-start.9 = (bf16[16,2048]{1,0:T(8,128)(2,1)S(1)}, bf16[16,2048]{1,0:T(8,128)(2,1)S(1)}, u32[]{:S(2)}, u32[]{:S(2)}) collective-permute-start(bf16[16,2048]{1,0:T(8,128)(2,1)S(1)} %get-tuple-element.12), channel_id=1, source_target_pairs={{0,4},{1,5},{2,6},{3,7},{4,0},{5,1},{6,2},{7,3},{8,12},{9,13},{10,... | collective-permute-start | bytes 196616 | tf_op jit(solution)/shard_map/ppermute | solution.py:181
  47.6 5.8 %collective-permute-start.11 = (bf16[8,2048]{1,0:T(8,128)(2,1)S(1)}, bf16[8,2048]{1,0:T(8,128)(2,1)S(1)}, u32[]{:S(2)}, u32[]{:S(2)}) collective-permute-start(bf16[8,2048]{1,0:T(8,128)(2,1)S(1)} %broadcast_select_fusion.1), channel_id=1, source_target_pairs={{0,24},{1,25},{2,26},{3,27},{4,28},{5,29},{6,30},{7,31},{8,16},{9,... | collective-permute-start | bytes 98312 | tf_op jit(solution)/shard_map/ppermute | solution.py:181

commit v2 on v1

--- a/solution.py
+++ b/solution.py
@@ -182,29 +182,19 @@
 
 
 def expert_kernel(
-    where_ref, near_ref, far_ref, gain_ref, gain_far_ref, router_ref,
-    gate_hbm, up_hbm, down_hbm, kept_ref, sent_ref,
-    gate_ref, up_ref, down_ref, sems,
+    where_ref, near_ref, far_ref, across_ref, gain_ref, router_ref,
+    gate_ref, up_ref, down_ref, kept_ref, sent_ref,
 ):
     width = gain_ref.shape[1]
     hidden_count = gate_ref.shape[1]
     step = 256 if hidden_count % 256 == 0 else hidden_count
     pieces = hidden_count // step
-    copies = []
-    for piece in range(pieces):
-        cols = pl.ds(piece * step, step)
-        copies.append((
-            pltpu.make_async_copy(gate_hbm.at[:, cols], gate_ref.at[:, cols], sems.at[0, piece]),
-            pltpu.make_async_copy(up_hbm.at[:, cols], up_ref.at[:, cols], sems.at[1, piece]),
-            pltpu.make_async_copy(down_hbm.at[cols, :], down_ref.at[cols, :], sems.at[2, piece]),
-        ))
-        for copy in copies[-1]:
-            copy.start()
-
     first_section = where_ref[0] == 0
     own_expert = where_ref[1]
     gain_here = gain_ref[...]
-    gain_there = gain_far_ref[...]
+    packed = across_ref[...].astype(jnp.float32)[:, width + LANES :]
+    packed = packed[:, :LANES] + packed[:, LANES:]
+    gain_there = jnp.concatenate([packed[k : k + 1] for k in range(16)], axis=1)
     gain_f = jnp.where(first_section, gain_here, gain_there)
     gain_b = jnp.where(first_section, gain_there, gain_here)
 
@@ -225,8 +215,8 @@
     grads_low = grads.astype(jnp.bfloat16)
 
     router = router_ref[...]
-    experts = router.shape[1]
-    logits = jnp.dot(normed, router, preferred_element_type=jnp.float32)
+    contract = (((1,), (1,)), ((), ()))
+    logits = lax.dot_general(normed, router, contract, preferred_element_type=jnp.float32)
     labels = lax.broadcasted_iota(jnp.int32, logits.shape, 1)
     labels_real = labels.astype(jnp.float32)
     chosen = routes[:, 0:1] == labels_real
@@ -237,13 +227,10 @@
     own = labels == own_expert
     gate_own = jnp.sum(jnp.where(own, gates, 0.0), axis=-1, keepdims=True)
 
-    contract = (((1,), (1,)), ((), ()))
     expert_out = None
     pair_grad = None
     for piece in range(pieces):
         cols = slice(piece * step, piece * step + step)
-        for copy in copies[piece]:
-            copy.wait()
         gate_mat = gate_ref[:, cols]
         up_mat = up_ref[:, cols]
         down_mat = down_ref[cols, :]
@@ -272,12 +259,8 @@
     spread_high = spread.astype(jnp.bfloat16)
     spread_low = (spread - spread_high.astype(jnp.float32)).astype(jnp.bfloat16)
     d_normed = gate_b * pair_grad
-    d_normed = d_normed + lax.dot_general(
-        spread_high, router, contract, preferred_element_type=jnp.float32
-    )
-    d_normed = d_normed + lax.dot_general(
-        spread_low, router, contract, preferred_element_type=jnp.float32
-    )
+    d_normed = d_normed + jnp.dot(spread_high, router, preferred_element_type=jnp.float32)
+    d_normed = d_normed + jnp.dot(spread_low, router, preferred_element_type=jnp.float32)
     d_unit = d_normed * gain_b
     unit_b = unit[half:]
     out_b = factor[half:] * (
@@ -297,25 +280,113 @@
 TOP_COUNT = 8
 
 
-def run_experts(where, near, far, gain_row, gain_far, router, gate_mat, up_mat, down_mat):
-    width, hidden_count = gate_mat.shape
+def in_hbm(array):
+    return pltpu.with_memory_space_constraint(array, pltpu.HBM)
+
+
+def pack_kernel(
+    where_ref, fwd_act, fwd_routes, bwd_saved, bwd_grad, bwd_routes, gain, router,
+    rows_ref, gain_ref, router_ref, acts_ref, grads_ref, routes_ref, sems,
+):
+    first_section = where_ref[0] == 0
+    grad_copy = pltpu.make_async_copy(bwd_grad.at[0], grads_ref, sems.at[0])
+    gain_copy = pltpu.make_async_copy(gain, gain_ref, sems.at[1])
+    router_copy = pltpu.make_async_copy(router, router_ref, sems.at[4])
+    grad_copy.start()
+    gain_copy.start()
+    router_copy.start()
+
+    @pl.when(first_section)
+    def _():
+        pltpu.make_async_copy(fwd_act.at[0], acts_ref, sems.at[2]).start()
+        pltpu.make_async_copy(fwd_routes.at[0], routes_ref, sems.at[3]).start()
+
+    @pl.when(jnp.logical_not(first_section))
+    def _():
+        pltpu.make_async_copy(bwd_saved.at[0], acts_ref, sems.at[2]).start()
+        pltpu.make_async_copy(bwd_routes.at[0], routes_ref, sems.at[3]).start()
+
+    grad_copy.wait()
+    gain_copy.wait()
+    router_copy.wait()
+    pltpu.make_async_copy(fwd_act.at[0], acts_ref, sems.at[2]).wait()
+    pltpu.make_async_copy(fwd_routes.at[0], routes_ref, sems.at[3]).wait()
+
+    body = jnp.concatenate(
+        [acts_ref[...].astype(jnp.float32), grads_ref[...].astype(jnp.float32)], axis=0
+    )
+    rows = body.shape[0]
+    routes = routes_ref[...].astype(jnp.float32)
+    routes = jnp.concatenate([routes, jnp.zeros((8, LANES - TOP_COUNT), jnp.float32)], axis=1)
+    tail = jnp.concatenate([routes, jnp.zeros((rows - 8, LANES), jnp.float32)], axis=0)
+    gain_row = gain_ref[...]
+    gain_rows = jnp.concatenate(
+        [gain_row[:, LANES * k : LANES * k + LANES] for k in range(rows)], axis=0
+    )
+    gain_high = gain_rows.astype(jnp.bfloat16).astype(jnp.float32)
+    rows_ref[...] = jnp.concatenate(
+        [body, tail, gain_high, gain_rows - gain_high], axis=1
+    ).astype(jnp.bfloat16)
+
+
+def pack_rows(where, *arrays):
+    fwd_act, fwd_routes, _, _, _, gain, router = arrays
+    count, width = fwd_act.shape[1:]
+    vmem = pl.BlockSpec(memory_space=pltpu.VMEM)
+    return pl.pallas_call(
+        pack_kernel,
+        out_shape=[
+            jax.ShapeDtypeStruct((2 * count, width + 3 * LANES), jnp.bfloat16),
+            jax.ShapeDtypeStruct(gain.shape, gain.dtype),
+            jax.ShapeDtypeStruct(router.shape, router.dtype),
+        ],
+        in_specs=[pl.BlockSpec(memory_space=pltpu.SMEM)]
+        + [pl.BlockSpec(memory_space=pltpu.HBM)] * 7,
+        out_specs=[vmem] * 3,
+        scratch_shapes=[
+            pltpu.VMEM((count, width), jnp.bfloat16),
+            pltpu.VMEM((count, width), jnp.bfloat16),
+            pltpu.VMEM(fwd_routes.shape[1:], jnp.int32),
+            pltpu.SemaphoreType.DMA((5,)),
+        ],
+        compiler_params=pltpu.CompilerParams(vmem_limit_bytes=4 * 1024 * 1024),
+        name="pack",
+    )(where, *[in_hbm(x) for x in arrays])
+
+
+def fetch_kernel(weights, held_ref, sem):
+    copy = pltpu.make_async_copy(weights, held_ref, sem)
+    copy.start()
+    copy.wait()
+
+
+def fetched(weights):
+    return pl.pallas_call(
+        fetch_kernel,
+        out_shape=jax.ShapeDtypeStruct(weights.shape, weights.dtype),
+        in_specs=[pl.BlockSpec(memory_space=pltpu.HBM)],
+        out_specs=pl.BlockSpec(memory_space=pltpu.VMEM),
+        scratch_shapes=[pltpu.SemaphoreType.DMA],
+        compiler_params=pltpu.CompilerParams(vmem_limit_bytes=4 * 1024 * 1024),
+        cost_estimate=pl.CostEstimate(
+            flops=0, bytes_accessed=2 * weights.size * weights.dtype.itemsize, transcendentals=0
+        ),
+        name="fetch",
+    )(in_hbm(weights))
+
+
+def run_experts(where, near, far, across, gain_row, router, gate_mat, up_mat, down_mat):
+    width = gate_mat.shape[0]
     rows = SQUARE // 2 * 16
     vmem = pl.BlockSpec(memory_space=pltpu.VMEM)
-    hbm = pl.BlockSpec(memory_space=pl.ANY)
     return pl.pallas_call(
         expert_kernel,
         out_shape=[jax.ShapeDtypeStruct((rows, width), jnp.bfloat16)] * 2,
-        in_specs=[pl.BlockSpec(memory_space=pltpu.SMEM)] + [vmem] * 5 + [hbm] * 3,
+        in_specs=[pl.BlockSpec(memory_space=pltpu.SMEM)] + [vmem] * 8,
         out_specs=[vmem] * 2,
-        scratch_shapes=[
-            pltpu.VMEM((width, hidden_count), jnp.bfloat16),
-            pltpu.VMEM((width, hidden_count), jnp.bfloat16),
-            pltpu.VMEM((hidden_count, width), jnp.bfloat16),
-            pltpu.SemaphoreType.DMA((3, max(1, hidden_count // 256))),
-        ],
-        compiler_params=pltpu.CompilerParams(vmem_limit_bytes=40 * 1024 * 1024),
+        compiler_params=pltpu.CompilerParams(vmem_limit_bytes=32 * 1024 * 1024),
         name="experts",
-    )(where, near, far, gain_row, gain_far, router, gate_mat, up_mat, down_mat)
+    )(where, near, far, across, gain_row, router, gate_mat, up_mat, down_mat)
 
 
 def added(*blocks):
@@ -329,28 +400,23 @@
     first = section == 0
     where = jnp.stack([section, lax.axis_index("expert")]).astype(jnp.int32)
 
-    acts = jnp.where(first, fwd_act[0], bwd_saved[0])
-    routes = jnp.where(first, fwd_routes[0], bwd_routes[0]).astype(jnp.bfloat16)
-    tail = jnp.pad(routes, ((0, 0), (0, LANES - routes.shape[1])))
-    own_rows = jnp.concatenate(
-        [
-            jnp.concatenate([acts, tail], axis=1),
-            jnp.pad(bwd_grad[0], ((0, 0), (0, LANES))),
-        ],
-        axis=0,
+    own_rows, gain_row, router_rows = pack_rows(
+        where, fwd_act, fwd_routes, bwd_saved, bwd_grad, bwd_routes, norm_gain, router.T
     )
     across = swapped(own_rows, SECTION)
     along = swapped(own_rows, HALF)
-    gain_far = swapped(norm_gain, SECTION)
-    forward = jnp.where(first, along[:8], across[:8])
-    backward = jnp.where(first, across, along)
+    gate_mat, up_mat = fetched(w_gate[0]), fetched(w_up[0])
+    used = norm_gain.shape[1] + LANES
+    forward = jnp.where(first, along[:8, :used], across[:8, :used])
+    backward = jnp.where(first, across[:, :used], along[:, :used])
     mine = jnp.concatenate([forward, backward], axis=0)
+    mine, gate_mat, up_mat = lax.optimization_barrier((mine, gate_mat, up_mat))
+    down_mat = fetched(lax.optimization_barrier((w_down[0], mine))[0])
     near = jnp.concatenate([mine] + [swapped(mine, k) for k in (2, 4, 6)], axis=0)
+    near, down_mat = lax.optimization_barrier((near, down_mat))
     far = swapped(near, CORE)
 
-    kept, sent = run_experts(
-        where, near, far, norm_gain, gain_far, router, w_gate[0], w_up[0], w_down[0]
-    )
+    kept, sent = run_experts(where, near, far, across, gain_row, router_rows, gate_mat, up_mat, down_mat)
 
     chip = added(kept, swapped(sent, CORE)).astype(jnp.bfloat16)
     total = added(
@@ -364,6 +430,16 @@
     fwd_next = jnp.where(first, nothing, result)[None]
     grad_prev = jnp.where(first, result, nothing)[None]
     return (fwd_next, grad_prev)
+
+
+def per_device(fwd_act, fwd_routes, *rest):
+    sections, devices = lax.axis_size("section"), lax.axis_size("expert")
+    tokens, top_count = fwd_routes.shape[1:]
+    router = rest[4]
+    paired = sections == 2 and devices == 2 * SQUARE and router.shape == (16 * LANES, devices)
+    paired = paired and tokens == 8 and top_count == TOP_COUNT
+    plan = paired_plan if paired else routed_plan
+    return plan(fwd_act, fwd_routes, *rest)
 
 
 def solution(mesh):
@@ -380,8 +456,6 @@
         P("expert", None, None),
     )
     out_specs = (P("section", "expert", None), P("section", "expert", None))
-    shape = dict(mesh.shape)
-    paired = shape["section"] == 2 and shape["expert"] == 2 * SQUARE
     return jax.shard_map(
-        paired_plan if paired else routed_plan, mesh=mesh, in_specs=in_specs, out_specs=out_specs, check_vma=False
-    )
+        per_device, mesh=mesh, in_specs=in_specs, out_specs=out_specs, check_vma=False
+    )

time: 54.5 us -> 42.8 us (0.79)
  local copies, waits for them, and re-layouts: 7.53 us -> 0.02 us
  waiting for transfers between devices: 16.7 us -> 12.5 us
  Pallas kernels: 9.3 us -> 12.9 us
  other arithmetic: 3.12 us -> 0.9 us
  starting transfers between devices: 16.6 us -> 15.5 us
    unnamed x11 -> x0, local copies, waits for them, and re-layouts: 7.5 us -> none
    pallas_call x0 -> x4, Pallas kernels: none -> 7.17 us  [the longest x3 5.69 us: fetched(): pl.pallas_call(fetch_kernel, out_shape=jax.ShapeDtypeStruct(weights.shape...]
    ppermute x12 -> x11, waiting for transfers between devices: 16.7 us -> 12.5 us  [swapped(): return lax.ppermute(block, AXES, [(i, i ^ distance) for i in range(count)])]
    pallas_call x1, Pallas kernels: 9.3 us -> 5.69 us  [run_experts(): pl.pallas_call(expert_kernel, out_shape=[jax.ShapeDtypeStruct((rows, widt...]
    ppermute x12 -> x11, starting transfers between devices: 16.6 us -> 15.5 us  [swapped(): return lax.ppermute(block, AXES, [(i, i ^ distance) for i in range(count)])]
    select_n x1 -> x2, other arithmetic: 0.77 us -> 0.02 us  [the longest x1 0.02 us: paired_plan(): backward = jnp.where(first, across[:, :used], along[:, :used])]
    concatenate x1, other arithmetic: 0.76 us -> 0.03 us  [paired_plan(): jnp.concatenate([mine] + [swapped(mine, k) for k in (2, 4, 6)], axis=0)]
    convert_element_type x1 -> x0, other arithmetic: 0.7 us -> none  [paired_plan(): routes = jnp.where(first, fwd_routes[0], bwd_routes[0]).astype(jnp.bfloat16)]
  transfers between devices with their start and end apart: 12 -> 11, of which waited for: 8 -> 10; matrix products, arithmetic and copies ran while one was open for 2% -> 0% of each run, Pallas kernels for 0% -> 13%
where the time goes in v2:
time: 42.8 us; the launch traced here: 42.5 us
  starting transfers between devices  15.5 us (36%)
  Pallas kernels  12.9 us (30%)
  waiting for transfers between devices  12.5 us (29%)
  other arithmetic  0.9 us (2%)
  between operations  0.74 us (2%)
    ppermute x11, starting transfers between devices, swapped(): return lax.ppermute(block, AXES, [(i, i ^ distance) for i in range(count)])  15.5 us
    ppermute x11, waiting for transfers between devices, swapped(): return lax.ppermute(block, AXES, [(i, i ^ distance) for i in range(count)])  12.5 us
    pallas_call x3, Pallas kernels, fetched(): pl.pallas_call(fetch_kernel, out_shape=jax.ShapeDtypeStruct(weights.shape...  5.69 us
    pallas_call x1, Pallas kernels, run_experts(): pl.pallas_call(expert_kernel, out_shape=[jax.ShapeDtypeStruct((rows, widt...  5.69 us
    pallas_call x1, Pallas kernels, pack_rows(): pl.pallas_call(pack_kernel, out_shape=[jax.ShapeDtypeStruct((2 * count, w...  1.48 us
  transfers between devices with their start and end apart: 11, of which 10 were waited for; matrix products, arithmetic and copies ran while one was open for 0% of the time, Pallas kernels for 13%

profile of v2, /device:TPU:0, one launch (start us, length us, event | category | flops | bytes accessed | tf_op | source)
XLA Modules:
  0.0 42.5 jit_solution(7950469249408906032)
XLA Ops:
  0.6 0.1 pad_add_fusion.where_ref
  0.7 1.5 %pack.1 = (bf16[16,2432]{1,0:T(8,128)(2,1)S(1)}, f32[1,2048]{1,0:T(1,128)S(1)}, bf16[16,2048]{1,0:T(8,128)(2,1)S(1)}) custom-call(s32[2]{0:T(128)S(1)} %pad_add_fusion.where_ref, bf16[1,8,2048]{2,1,0:T(8,128)(2,1)} %fwd_act.1, s32[1,8,8]{2,1,0:T(8,128)} %fwd_routes.1, bf16[1,8,2048]{2,1,0:T(8,128)(2,1)} %bwd_saved.1, bf16[1,8,2048]{2,1,0:T(8,128)(2,1)} %bwd_grad.1, ...), custom_call_target="tpu_custom_call" | custom-call | tf_op jit(solution)/shard_map/pack/pallas_call | solution.py:336
  2.2 3.0 %collective-permute-start.1 = (bf16[16,2432]{1,0:T(8,128)(2,1)S(1)}, bf16[16,2432]{1,0:T(8,128)(2,1)S(1)}, u32[]{:S(2)}, u32[]{:S(2)}) collective-permute-start(bf16[16,2432]{1,0:T(8,128)(2,1)S(1)} %get-tuple-element.13), channel_id=1, source_target_pairs={{0,16},{1,17},{2,18},{3,19},{4,20},{5,21},{6,22},{7,23},{8,24},{9,... | collective-permute-start | bytes 233480 | tf_op jit(solution)/shard_map/ppermute | solution.py:181
  5.2 2.6 %collective-permute-start = (bf16[16,2432]{1,0:T(8,128)(2,1)S(1)}, bf16[16,2432]{1,0:T(8,128)(2,1)S(1)}, u32[]{:S(2)}, u32[]{:S(2)}) collective-permute-start(bf16[16,2432]{1,0:T(8,128)(2,1)S(1)} %get-tuple-element.13), channel_id=1, source_target_pairs={{0,8},{1,9},{2,10},{3,11},{4,12},{5,13},{6,14},{7,15},{8,0},{9,1},... | collective-permute-start | bytes 233480 | tf_op jit(solution)/shard_map/ppermute | solution.py:181
  7.8 1.9 %fetch.3.gate_ref = bf16[2048,768]{1,0:T(8,128)(2,1)S(1)} custom-call(bf16[2048,768]{1,0:T(8,128)(2,1)} %bitcast.10), custom_call_target="tpu_custom_call" | custom-call | bytes 6291456 | tf_op jit(solution)/shard_map/fetch/pallas_call | solution.py:364
  9.7 1.9 %fetch.4.up_ref = bf16[2048,768]{1,0:T(8,128)(2,1)S(1)} custom-call(bf16[2048,768]{1,0:T(8,128)(2,1)} %bitcast.11), custom_call_target="tpu_custom_call" | custom-call | bytes 6291456 | tf_op jit(solution)/shard_map/fetch/pallas_call | solution.py:364
  11.6 0.0 collective-permute-done.1.across_ref
  11.6 0.1 collective-permute-done
  11.8 2.5 %collective-permute-start.4 = (bf16[24,2176]{1,0:T(8,128)(2,1)S(1)}, bf16[24,2176]{1,0:T(8,128)(2,1)S(1)}, u32[]{:S(2)}, u32[]{:S(2)}) collective-permute-start(bf16[24,2176]{1,0:T(8,128)(2,1)S(1)} %pad_maximum_fusion.1), channel_id=1, source_target_pairs={{0,6},{1,7},{2,4},{3,5},{4,2},{5,3},{6,0},{7,1},{8,14},{9,15},{10,... | collective-permute-start | bytes 313352 | tf_op jit(solution)/shard_map/ppermute | solution.py:181
  14.3 0.6 %collective-permute-start.3 = (bf16[24,2176]{1,0:T(8,128)(2,1)S(1)}, bf16[24,2176]{1,0:T(8,128)(2,1)S(1)}, u32[]{:S(2)}, u32[]{:S(2)}) collective-permute-start(bf16[24,2176]{1,0:T(8,128)(2,1)S(1)} %pad_maximum_fusion.1), channel_id=1, source_target_pairs={{0,4},{1,5},{2,6},{3,7},{4,0},{5,1},{6,2},{7,3},{8,12},{9,13},{10,... | collective-permute-start | bytes 313352 | tf_op jit(solution)/shard_map/ppermute | solution.py:181
  14.9 0.5 %collective-permute-start.2 = (bf16[24,2176]{1,0:T(8,128)(2,1)S(1)}, bf16[24,2176]{1,0:T(8,128)(2,1)S(1)}, u32[]{:S(2)}, u32[]{:S(2)}) collective-permute-start(bf16[24,2176]{1,0:T(8,128)(2,1)S(1)} %pad_maximum_fusion.1), channel_id=1, source_target_pairs={{0,2},{1,3},{2,0},{3,1},{4,6},{5,7},{6,4},{7,5},{8,10},{9,11},{10,... | collective-permute-start | bytes 313352 | tf_op jit(solution)/shard_map/ppermute | solution.py:181
  15.4 1.9 %fetch.5.down_ref = bf16[768,2048]{1,0:T(8,128)(2,1)S(1)} custom-call(bf16[768,2048]{1,0:T(8,128)(2,1)} %bitcast.12), custom_call_target="tpu_custom_call" | custom-call | bytes 6291456 | tf_op jit(solution)/shard_map/fetch/pallas_call | solution.py:364
  17.3 0.8 %collective-permute-done.4 = bf16[24,2176]{1,0:T(8,128)(2,1)S(1)} collective-permute-done((bf16[24,2176]{1,0:T(8,128)(2,1)S(1)}, bf16[24,2176]{1,0:T(8,128)(2,1)S(1)}, u32[]{:S(2)}, u32[]{:S(2)}) %collective-permute-start.4) | collective-permute-done | bytes 104480 | tf_op jit(solution)/shard_map/ppermute | solution.py:181
  18.1 1.1 %collective-permute-done.3 = bf16[24,2176]{1,0:T(8,128)(2,1)S(1)} collective-permute-done((bf16[24,2176]{1,0:T(8,128)(2,1)S(1)}, bf16[24,2176]{1,0:T(8,128)(2,1)S(1)}, u32[]{:S(2)}, u32[]{:S(2)}) %collective-permute-start.3) | collective-permute-done | bytes 104480 | tf_op jit(solution)/shard_map/ppermute | solution.py:181
  19.2 0.3 collective-permute-done.2
  19.6 0.1 collective-permute-start.5
  19.7 1.7 %collective-permute-done.5.far_ref = bf16[96,2176]{1,0:T(8,128)(2,1)S(1)} collective-permute-done((bf16[96,2176]{1,0:T(8,128)(2,1)S(1)}, bf16[96,2176]{1,0:T(8,128)(2,1)S(1)}, u32[]{:S(2)}, u32[]{:S(2)}) %collective-permute-start.5) | collective-permute-done | bytes 417824 | tf_op jit(solution)/shard_map/ppermute | solution.py:181
  21.4 5.7 %experts.1 = (bf16[64,2048]{1,0:T(8,128)(2,1)S(1)}, bf16[64,2048]{1,0:T(8,128)(2,1)S(1)}) custom-call(s32[2]{0:T(128)S(1)} %pad_add_fusion.where_ref, bf16[96,2176]{1,0:T(8,128)(2,1)S(1)} %pad_maximum_fusion.near_ref, bf16[96,2176]{1,0:T(8,128)(2,1)S(1)} %collective-permute-done.5.far_ref, bf16[16,2432]{1,0:T(8,128)(2,1)S(1)} %collective-permute-done.1.across_ref, ...), custom_call_target="tpu_custom_call" | custom-call | tf_op jit(solution)/shard_map/experts/pallas_call | solution.py:382
  27.1 0.2 collective-permute-start.6
  27.3 1.4 %collective-permute-done.6 = bf16[64,2048]{1,0:T(8,128)(2,1)S(1)} collective-permute-done((bf16[64,2048]{1,0:T(8,128)(2,1)S(1)}, bf16[64,2048]{1,0:T(8,128)(2,1)S(1)}, u32[]{:S(2)}, u32[]{:S(2)}) %collective-permute-start.6) | collective-permute-done | bytes 262176 | tf_op jit(solution)/shard_map/ppermute | solution.py:181
  28.7 0.1 add_convert_fusion
  28.8 1.1 %collective-permute-start.7 = (bf16[16,2048]{1,0:T(8,128)(2,1)S(1)}, bf16[16,2048]{1,0:T(8,128)(2,1)S(1)}, u32[]{:S(2)}, u32[]{:S(2)}) collective-permute-start(bf16[16,2048]{1,0:T(8,128)(2,1)S(1)} %get-tuple-element.24), channel_id=1, source_target_pairs={{0,2},{1,3},{2,0},{3,1},{4,6},{5,7},{6,4},{7,5},{8,10},{9,11},{10,... | collective-permute-start | bytes 196616 | tf_op jit(solution)/shard_map/ppermute | solution.py:181
  29.9 1.9 %collective-permute-start.9 = (bf16[16,2048]{1,0:T(8,128)(2,1)S(1)}, bf16[16,2048]{1,0:T(8,128)(2,1)S(1)}, u32[]{:S(2)}, u32[]{:S(2)}) collective-permute-start(bf16[16,2048]{1,0:T(8,128)(2,1)S(1)} %get-tuple-element.25), channel_id=1, source_target_pairs={{0,6},{1,7},{2,4},{3,5},{4,2},{5,3},{6,0},{7,1},{8,14},{9,15},{10,... | collective-permute-start | bytes 196616 | tf_op jit(solution)/shard_map/ppermute | solution.py:181
  31.8 0.6 %collective-permute-start.8 = (bf16[16,2048]{1,0:T(8,128)(2,1)S(1)}, bf16[16,2048]{1,0:T(8,128)(2,1)S(1)}, u32[]{:S(2)}, u32[]{:S(2)}) collective-permute-start(bf16[16,2048]{1,0:T(8,128)(2,1)S(1)} %get-tuple-element.26), channel_id=1, source_target_pairs={{0,4},{1,5},{2,6},{3,7},{4,0},{5,1},{6,2},{7,3},{8,12},{9,13},{10,... | collective-permute-start | bytes 196616 | tf_op jit(solution)/shard_map/ppermute | solution.py:181
  32.3 0.8 %collective-permute-done.7 = bf16[16,2048]{1,0:T(8,128)(2,1)S(1)} collective-permute-done((bf16[16,2048]{1,0:T(8,128)(2,1)S(1)}, bf16[16,2048]{1,0:T(8,128)(2,1)S(1)}, u32[]{:S(2)}, u32[]{:S(2)}) %collective-permute-start.7) | collective-permute-done | bytes 65568 | tf_op jit(solution)/shard_map/ppermute | solution.py:181
  33.1 2.6 %collective-permute-done.9 = bf16[16,2048]{1,0:T(8,128)(2,1)S(1)} collective-permute-done((bf16[16,2048]{1,0:T(8,128)(2,1)S(1)}, bf16[16,2048]{1,0:T(8,128)(2,1)S(1)}, u32[]{:S(2)}, u32[]{:S(2)}) %collective-permute-start.9) | collective-permute-done | bytes 65568 | tf_op jit(solution)/shard_map/ppermute | solution.py:181
  35.7 0.4 collective-permute-done.8
  36.1 2.5 %collective-permute-start.10 = (bf16[8,2048]{1,0:T(8,128)(2,1)S(1)}, bf16[8,2048]{1,0:T(8,128)(2,1)S(1)}, u32[]{:S(2)}, u32[]{:S(2)}) collective-permute-start(bf16[8,2048]{1,0:T(8,128)(2,1)S(1)} %broadcast_select_fusion), channel_id=1, source_target_pairs={{0,24},{1,25},{2,26},{3,27},{4,28},{5,29},{6,30},{7,31},{8,16},{9,... | collective-permute-start | bytes 98312 | tf_op jit(solution)/shard_map/ppermute | solution.py:181
  38.6 3.2 %collective-permute-done.10 = bf16[8,2048]{1,0:T(8,128)(2,1)S(1)} collective-permute-done((bf16[8,2048]{1,0:T(8,128)(2,1)S(1)}, bf16[8,2048]{1,0:T(8,128)(2,1)S(1)}, u32[]{:S(2)}, u32[]{:S(2)}) %collective-permute-start.10) | collective-permute-done | bytes 32800 | tf_op jit(solution)/shard_map/ppermute | solution.py:181
  41.9 0.6 %select_bitcast_fusion = (bf16[1,8,2048]{2,1,0:T(8,128)(2,1)}, bf16[1,8,2048]{2,1,0:T(8,128)(2,1)}) fusion(pred[]{:T(512)S(6)} %eq.3, bf16[8,2048]{1,0:T(8,128)(2,1)S(1)} %collective-permute-done.10, bf16[16,2048]{1,0:T(8,128)(2,1)S(1)} %add_convert_fusion.1), kind=kLoop, calls=%fused_computation.7 | loop fusion | flops 114688 | bytes 163841 | tf_op jit(solution)/shard_map/broadcast_in_dim | solution.py:431
  (7 shorter events, 0.1 us)
Async XLA Ops:
  2.2 9.4 %collective-permute-start.1 = (bf16[16,2432]{1,0:T(8,128)(2,1)S(1)}, bf16[16,2432]{1,0:T(8,128)(2,1)S(1)}, u32[]{:S(2)}, u32[]{:S(2)}) collective-permute-start(bf16[16,2432]{1,0:T(8,128)(2,1)S(1)} %get-tuple-element.13), channel_id=1, source_target_pairs={{0,16},{1,17},{2,18},{3,19},{4,20},{5,21},{6,22},{7,23},{8,24},{9,... | collective-permute-start | bytes 233480 | tf_op jit(solution)/shard_map/ppermute | solution.py:181
  5.2 6.6 %collective-permute-start = (bf16[16,2432]{1,0:T(8,128)(2,1)S(1)}, bf16[16,2432]{1,0:T(8,128)(2,1)S(1)}, u32[]{:S(2)}, u32[]{:S(2)}) collective-permute-start(bf16[16,2432]{1,0:T(8,128)(2,1)S(1)} %get-tuple-element.13), channel_id=1, source_target_pairs={{0,8},{1,9},{2,10},{3,11},{4,12},{5,13},{6,14},{7,15},{8,0},{9,1},... | collective-permute-start | bytes 233480 | tf_op jit(solution)/shard_map/ppermute | solution.py:181
  11.8 6.3 %collective-permute-start.4 = (bf16[24,2176]{1,0:T(8,128)(2,1)S(1)}, bf16[24,2176]{1,0:T(8,128)(2,1)S(1)}, u32[]{:S(2)}, u32[]{:S(2)}) collective-permute-start(bf16[24,2176]{1,0:T(8,128)(2,1)S(1)} %pad_maximum_fusion.1), channel_id=1, source_target_pairs={{0,6},{1,7},{2,4},{3,5},{4,2},{5,3},{6,0},{7,1},{8,14},{9,15},{10,... | collective-permute-start | bytes 313352 | tf_op jit(solution)/shard_map/ppermute | solution.py:181
  14.3 4.9 %collective-permute-start.3 = (bf16[24,2176]{1,0:T(8,128)(2,1)S(1)}, bf16[24,2176]{1,0:T(8,128)(2,1)S(1)}, u32[]{:S(2)}, u32[]{:S(2)}) collective-permute-start(bf16[24,2176]{1,0:T(8,128)(2,1)S(1)} %pad_maximum_fusion.1), channel_id=1, source_target_pairs={{0,4},{1,5},{2,6},{3,7},{4,0},{5,1},{6,2},{7,3},{8,12},{9,13},{10,... | collective-permute-start | bytes 313352 | tf_op jit(solution)/shard_map/ppermute | solution.py:181
  14.9 4.7 %collective-permute-start.2 = (bf16[24,2176]{1,0:T(8,128)(2,1)S(1)}, bf16[24,2176]{1,0:T(8,128)(2,1)S(1)}, u32[]{:S(2)}, u32[]{:S(2)}) collective-permute-start(bf16[24,2176]{1,0:T(8,128)(2,1)S(1)} %pad_maximum_fusion.1), channel_id=1, source_target_pairs={{0,2},{1,3},{2,0},{3,1},{4,6},{5,7},{6,4},{7,5},{8,10},{9,11},{10,... | collective-permute-start | bytes 313352 | tf_op jit(solution)/shard_map/ppermute | solution.py:181
  19.6 1.8 %collective-permute-start.5 = (bf16[96,2176]{1,0:T(8,128)(2,1)S(1)}, bf16[96,2176]{1,0:T(8,128)(2,1)S(1)}, u32[]{:S(2)}, u32[]{:S(2)}) collective-permute-start(bf16[96,2176]{1,0:T(8,128)(2,1)S(1)} %pad_maximum_fusion.near_ref), channel_id=1, source_target_pairs={{0,1},{1,0},{2,3},{3,2},{4,5},{5,4},{6,7},{7,6},{8,9},{9,8},{10,11... | collective-permute-start | bytes 1253384 | tf_op jit(solution)/shard_map/ppermute | solution.py:181
  27.1 1.6 %collective-permute-start.6 = (bf16[64,2048]{1,0:T(8,128)(2,1)S(1)}, bf16[64,2048]{1,0:T(8,128)(2,1)S(1)}, u32[]{:S(2)}, u32[]{:S(2)}) collective-permute-start(bf16[64,2048]{1,0:T(8,128)(2,1)S(1)} %get-tuple-element.23), channel_id=1, source_target_pairs={{0,1},{1,0},{2,3},{3,2},{4,5},{5,4},{6,7},{7,6},{8,9},{9,8},{10,11... | collective-permute-start | bytes 786440 | tf_op jit(solution)/shard_map/ppermute | solution.py:181
  28.8 4.3 %collective-permute-start.7 = (bf16[16,2048]{1,0:T(8,128)(2,1)S(1)}, bf16[16,2048]{1,0:T(8,128)(2,1)S(1)}, u32[]{:S(2)}, u32[]{:S(2)}) collective-permute-start(bf16[16,2048]{1,0:T(8,128)(2,1)S(1)} %get-tuple-element.24), channel_id=1, source_target_pairs={{0,2},{1,3},{2,0},{3,1},{4,6},{5,7},{6,4},{7,5},{8,10},{9,11},{10,... | collective-permute-start | bytes 196616 | tf_op jit(solution)/shard_map/ppermute | solution.py:181
  29.9 5.8 %collective-permute-start.9 = (bf16[16,2048]{1,0:T(8,128)(2,1)S(1)}, bf16[16,2048]{1,0:T(8,128)(2,1)S(1)}, u32[]{:S(2)}, u32[]{:S(2)}) collective-permute-start(bf16[16,2048]{1,0:T(8,128)(2,1)S(1)} %get-tuple-element.25), channel_id=1, source_target_pairs={{0,6},{1,7},{2,4},{3,5},{4,2},{5,3},{6,0},{7,1},{8,14},{9,15},{10,... | collective-permute-start | bytes 196616 | tf_op jit(solution)/shard_map/ppermute | solution.py:181
  31.8 4.3 %collective-permute-start.8 = (bf16[16,2048]{1,0:T(8,128)(2,1)S(1)}, bf16[16,2048]{1,0:T(8,128)(2,1)S(1)}, u32[]{:S(2)}, u32[]{:S(2)}) collective-permute-start(bf16[16,2048]{1,0:T(8,128)(2,1)S(1)} %get-tuple-element.26), channel_id=1, source_target_pairs={{0,4},{1,5},{2,6},{3,7},{4,0},{5,1},{6,2},{7,3},{8,12},{9,13},{10,... | collective-permute-start | bytes 196616 | tf_op jit(solution)/shard_map/ppermute | solution.py:181
  36.1 5.8 %collective-permute-start.10 = (bf16[8,2048]{1,0:T(8,128)(2,1)S(1)}, bf16[8,2048]{1,0:T(8,128)(2,1)S(1)}, u32[]{:S(2)}, u32[]{:S(2)}) collective-permute-start(bf16[8,2048]{1,0:T(8,128)(2,1)S(1)} %broadcast_select_fusion), channel_id=1, source_target_pairs={{0,24},{1,25},{2,26},{3,27},{4,28},{5,29},{6,30},{7,31},{8,16},{9,... | collective-permute-start | bytes 98312 | tf_op jit(solution)/shard_map/ppermute | solution.py:181

commit v3 on v0

--- a/solution.py
+++ b/solution.py
@@ -1,6 +1,9 @@
+import functools
 import jax
 import jax.numpy as jnp
 from jax import lax
+from jax.experimental import pallas as pl
+from jax.experimental.pallas import tpu as pltpu
 from jax.sharding import PartitionSpec as P
 
 EPSILON = 1e-06
@@ -90,7 +93,7 @@
     return placed.reshape(expert_count, capacity, rows_in.shape[1])
 
 
-def per_device(
+def routed_plan(
     fwd_act, fwd_routes, bwd_saved, bwd_grad, bwd_routes, norm_gain, router, w_gate, w_up, w_down
 ):
     tok_count = fwd_act.shape[1]
@@ -168,6 +171,404 @@
     return (fwd_next, grad_prev)
 
 
+AXES = ("section", "expert")
+SQUARE = 8
+CORE, HALF, SECTION = 1, 8, 16
+LANES = 128
+TOP_COUNT = 8
+VMEM = pl.BlockSpec(memory_space=pltpu.VMEM)
+SMEM = pl.BlockSpec(memory_space=pltpu.SMEM)
+HBM = pl.BlockSpec(memory_space=pltpu.HBM)
+MIB = 1024 * 1024
+
+
+def swapped(block, distance):
+    count = lax.axis_size(AXES)
+    return lax.ppermute(block, AXES, [(i, i ^ distance) for i in range(count)])
+
+
+def in_hbm(array):
+    return pltpu.with_memory_space_constraint(array, pltpu.HBM)
+
+
+def root_factor(values):
+    return lax.rsqrt(jnp.mean(values * values, axis=-1, keepdims=True) + EPSILON)
+
+
+def in_first_section():
+    return lax.axis_index("section") == 0
+
+
+def pack_kernel(
+    fwd_act, fwd_routes, bwd_saved, bwd_grad, bwd_routes, gain, router,
+    along_ref, acts_ref, gain_ref, router_ref, grads_ref, routes_ref, sems,
+):
+    first_section = in_first_section()
+    grad_copy = pltpu.make_async_copy(bwd_grad.at[0], grads_ref, sems.at[0])
+    gain_copy = pltpu.make_async_copy(gain, gain_ref, sems.at[1])
+    router_copy = pltpu.make_async_copy(router, router_ref, sems.at[4])
+
+    @pl.when(first_section)
+    def _():
+        pltpu.make_async_copy(fwd_act.at[0], acts_ref, sems.at[2]).start()
+        pltpu.make_async_copy(fwd_routes.at[0], routes_ref, sems.at[3]).start()
+
+    @pl.when(jnp.logical_not(first_section))
+    def _():
+        pltpu.make_async_copy(bwd_saved.at[0], acts_ref, sems.at[2]).start()
+        pltpu.make_async_copy(bwd_routes.at[0], routes_ref, sems.at[3]).start()
+
+    gain_copy.start()
+    grad_copy.start()
+    router_copy.start()
+    pltpu.make_async_copy(fwd_act.at[0], acts_ref, sems.at[2]).wait()
+    gain_copy.wait()
+    acts = acts_ref[...].astype(jnp.float32)
+    normed = acts * root_factor(acts) * gain_ref[...]
+    pltpu.make_async_copy(fwd_routes.at[0], routes_ref, sems.at[3]).wait()
+    grad_copy.wait()
+    routes = routes_ref[...].astype(jnp.float32)
+    routes = jnp.concatenate([routes, jnp.zeros((8, LANES - TOP_COUNT), jnp.float32)], axis=1)
+    blank = jnp.zeros((8, LANES), jnp.float32)
+    grads = grads_ref[...].astype(jnp.float32)
+    along_ref[...] = jnp.concatenate(
+        [jnp.concatenate([normed, routes], axis=1), jnp.concatenate([grads, blank], axis=1)],
+        axis=0,
+    ).astype(jnp.bfloat16)
+    router_copy.wait()
+
+
+def pack_rows(*arrays):
+    fwd_act, fwd_routes, _, _, _, gain, router = arrays
+    count, width = fwd_act.shape[1:]
+    return pl.pallas_call(
+        pack_kernel,
+        out_shape=[
+            jax.ShapeDtypeStruct((2 * count, width + LANES), jnp.bfloat16),
+            jax.ShapeDtypeStruct((count, width), jnp.bfloat16),
+            jax.ShapeDtypeStruct(gain.shape, gain.dtype),
+            jax.ShapeDtypeStruct(router.shape, router.dtype),
+        ],
+        in_specs=[HBM] * 7,
+        out_specs=[VMEM] * 4,
+        scratch_shapes=[
+            pltpu.VMEM((count, width), jnp.bfloat16),
+            pltpu.VMEM(fwd_routes.shape[1:], jnp.int32),
+            pltpu.SemaphoreType.DMA((5,)),
+        ],
+        compiler_params=pltpu.CompilerParams(vmem_limit_bytes=4 * MIB),
+        name="pack",
+    )(*[in_hbm(x) for x in arrays])
+
+
+def widen_kernel(along_ref, acts_ref, gain_ref, across_ref):
+    rows = along_ref[...].astype(jnp.float32)
+    acts = acts_ref[...].astype(jnp.float32)
+    gain_row = gain_ref[...]
+    width = gain_row.shape[1]
+    gain_rows = jnp.concatenate(
+        [gain_row[:, LANES * k : LANES * k + LANES] for k in range(16)], axis=0
+    )
+    gain_high = gain_rows.astype(jnp.bfloat16).astype(jnp.float32)
+    gain_low = gain_rows - gain_high
+    blank = jnp.zeros((8, LANES), jnp.float32)
+    across_ref[...] = jnp.concatenate(
+        [
+            jnp.concatenate([rows[0:8], gain_low[:8]], axis=1),
+            jnp.concatenate([rows[8:16, :width], gain_high[:8], gain_low[8:]], axis=1),
+            jnp.concatenate([acts, gain_high[8:], blank], axis=1),
+        ],
+        axis=0,
+    ).astype(jnp.bfloat16)
+
+
+def in_vmem(body, name, out_shape, *arrays):
+    return pl.pallas_call(
+        body,
+        out_shape=out_shape,
+        in_specs=[VMEM] * len(arrays),
+        out_specs=[VMEM] * len(out_shape),
+        compiler_params=pltpu.CompilerParams(vmem_limit_bytes=4 * MIB),
+        name=name,
+    )(*arrays)
+
+
+def merge_kernel(along_ref, across_ref, mine_ref):
+    first_section = in_first_section()
+    used = mine_ref.shape[1]
+    along = along_ref[...].astype(jnp.float32)
+    across = across_ref[...].astype(jnp.float32)[:, :used]
+    mine_ref[...] = jnp.concatenate(
+        [
+            jnp.where(first_section, along[:8], across[:8]),
+            jnp.where(first_section, across[:16], along),
+        ],
+        axis=0,
+    ).astype(jnp.bfloat16)
+
+
+def leave_kernel(a_ref, b_ref, c_ref, d_ref, leaving_ref, staying_ref):
+    first_section = in_first_section()
+    total = a_ref[...].astype(jnp.float32) + b_ref[...].astype(jnp.float32)
+    total = total + c_ref[...].astype(jnp.float32) + d_ref[...].astype(jnp.float32)
+    leaving_ref[...] = jnp.where(first_section, total[:8], total[8:]).astype(jnp.bfloat16)
+    staying_ref[...] = jnp.where(first_section, total[8:], total[:8])
+
+
+def finish_kernel(
+    staying_ref, other_ref, scale_ref, towards_ref, back_ref, rest_ref, fwd_hbm, grad_hbm,
+    result_ref, nothing_ref, sems,
+):
+    first_section = in_first_section()
+    nothing_ref[...] = jnp.zeros_like(nothing_ref)
+
+    @pl.when(first_section)
+    def _():
+        pltpu.make_async_copy(nothing_ref, fwd_hbm.at[0], sems.at[0]).start()
+
+    @pl.when(jnp.logical_not(first_section))
+    def _():
+        pltpu.make_async_copy(nothing_ref, grad_hbm.at[0], sems.at[0]).start()
+
+    sums = staying_ref[...] + other_ref[...].astype(jnp.float32)
+    mean = jnp.mean(sums * towards_ref[...], axis=-1, keepdims=True)
+    result = sums * scale_ref[...] + rest_ref[...] - back_ref[...] * mean
+    result_ref[...] = result.astype(jnp.bfloat16)
+
+    @pl.when(first_section)
+    def _():
+        pltpu.make_async_copy(result_ref, grad_hbm.at[0], sems.at[1]).start()
+
+    @pl.when(jnp.logical_not(first_section))
+    def _():
+        pltpu.make_async_copy(result_ref, fwd_hbm.at[0], sems.at[1]).start()
+
+    pltpu.make_async_copy(nothing_ref, fwd_hbm.at[0], sems.at[0]).wait()
+    pltpu.make_async_copy(result_ref, grad_hbm.at[0], sems.at[1]).wait()
+
+
+def finish(*arrays):
+    count, width = arrays[0].shape
+    return pl.pallas_call(
+        finish_kernel,
+        out_shape=[jax.ShapeDtypeStruct((1, count, width), jnp.bfloat16)] * 2,
+        in_specs=[VMEM] * len(arrays),
+        out_specs=[HBM] * 2,
+        scratch_shapes=[
+            pltpu.VMEM((count, width), jnp.bfloat16),
+            pltpu.VMEM((count, width), jnp.bfloat16),
+            pltpu.SemaphoreType.DMA((2,)),
+        ],
+        compiler_params=pltpu.CompilerParams(vmem_limit_bytes=4 * MIB),
+        name="finish",
+    )(*arrays)
+
+
+def fetch_kernel(*refs, parts):
+    count = len(parts)
+    weights, held_refs, turned_refs = refs[:count], refs[count : 2 * count], refs[2 * count : 3 * count]
+    sems = refs[-1]
+    step = 256
+    waiting = []
+    for (first, rows), source, held, turned in zip(parts, weights, held_refs, turned_refs):
+        for k in range(rows // step):
+            copy = pltpu.make_async_copy(
+                source.at[pl.ds(first + k * step, step)],
+                held.at[pl.ds(k * step, step)],
+                sems.at[len(waiting)],
+            )
+            copy.start()
+            waiting.append((copy, held, turned, k * step))
+    for copy, held, turned, start in waiting:
+        copy.wait()
+        turned[:, start : start + step] = held[start : start + step, :].T
+
+
+def fetched(*parts):
+    weights = [w for w, _, _ in parts]
+    sizes = tuple((first, rows) for _, first, rows in parts)
+    moved = sum(rows * w.shape[1] for w, _, rows in parts)
+    held = [jax.ShapeDtypeStruct((rows, w.shape[1]), w.dtype) for w, _, rows in parts]
+    turned = [jax.ShapeDtypeStruct((w.shape[1], rows), w.dtype) for w, _, rows in parts]
+    outs = pl.pallas_call(
+        functools.partial(fetch_kernel, parts=sizes),
+        out_shape=held + turned,
+        in_specs=[HBM] * len(parts),
+        out_specs=[VMEM] * (2 * len(parts)),
+        scratch_shapes=[pltpu.SemaphoreType.DMA((sum(rows for _, rows in sizes) // 256,))],
+        compiler_params=pltpu.CompilerParams(vmem_limit_bytes=8 * MIB),
+        cost_estimate=pl.CostEstimate(flops=0, bytes_accessed=4 * moved, transcendentals=0),
+        name="fetch",
+    )(*[in_hbm(w) for w in weights])
+    return tuple(zip(outs[: len(parts)], outs[len(parts) :]))
+
+
+def expert_kernel(
+    near_ref, far_ref, router_ref, gate_ref, gate_turned_ref,
+    up_ref, up_turned_ref, up_rest_ref, up_rest_turned_ref, down_ref, down_turned_ref,
+    kept_ref, sent_ref,
+):
+    width, hidden_count = gate_ref.shape
+    step = 256
+    split = up_ref.shape[0]
+    own_expert = lax.axis_index("expert")
+
+    pairs = near_ref.shape[0] * 2 // 3
+    tops = jnp.concatenate([near_ref[:pairs], far_ref[:pairs]], axis=0)
+    grads = jnp.concatenate([near_ref[pairs:, :width], far_ref[pairs:, :width]], axis=0)
+    routes = tops[:, width:].astype(jnp.float32)
+    normed = tops[:, :width]
+
+    def forward(rows):
+        return jnp.concatenate([rows[16 * k : 16 * k + 8] for k in range(SQUARE)], axis=0)
+
+    def backward(rows):
+        return jnp.concatenate([rows[16 * k + 8 : 16 * k + 16] for k in range(SQUARE)], axis=0)
+
+    router = router_ref[...]
+    contract = (((1,), (1,)), ((), ()))
+    logits = lax.dot_general(normed, router, contract, preferred_element_type=jnp.float32)
+    labels = lax.broadcasted_iota(jnp.int32, logits.shape, 1)
+    labels_real = labels.astype(jnp.float32)
+    chosen = routes[:, 0:1] == labels_real
+    for k in range(1, TOP_COUNT):
+        chosen = jnp.logical_or(chosen, routes[:, k : k + 1] == labels_real)
+    raised = jnp.where(chosen, jnp.exp(logits), 0.0)
+    gates = raised / jnp.sum(raised, axis=-1, keepdims=True)
+    own = jnp.where(labels == own_expert, 1.0, 0.0)
+    gate_own = jnp.sum(own * gates, axis=-1, keepdims=True)
+    gate_f, gate_b = forward(gate_own), backward(gate_own)
+
+    hiddens, d_pres, d_ups = [], [], []
+    dgate = 0.0
+    for piece in range(hidden_count // step):
+        cols = slice(piece * step, piece * step + step)
+        pre_gate = jnp.dot(normed, gate_ref[:, cols], preferred_element_type=jnp.float32)
+        pre_up = jnp.dot(normed[:, :split], up_ref[:, cols], preferred_element_type=jnp.float32)
+        pre_up = pre_up + jnp.dot(
+            normed[:, split:], up_rest_ref[:, cols], preferred_element_type=jnp.float32
+        )
+        d_hidden = jnp.dot(grads, down_turned_ref[:, cols], preferred_element_type=jnp.float32)
+        sigma = jax.nn.sigmoid(pre_gate)
+        silu_val = pre_gate * sigma
+        hidden = silu_val * pre_up
+        hiddens.append((forward(hidden) * gate_f).astype(jnp.bfloat16))
+        dgate = dgate + jnp.sum(backward(hidden) * d_hidden, axis=-1, keepdims=True)
+        d_hidden = d_hidden * gate_b
+        d_ups.append((d_hidden * backward(silu_val)).astype(jnp.bfloat16))
+        sigma_b = backward(sigma)
+        slope = sigma_b * (1.0 + backward(pre_gate) * (1.0 - sigma_b))
+        d_pres.append((d_hidden * backward(pre_up) * slope).astype(jnp.bfloat16))
+
+    hidden = jnp.concatenate(hiddens, axis=1)
+    d_pre = jnp.concatenate(d_pres, axis=1)
+    d_up = jnp.concatenate(d_ups, axis=1)
+    out_f = jnp.dot(hidden, down_ref[...], preferred_element_type=jnp.float32)
+    d_normed = jnp.concatenate(
+        [
+            jnp.dot(d_up, mat[...], preferred_element_type=jnp.float32)
+            for mat in (up_turned_ref, up_rest_turned_ref)
+        ],
+        axis=1,
+    )
+    d_normed = d_normed + jnp.dot(d_pre, gate_turned_ref[...], preferred_element_type=jnp.float32)
+    spread = gate_b * dgate * (backward(own) - backward(gates))
+    spread_high = spread.astype(jnp.bfloat16)
+    spread_low = (spread - spread_high.astype(jnp.float32)).astype(jnp.bfloat16)
+    d_normed = d_normed + jnp.dot(spread_high, router, preferred_element_type=jnp.float32)
+    d_normed = d_normed + jnp.dot(spread_low, router, preferred_element_type=jnp.float32)
+
+    parts = []
+    for k in range(SQUARE):
+        parts.append(out_f[8 * k : 8 * k + 8])
+        parts.append(d_normed[8 * k : 8 * k + 8])
+    kept_ref[...] = jnp.concatenate(parts[:SQUARE], axis=0).astype(jnp.bfloat16)
+    sent_ref[...] = jnp.concatenate(parts[SQUARE:], axis=0).astype(jnp.bfloat16)
+
+
+def run_experts(near, far, router, *weights):
+    width = router.shape[1]
+    rows = SQUARE // 2 * 16
+    return pl.pallas_call(
+        expert_kernel,
+        out_shape=[jax.ShapeDtypeStruct((rows, width), jnp.bfloat16)] * 2,
+        in_specs=[VMEM] * (3 + len(weights)),
+        out_specs=[VMEM] * 2,
+        compiler_params=pltpu.CompilerParams(vmem_limit_bytes=24 * MIB),
+        name="experts",
+    )(near, far, router, *weights)
+
+
+def ending_kernel(across_ref, scale_ref, along_ref, back_ref, rest_ref):
+    first_section = in_first_section()
+    packed = across_ref[...].astype(jnp.float32)
+    width = scale_ref.shape[1]
+    grads = packed[8:16, :width]
+    acts = packed[16:24, :width]
+    gain_rows = packed[8:24, width : width + LANES] + packed[0:16, width + LANES :]
+    gain_row = jnp.concatenate([gain_rows[k : k + 1] for k in range(16)], axis=1)
+    factor = root_factor(acts)
+    unit = acts * factor
+    scale_ref[...] = jnp.where(first_section, factor * gain_row, 1.0)
+    along_ref[...] = jnp.where(first_section, unit * gain_row, 0.0)
+    back_ref[...] = jnp.where(first_section, unit * factor, 0.0)
+    rest_ref[...] = jnp.where(first_section, grads, acts)
+
+
+def added(*blocks):
+    return sum(block.astype(jnp.float32) for block in blocks).astype(jnp.bfloat16)
+
+
+def paired_plan(
+    fwd_act, fwd_routes, bwd_saved, bwd_grad, bwd_routes, norm_gain, router, w_gate, w_up, w_down
+):
+    count, width = fwd_act.shape[1:]
+    used = width + LANES
+    along, acts, gain_row, router_rows = pack_rows(
+        fwd_act, fwd_routes, bwd_saved, bwd_grad, bwd_routes, norm_gain, router.T
+    )
+    wide = jax.ShapeDtypeStruct((3 * count, used + LANES), jnp.bfloat16)
+    across = in_vmem(widen_kernel, "widen", [wide], along, acts, gain_row)[0]
+    across = swapped(across, SECTION)
+    along = swapped(along, HALF)
+    upper = width // 2
+    gate_mats, up_mats = fetched((w_gate[0], 0, width), (w_up[0], 0, upper))
+    along, gate_mats, up_mats = lax.optimization_barrier((along, gate_mats, up_mats))
+    rows = jax.ShapeDtypeStruct((3 * count, used), jnp.bfloat16)
+    mine = in_vmem(merge_kernel, "merge", [rows], along, across)[0]
+    down_hbm, up_hbm, _ = lax.optimization_barrier((w_down[0], w_up[0], mine))
+    rest_mats, down_mats = fetched((up_hbm, upper, width - upper), (down_hbm, 0, down_hbm.shape[0]))
+    real = jax.ShapeDtypeStruct((count, width), jnp.float32)
+    ending = in_vmem(ending_kernel, "endings", [real] * 4, across)
+    blocks = [mine] + [swapped(mine, k) for k in (2, 4, 6)]
+    near = jnp.concatenate([b[:16] for b in blocks] + [b[16:] for b in blocks], axis=0)
+    near, rest_mats, down_mats, ending = lax.optimization_barrier(
+        (near, rest_mats, down_mats, ending)
+    )
+    far = swapped(near, CORE)
+
+    kept, sent = run_experts(
+        near, far, router_rows, *gate_mats, *up_mats, *rest_mats, *down_mats
+    )
+
+    chip = added(kept, swapped(sent, CORE))
+    pieces = [chip[0:16]] + [swapped(chip[8 * k : 8 * k + 16], k) for k in (2, 4, 6)]
+    small = jax.ShapeDtypeStruct((count, width), jnp.bfloat16)
+    leaving, staying = in_vmem(leave_kernel, "leave", [small, real], *pieces)
+    other = swapped(leaving, SECTION + HALF)
+    return tuple(finish(staying, other, *ending))
+
+
+def per_device(fwd_act, fwd_routes, *rest):
+    sections, devices = lax.axis_size("section"), lax.axis_size("expert")
+    tokens, top_count = fwd_routes.shape[1:]
+    router = rest[4]
+    paired = sections == 2 and devices == 2 * SQUARE and router.shape == (16 * LANES, devices)
+    paired = paired and tokens == 8 and top_count == TOP_COUNT
+    plan = paired_plan if paired else routed_plan
+    return plan(fwd_act, fwd_routes, *rest)
+
+
 def solution(mesh):
     in_specs = (
         P("section", "expert", None),

time: 124 us -> 38.4 us (0.31); the launches traced: 122 us -> 38.3 us
  matrix products: 28.1 us -> 0 us
  waiting for transfers between devices: 35 us -> 11.4 us
  starting transfers between devices: 33.1 us -> 15.1 us
  local copies, waits for them, and re-layouts: 12.6 us -> 0.11 us
  other arithmetic: 12.4 us -> 0.07 us
  Pallas kernels: 0 us -> 10.8 us
    all_to_all x6 -> x0, waiting for transfers between devices: 33.4 us -> none  [the longest x1 9.23 us: per_device(): lax.all_to_all(result.reshape(sources, slots, model_width), 'expert', spl...]
    all_to_all x6 -> x0, starting transfers between devices: 28.5 us -> none  [the longest x1 7.44 us: per_device(): lax.all_to_all(send_x, 'expert', split_axis=0, concat_axis=0, tiled=True)]
    dot_general x14 -> x0, matrix products: 28.1 us -> none  [the longest x3 4.24 us: dispatch(): jnp.dot(spread, rows_in, preferred_element_type=jnp.float32)]
    pallas_call x0 -> x9, Pallas kernels: none -> 10.8 us  [the longest x2 5.82 us: fetched(): pl.pallas_call(functools.partial(fetch_kernel, parts=sizes), out_shape=he...]
    ppermute x2 -> x11, starting transfers between devices: 4.69 us -> 15.1 us  [swapped(): return lax.ppermute(block, AXES, [(i, i ^ distance) for i in range(count)])]
    ppermute x2 -> x11, waiting for transfers between devices: 1.57 us -> 11.4 us  [swapped(): return lax.ppermute(block, AXES, [(i, i ^ distance) for i in range(count)])]
    gather x10 -> x0, local copies, waits for them, and re-layouts: 7.22 us -> none  [the longest x1 2.22 us: per_device(): jnp.take(back_rows.reshape(expert_count * capacity, model_width), target_...]
    reduce_sum x12 -> x0, other arithmetic: 4.81 us -> none  [the longest x2 1.03 us: normalize(): jnp.mean(values * values, axis=-1, keepdims=True) + EPSILON]
  transfers between devices with their start and end apart: 8 -> 11, of which waited for: 7 -> 7; matrix products, arithmetic and copies ran while one was open for 38% -> 0% of each run, Pallas kernels for 0% -> 15%
where the time goes in v3:
time: 38.4 us; the launch traced here: 38.3 us
  starting transfers between devices  15.1 us (39%)
  waiting for transfers between devices  11.4 us (30%)
  Pallas kernels  10.8 us (28%)
  between operations  0.76 us (2%)
    ppermute x11, starting transfers between devices, swapped(): return lax.ppermute(block, AXES, [(i, i ^ distance) for i in range(count)])  15.1 us
    ppermute x11, waiting for transfers between devices, swapped(): return lax.ppermute(block, AXES, [(i, i ^ distance) for i in range(count)])  11.4 us
    pallas_call x2, Pallas kernels, fetched(): pl.pallas_call(functools.partial(fetch_kernel, parts=sizes), out_shape=he...  5.82 us
    pallas_call x1, Pallas kernels, run_experts(): pl.pallas_call(expert_kernel, out_shape=[jax.ShapeDtypeStruct((rows, widt...  3.08 us
    pallas_call x1, Pallas kernels, pack_rows(): pl.pallas_call(pack_kernel, out_shape=[jax.ShapeDtypeStruct((2 * count, w...  0.97 us
  transfers between devices with their start and end apart: 11, of which 7 were waited for; matrix products, arithmetic and copies ran while one was open for 0% of the time, Pallas kernels for 15%

profile of v3, /device:TPU:0, one launch (start us, length us, event | category | flops | bytes accessed | tf_op | source)
XLA Modules:
  0.0 38.3 jit_solution(13788689788345085870)
XLA Ops:
  0.6 1.0 %pack.1 = (bf16[16,2176]{1,0:T(8,128)(2,1)S(1)}, bf16[8,2048]{1,0:T(8,128)(2,1)S(1)}, f32[1,2048]{1,0:T(1,128)S(1)}, bf16[16,2048]{1,0:T(8,128)(2,1)S(1)}) custom-call(bf16[1,8,2048]{2,1,0:T(8,128)(2,1)} %fwd_act.1, s32[1,8,8]{2,1,0:T(8,128)} %fwd_routes.1, bf16[1,8,2048]{2,1,0:T(8,128)(2,1)} %bwd_saved.1, bf16[1,8,2048]{2,1,0:T(8,128)(2,1)} %bwd_grad.1, ...), custom_call_target="tpu_custom_call" | custom-call | tf_op jit(solution)/shard_map/pack/pallas_call | solution.py:244
  1.6 3.0 %collective-permute-start.1 = (bf16[24,2304]{1,0:T(8,128)(2,1)S(1)}, bf16[24,2304]{1,0:T(8,128)(2,1)S(1)}, u32[]{:S(2)}, u32[]{:S(2)}) collective-permute-start(bf16[24,2304]{1,0:T(8,128)(2,1)S(1)} %widen.1), channel_id=1, source_target_pairs={{0,16},{1,17},{2,18},{3,19},{4,20},{5,21},{6,22},{7,23},{8,24},{9,... | collective-permute-start | bytes 331784 | tf_op jit(solution)/shard_map/ppermute | solution.py:187
  4.6 2.6 %collective-permute-start = (bf16[16,2176]{1,0:T(8,128)(2,1)S(1)}, bf16[16,2176]{1,0:T(8,128)(2,1)S(1)}, u32[]{:S(2)}, u32[]{:S(2)}) collective-permute-start(bf16[16,2176]{1,0:T(8,128)(2,1)S(1)} %get-tuple-element.38.along_ref), channel_id=1, source_target_pairs={{0,8},{1,9},{2,10},{3,11},{4,12},{5,13},{6,14},{7,15},{8,0},{9,1},... | collective-permute-start | bytes 208904 | tf_op jit(solution)/shard_map/ppermute | solution.py:187
  7.2 3.1 %fetch.2 = (bf16[2048,768]{1,0:T(8,128)(2,1)S(1)}, bf16[1024,768]{1,0:T(8,128)(2,1)S(1)}, bf16[768,2048]{1,0:T(8,128)(2,1)S(1)}, bf16[768,1024]{1,0:T(8,128)(2,1)S(1)}) custom-call(bf16[2048,768]{1,0:T(8,128)(2,1)} %bitcast.6, bf16[2048,768]{1,0:T(8,128)(2,1)} %bitcast.4), custom_call_target="tpu_custom_call" | custom-call | bytes 9437184 | tf_op jit(solution)/shard_map/fetch/pallas_call | solution.py:393
  10.3 0.0 collective-permute-done.along_ref
  10.3 0.0 collective-permute-done.1.across_ref
  10.4 2.6 %collective-permute-start.4 = (bf16[24,2176]{1,0:T(8,128)(2,1)S(1)}, bf16[24,2176]{1,0:T(8,128)(2,1)S(1)}, u32[]{:S(2)}, u32[]{:S(2)}) collective-permute-start(bf16[24,2176]{1,0:T(8,128)(2,1)S(1)} %merge.1), channel_id=1, source_target_pairs={{0,6},{1,7},{2,4},{3,5},{4,2},{5,3},{6,0},{7,1},{8,14},{9,15},{10,... | collective-permute-start | bytes 313352 | tf_op jit(solution)/shard_map/ppermute | solution.py:187
  13.0 0.4 %collective-permute-start.3 = (bf16[24,2176]{1,0:T(8,128)(2,1)S(1)}, bf16[24,2176]{1,0:T(8,128)(2,1)S(1)}, u32[]{:S(2)}, u32[]{:S(2)}) collective-permute-start(bf16[24,2176]{1,0:T(8,128)(2,1)S(1)} %merge.1), channel_id=1, source_target_pairs={{0,4},{1,5},{2,6},{3,7},{4,0},{5,1},{6,2},{7,3},{8,12},{9,13},{10,... | collective-permute-start | bytes 313352 | tf_op jit(solution)/shard_map/ppermute | solution.py:187
  13.4 0.5 %collective-permute-start.2 = (bf16[24,2176]{1,0:T(8,128)(2,1)S(1)}, bf16[24,2176]{1,0:T(8,128)(2,1)S(1)}, u32[]{:S(2)}, u32[]{:S(2)}) collective-permute-start(bf16[24,2176]{1,0:T(8,128)(2,1)S(1)} %merge.1), channel_id=1, source_target_pairs={{0,2},{1,3},{2,0},{3,1},{4,6},{5,7},{6,4},{7,5},{8,10},{9,11},{10,... | collective-permute-start | bytes 313352 | tf_op jit(solution)/shard_map/ppermute | solution.py:187
  13.9 2.7 %fetch.3 = (bf16[1024,768]{1,0:T(8,128)(2,1)S(1)}, bf16[768,2048]{1,0:T(8,128)(2,1)S(1)}, bf16[768,1024]{1,0:T(8,128)(2,1)S(1)}, bf16[2048,768]{1,0:T(8,128)(2,1)S(1)}) custom-call(bf16[2048,768]{1,0:T(8,128)(2,1)} %bitcast.5, bf16[768,2048]{1,0:T(8,128)(2,1)} %bitcast.7), custom_call_target="tpu_custom_call" | custom-call | bytes 9437184 | tf_op jit(solution)/shard_map/fetch/pallas_call | solution.py:393
  16.7 0.1 endings.1
  16.8 1.3 %collective-permute-done.2 = bf16[24,2176]{1,0:T(8,128)(2,1)S(1)} collective-permute-done((bf16[24,2176]{1,0:T(8,128)(2,1)S(1)}, bf16[24,2176]{1,0:T(8,128)(2,1)S(1)}, u32[]{:S(2)}, u32[]{:S(2)}) %collective-permute-start.2) | collective-permute-done | bytes 104480 | tf_op jit(solution)/shard_map/ppermute | solution.py:187
  18.1 0.0 collective-permute-done.3
  18.1 0.0 collective-permute-done.4
  18.2 0.1 collective-permute-start.5
  18.3 1.7 %collective-permute-done.5.far_ref = bf16[96,2176]{1,0:T(8,128)(2,1)S(1)} collective-permute-done((bf16[96,2176]{1,0:T(8,128)(2,1)S(1)}, bf16[96,2176]{1,0:T(8,128)(2,1)S(1)}, u32[]{:S(2)}, u32[]{:S(2)}) %collective-permute-start.5) | collective-permute-done | bytes 417824 | tf_op jit(solution)/shard_map/ppermute | solution.py:187
  20.0 3.1 %experts.1 = (bf16[64,2048]{1,0:T(8,128)(2,1)S(1)}, bf16[64,2048]{1,0:T(8,128)(2,1)S(1)}) custom-call(bf16[96,2176]{1,0:T(8,128)(2,1)S(1)} %slice_dynamic-update-slice_fusion.4.near_ref, bf16[96,2176]{1,0:T(8,128)(2,1)S(1)} %collective-permute-done.5.far_ref, bf16[16,2048]{1,0:T(8,128)(2,1)S(1)} %get-tuple-element.57.router_ref, ...), custom_call_target="tpu_custom_call" | custom-call | tf_op jit(solution)/shard_map/experts/pallas_call | solution.py:492
  23.1 0.2 collective-permute-start.6
  23.3 1.4 %collective-permute-done.6 = bf16[64,2048]{1,0:T(8,128)(2,1)S(1)} collective-permute-done((bf16[64,2048]{1,0:T(8,128)(2,1)S(1)}, bf16[64,2048]{1,0:T(8,128)(2,1)S(1)}, u32[]{:S(2)}, u32[]{:S(2)}) %collective-permute-start.6) | collective-permute-done | bytes 262176 | tf_op jit(solution)/shard_map/ppermute | solution.py:187
  24.7 0.1 add_convert_fusion
  24.8 2.2 %collective-permute-start.9 = (bf16[16,2048]{1,0:T(8,128)(2,1)S(1)}, bf16[16,2048]{1,0:T(8,128)(2,1)S(1)}, u32[]{:S(2)}, u32[]{:S(2)}) collective-permute-start(bf16[16,2048]{1,0:T(8,128)(2,1)S(1)} %get-tuple-element.74), channel_id=1, source_target_pairs={{0,6},{1,7},{2,4},{3,5},{4,2},{5,3},{6,0},{7,1},{8,14},{9,15},{10,... | collective-permute-start | bytes 196616 | tf_op jit(solution)/shard_map/ppermute | solution.py:187
  27.0 0.4 %collective-permute-start.8 = (bf16[16,2048]{1,0:T(8,128)(2,1)S(1)}, bf16[16,2048]{1,0:T(8,128)(2,1)S(1)}, u32[]{:S(2)}, u32[]{:S(2)}) collective-permute-start(bf16[16,2048]{1,0:T(8,128)(2,1)S(1)} %get-tuple-element.75), channel_id=1, source_target_pairs={{0,4},{1,5},{2,6},{3,7},{4,0},{5,1},{6,2},{7,3},{8,12},{9,13},{10,... | collective-permute-start | bytes 196616 | tf_op jit(solution)/shard_map/ppermute | solution.py:187
  27.4 0.9 %collective-permute-start.7 = (bf16[16,2048]{1,0:T(8,128)(2,1)S(1)}, bf16[16,2048]{1,0:T(8,128)(2,1)S(1)}, u32[]{:S(2)}, u32[]{:S(2)}) collective-permute-start(bf16[16,2048]{1,0:T(8,128)(2,1)S(1)} %get-tuple-element.76), channel_id=1, source_target_pairs={{0,2},{1,3},{2,0},{3,1},{4,6},{5,7},{6,4},{7,5},{8,10},{9,11},{10,... | collective-permute-start | bytes 196616 | tf_op jit(solution)/shard_map/ppermute | solution.py:187
  28.4 2.0 %collective-permute-done.9.d_ref = bf16[16,2048]{1,0:T(8,128)(2,1)S(1)} collective-permute-done((bf16[16,2048]{1,0:T(8,128)(2,1)S(1)}, bf16[16,2048]{1,0:T(8,128)(2,1)S(1)}, u32[]{:S(2)}, u32[]{:S(2)}) %collective-permute-start.9) | collective-permute-done | bytes 65568 | tf_op jit(solution)/shard_map/ppermute | solution.py:187
  30.3 0.9 %collective-permute-done.8.c_ref = bf16[16,2048]{1,0:T(8,128)(2,1)S(1)} collective-permute-done((bf16[16,2048]{1,0:T(8,128)(2,1)S(1)}, bf16[16,2048]{1,0:T(8,128)(2,1)S(1)}, u32[]{:S(2)}, u32[]{:S(2)}) %collective-permute-start.8) | collective-permute-done | bytes 65568 | tf_op jit(solution)/shard_map/ppermute | solution.py:187
  31.3 0.4 %collective-permute-done.7.b_ref = bf16[16,2048]{1,0:T(8,128)(2,1)S(1)} collective-permute-done((bf16[16,2048]{1,0:T(8,128)(2,1)S(1)}, bf16[16,2048]{1,0:T(8,128)(2,1)S(1)}, u32[]{:S(2)}, u32[]{:S(2)}) %collective-permute-start.7) | collective-permute-done | bytes 65568 | tf_op jit(solution)/shard_map/ppermute | solution.py:187
  31.8 2.2 %collective-permute-start.10 = (bf16[8,2048]{1,0:T(8,128)(2,1)S(1)}, bf16[8,2048]{1,0:T(8,128)(2,1)S(1)}, u32[]{:S(2)}, u32[]{:S(2)}) collective-permute-start(bf16[8,2048]{1,0:T(8,128)(2,1)S(1)} %get-tuple-element.69), channel_id=1, source_target_pairs={{0,24},{1,25},{2,26},{3,27},{4,28},{5,29},{6,30},{7,31},{8,16},{9,... | collective-permute-start | bytes 98312 | tf_op jit(solution)/shard_map/ppermute | solution.py:187
  33.9 3.6 %collective-permute-done.10.other_ref = bf16[8,2048]{1,0:T(8,128)(2,1)S(1)} collective-permute-done((bf16[8,2048]{1,0:T(8,128)(2,1)S(1)}, bf16[8,2048]{1,0:T(8,128)(2,1)S(1)}, u32[]{:S(2)}, u32[]{:S(2)}) %collective-permute-start.10) | collective-permute-done | bytes 32800 | tf_op jit(solution)/shard_map/ppermute | solution.py:187
  37.5 0.7 %finish.1 = (bf16[1,8,2048]{2,1,0:T(8,128)(2,1)}, bf16[1,8,2048]{2,1,0:T(8,128)(2,1)}) custom-call(f32[8,2048]{1,0:T(8,128)S(1)} %get-tuple-element.68.staying_ref, bf16[8,2048]{1,0:T(8,128)(2,1)S(1)} %collective-permute-done.10.other_ref, f32[8,2048]{1,0:T(8,128)S(1)} %get-tuple-element.70.scale_ref, f32[8,2048]{1,0:T(8,128)S(1)} %get-tuple-element.71.towards_ref, ...), custom_call_target="tpu_custom_call" | custom-call | tf_op jit(solution)/shard_map/finish/pallas_call | solution.py:352
  (12 shorter events, 0.2 us)
Async XLA Ops:
  1.6 8.7 %collective-permute-start.1 = (bf16[24,2304]{1,0:T(8,128)(2,1)S(1)}, bf16[24,2304]{1,0:T(8,128)(2,1)S(1)}, u32[]{:S(2)}, u32[]{:S(2)}) collective-permute-start(bf16[24,2304]{1,0:T(8,128)(2,1)S(1)} %widen.1), channel_id=1, source_target_pairs={{0,16},{1,17},{2,18},{3,19},{4,20},{5,21},{6,22},{7,23},{8,24},{9,... | collective-permute-start | bytes 331784 | tf_op jit(solution)/shard_map/ppermute | solution.py:187
  4.6 5.7 %collective-permute-start = (bf16[16,2176]{1,0:T(8,128)(2,1)S(1)}, bf16[16,2176]{1,0:T(8,128)(2,1)S(1)}, u32[]{:S(2)}, u32[]{:S(2)}) collective-permute-start(bf16[16,2176]{1,0:T(8,128)(2,1)S(1)} %get-tuple-element.38.along_ref), channel_id=1, source_target_pairs={{0,8},{1,9},{2,10},{3,11},{4,12},{5,13},{6,14},{7,15},{8,0},{9,1},... | collective-permute-start | bytes 208904 | tf_op jit(solution)/shard_map/ppermute | solution.py:187
  10.4 7.8 %collective-permute-start.4 = (bf16[24,2176]{1,0:T(8,128)(2,1)S(1)}, bf16[24,2176]{1,0:T(8,128)(2,1)S(1)}, u32[]{:S(2)}, u32[]{:S(2)}) collective-permute-start(bf16[24,2176]{1,0:T(8,128)(2,1)S(1)} %merge.1), channel_id=1, source_target_pairs={{0,6},{1,7},{2,4},{3,5},{4,2},{5,3},{6,0},{7,1},{8,14},{9,15},{10,... | collective-permute-start | bytes 313352 | tf_op jit(solution)/shard_map/ppermute | solution.py:187
  13.0 5.1 %collective-permute-start.3 = (bf16[24,2176]{1,0:T(8,128)(2,1)S(1)}, bf16[24,2176]{1,0:T(8,128)(2,1)S(1)}, u32[]{:S(2)}, u32[]{:S(2)}) collective-permute-start(bf16[24,2176]{1,0:T(8,128)(2,1)S(1)} %merge.1), channel_id=1, source_target_pairs={{0,4},{1,5},{2,6},{3,7},{4,0},{5,1},{6,2},{7,3},{8,12},{9,13},{10,... | collective-permute-start | bytes 313352 | tf_op jit(solution)/shard_map/ppermute | solution.py:187
  13.4 4.7 %collective-permute-start.2 = (bf16[24,2176]{1,0:T(8,128)(2,1)S(1)}, bf16[24,2176]{1,0:T(8,128)(2,1)S(1)}, u32[]{:S(2)}, u32[]{:S(2)}) collective-permute-start(bf16[24,2176]{1,0:T(8,128)(2,1)S(1)} %merge.1), channel_id=1, source_target_pairs={{0,2},{1,3},{2,0},{3,1},{4,6},{5,7},{6,4},{7,5},{8,10},{9,11},{10,... | collective-permute-start | bytes 313352 | tf_op jit(solution)/shard_map/ppermute | solution.py:187
  18.2 1.8 %collective-permute-start.5 = (bf16[96,2176]{1,0:T(8,128)(2,1)S(1)}, bf16[96,2176]{1,0:T(8,128)(2,1)S(1)}, u32[]{:S(2)}, u32[]{:S(2)}) collective-permute-start(bf16[96,2176]{1,0:T(8,128)(2,1)S(1)} %slice_dynamic-update-slice_fusion.4.near_ref), channel_id=1, source_target_pairs={{0,1},{1,0},{2,3},{3,2},{4,5},{5,4},{6,7},{7,6},{8,9},{9,8},{10,11... | collective-permute-start | bytes 1253384 | tf_op jit(solution)/shard_map/ppermute | solution.py:187
  23.1 1.6 %collective-permute-start.6 = (bf16[64,2048]{1,0:T(8,128)(2,1)S(1)}, bf16[64,2048]{1,0:T(8,128)(2,1)S(1)}, u32[]{:S(2)}, u32[]{:S(2)}) collective-permute-start(bf16[64,2048]{1,0:T(8,128)(2,1)S(1)} %get-tuple-element.67), channel_id=1, source_target_pairs={{0,1},{1,0},{2,3},{3,2},{4,5},{5,4},{6,7},{7,6},{8,9},{9,8},{10,11... | collective-permute-start | bytes 786440 | tf_op jit(solution)/shard_map/ppermute | solution.py:187
  24.8 5.5 %collective-permute-start.9 = (bf16[16,2048]{1,0:T(8,128)(2,1)S(1)}, bf16[16,2048]{1,0:T(8,128)(2,1)S(1)}, u32[]{:S(2)}, u32[]{:S(2)}) collective-permute-start(bf16[16,2048]{1,0:T(8,128)(2,1)S(1)} %get-tuple-element.74), channel_id=1, source_target_pairs={{0,6},{1,7},{2,4},{3,5},{4,2},{5,3},{6,0},{7,1},{8,14},{9,15},{10,... | collective-permute-start | bytes 196616 | tf_op jit(solution)/shard_map/ppermute | solution.py:187
  27.0 4.3 %collective-permute-start.8 = (bf16[16,2048]{1,0:T(8,128)(2,1)S(1)}, bf16[16,2048]{1,0:T(8,128)(2,1)S(1)}, u32[]{:S(2)}, u32[]{:S(2)}) collective-permute-start(bf16[16,2048]{1,0:T(8,128)(2,1)S(1)} %get-tuple-element.75), channel_id=1, source_target_pairs={{0,4},{1,5},{2,6},{3,7},{4,0},{5,1},{6,2},{7,3},{8,12},{9,13},{10,... | collective-permute-start | bytes 196616 | tf_op jit(solution)/shard_map/ppermute | solution.py:187
  27.4 4.3 %collective-permute-start.7 = (bf16[16,2048]{1,0:T(8,128)(2,1)S(1)}, bf16[16,2048]{1,0:T(8,128)(2,1)S(1)}, u32[]{:S(2)}, u32[]{:S(2)}) collective-permute-start(bf16[16,2048]{1,0:T(8,128)(2,1)S(1)} %get-tuple-element.76), channel_id=1, source_target_pairs={{0,2},{1,3},{2,0},{3,1},{4,6},{5,7},{6,4},{7,5},{8,10},{9,11},{10,... | collective-permute-start | bytes 196616 | tf_op jit(solution)/shard_map/ppermute | solution.py:187
  31.8 5.8 %collective-permute-start.10 = (bf16[8,2048]{1,0:T(8,128)(2,1)S(1)}, bf16[8,2048]{1,0:T(8,128)(2,1)S(1)}, u32[]{:S(2)}, u32[]{:S(2)}) collective-permute-start(bf16[8,2048]{1,0:T(8,128)(2,1)S(1)} %get-tuple-element.69), channel_id=1, source_target_pairs={{0,24},{1,25},{2,26},{3,27},{4,28},{5,29},{6,30},{7,31},{8,16},{9,... | collective-permute-start | bytes 98312 | tf_op jit(solution)/shard_map/ppermute | solution.py:187

commit v4 on v3

--- a/solution.py
+++ b/solution.py
@@ -174,7 +174,9 @@
 AXES = ("section", "expert")
 SQUARE = 8
 CORE, HALF, SECTION = 1, 8, 16
+EARLY = 2
 LANES = 128
+SQUARE_CHIPS = ((2, 2), (4, 4), (6, 6))
 TOP_COUNT = 8
 VMEM = pl.BlockSpec(memory_space=pltpu.VMEM)
 SMEM = pl.BlockSpec(memory_space=pltpu.SMEM)
@@ -182,9 +184,10 @@
 MIB = 1024 * 1024
 
 
-def swapped(block, distance):
+def swapped(block, even, odd=None):
+    distances = (even, even if odd is None else odd)
     count = lax.axis_size(AXES)
-    return lax.ppermute(block, AXES, [(i, i ^ distance) for i in range(count)])
+    return lax.ppermute(block, AXES, [(i, i ^ distances[i & CORE]) for i in range(count)])
 
 
 def in_hbm(array):
@@ -201,7 +204,7 @@
 
 def pack_kernel(
     fwd_act, fwd_routes, bwd_saved, bwd_grad, bwd_routes, gain, router,
-    along_ref, acts_ref, gain_ref, router_ref, grads_ref, routes_ref, sems,
+    across_ref, along_ref, acts_ref, gain_ref, router_ref, grads_ref, routes_ref, sems,
 ):
     first_section = in_first_section()
     grad_copy = pltpu.make_async_copy(bwd_grad.at[0], grads_ref, sems.at[0])
@@ -228,13 +231,14 @@
     pltpu.make_async_copy(fwd_routes.at[0], routes_ref, sems.at[3]).wait()
     grad_copy.wait()
     routes = routes_ref[...].astype(jnp.float32)
-    routes = jnp.concatenate([routes, jnp.zeros((8, LANES - TOP_COUNT), jnp.float32)], axis=1)
-    blank = jnp.zeros((8, LANES), jnp.float32)
-    grads = grads_ref[...].astype(jnp.float32)
-    along_ref[...] = jnp.concatenate(
-        [jnp.concatenate([normed, routes], axis=1), jnp.concatenate([grads, blank], axis=1)],
-        axis=0,
+    routes = jnp.concatenate(
+        [routes, jnp.zeros((routes.shape[0], LANES - TOP_COUNT), jnp.float32)], axis=1
+    )
+    rows = jnp.concatenate(
+        [normed, grads_ref[...].astype(jnp.float32), routes], axis=1
     ).astype(jnp.bfloat16)
+    across_ref[...] = rows
+    along_ref[...] = jnp.concatenate([rows, rows[:, -LANES:]], axis=1)
     router_copy.wait()
 
 
@@ -244,13 +248,14 @@
     return pl.pallas_call(
         pack_kernel,
         out_shape=[
-            jax.ShapeDtypeStruct((2 * count, width + LANES), jnp.bfloat16),
+            jax.ShapeDtypeStruct((count, 2 * width + LANES), jnp.bfloat16),
+            jax.ShapeDtypeStruct((count, 2 * width + 2 * LANES), jnp.bfloat16),
             jax.ShapeDtypeStruct((count, width), jnp.bfloat16),
             jax.ShapeDtypeStruct(gain.shape, gain.dtype),
             jax.ShapeDtypeStruct(router.shape, router.dtype),
         ],
         in_specs=[HBM] * 7,
-        out_specs=[VMEM] * 4,
+        out_specs=[VMEM] * 5,
         scratch_shapes=[
             pltpu.VMEM((count, width), jnp.bfloat16),
             pltpu.VMEM(fwd_routes.shape[1:], jnp.int32),
@@ -261,24 +266,17 @@
     )(*[in_hbm(x) for x in arrays])
 
 
-def widen_kernel(along_ref, acts_ref, gain_ref, across_ref):
-    rows = along_ref[...].astype(jnp.float32)
-    acts = acts_ref[...].astype(jnp.float32)
+def widen_kernel(acts_ref, gain_ref, raw_ref):
     gain_row = gain_ref[...]
-    width = gain_row.shape[1]
+    count = acts_ref.shape[0]
+    pieces = [gain_row[:, k : k + LANES] for k in range(0, gain_row.shape[1], LANES)]
     gain_rows = jnp.concatenate(
-        [gain_row[:, LANES * k : LANES * k + LANES] for k in range(16)], axis=0
+        [jnp.concatenate(pieces[k : k + count], axis=0) for k in range(0, len(pieces), count)],
+        axis=1,
     )
     gain_high = gain_rows.astype(jnp.bfloat16).astype(jnp.float32)
-    gain_low = gain_rows - gain_high
-    blank = jnp.zeros((8, LANES), jnp.float32)
-    across_ref[...] = jnp.concatenate(
-        [
-            jnp.concatenate([rows[0:8], gain_low[:8]], axis=1),
-            jnp.concatenate([rows[8:16, :width], gain_high[:8], gain_low[8:]], axis=1),
-            jnp.concatenate([acts, gain_high[8:], blank], axis=1),
-        ],
-        axis=0,
+    raw_ref[...] = jnp.concatenate(
+        [acts_ref[...].astype(jnp.float32), gain_high, gain_rows - gain_high], axis=1
     ).astype(jnp.bfloat16)
 
 
@@ -295,24 +293,28 @@
 
 def merge_kernel(along_ref, across_ref, mine_ref):
     first_section = in_first_section()
-    used = mine_ref.shape[1]
-    along = along_ref[...].astype(jnp.float32)
-    across = across_ref[...].astype(jnp.float32)[:, :used]
+    used = across_ref.shape[1]
+    width = (used - LANES) // 2
+    along = along_ref[...].astype(jnp.float32)[:, :used]
+    across = across_ref[...].astype(jnp.float32)
+    forward = jnp.where(first_section, along, across)
+    backward = jnp.where(first_section, across, along)
+    routes = jnp.concatenate(
+        [forward[:, 2 * width : 2 * width + TOP_COUNT], backward[:, 2 * width : -TOP_COUNT]], axis=1
+    )
     mine_ref[...] = jnp.concatenate(
-        [
-            jnp.where(first_section, along[:8], across[:8]),
-            jnp.where(first_section, across[:16], along),
-        ],
-        axis=0,
+        [forward[:, :width], backward[:, : 2 * width], routes], axis=1
     ).astype(jnp.bfloat16)
 
 
 def leave_kernel(a_ref, b_ref, c_ref, d_ref, leaving_ref, staying_ref):
     first_section = in_first_section()
+    width = leaving_ref.shape[1]
     total = a_ref[...].astype(jnp.float32) + b_ref[...].astype(jnp.float32)
     total = total + c_ref[...].astype(jnp.float32) + d_ref[...].astype(jnp.float32)
-    leaving_ref[...] = jnp.where(first_section, total[:8], total[8:]).astype(jnp.bfloat16)
-    staying_ref[...] = jnp.where(first_section, total[8:], total[:8])
+    forward, backward = total[:, :width], total[:, width:]
+    leaving_ref[...] = jnp.where(first_section, forward, backward).astype(jnp.bfloat16)
+    staying_ref[...] = jnp.where(first_section, backward, forward)
 
 
 def finish_kernel(
@@ -404,26 +406,23 @@
 
 
 def expert_kernel(
-    near_ref, far_ref, router_ref, gate_ref, gate_turned_ref,
-    up_ref, up_turned_ref, up_rest_ref, up_rest_turned_ref, down_ref, down_turned_ref,
-    kept_ref, sent_ref,
+    near_ref, next_ref, far_ref, last_ref, router_ref,
+    gate_ref, gate_turned_ref, down_ref, down_turned_ref, *refs,
 ):
+    up_refs, up_turned_refs, (kept_ref, sent_ref) = refs[:-2:2], refs[1:-2:2], refs[-2:]
     width, hidden_count = gate_ref.shape
     step = 256
-    split = up_ref.shape[0]
     own_expert = lax.axis_index("expert")
 
-    pairs = near_ref.shape[0] * 2 // 3
-    tops = jnp.concatenate([near_ref[:pairs], far_ref[:pairs]], axis=0)
-    grads = jnp.concatenate([near_ref[pairs:, :width], far_ref[pairs:, :width]], axis=0)
-    routes = tops[:, width:].astype(jnp.float32)
-    normed = tops[:, :width]
-
-    def forward(rows):
-        return jnp.concatenate([rows[16 * k : 16 * k + 8] for k in range(SQUARE)], axis=0)
-
-    def backward(rows):
-        return jnp.concatenate([rows[16 * k + 8 : 16 * k + 16] for k in range(SQUARE)], axis=0)
+    def both(first, last):
+        blocks = (near_ref, next_ref, far_ref, last_ref)
+        return jnp.concatenate([block[:, first:last] for block in blocks], axis=0)
+
+    normed = jnp.concatenate([both(0, width), both(width, 2 * width)], axis=0)
+    grads = both(2 * width, 3 * width)
+    routes = both(3 * width, 3 * width + LANES).astype(jnp.float32)
+    routes = jnp.concatenate([routes[:, :TOP_COUNT], routes[:, TOP_COUNT : 2 * TOP_COUNT]], axis=0)
+    half = grads.shape[0]
 
     router = router_ref[...]
     contract = (((1,), (1,)), ((), ()))
@@ -437,28 +436,29 @@
     gates = raised / jnp.sum(raised, axis=-1, keepdims=True)
     own = jnp.where(labels == own_expert, 1.0, 0.0)
     gate_own = jnp.sum(own * gates, axis=-1, keepdims=True)
-    gate_f, gate_b = forward(gate_own), backward(gate_own)
+    gate_f, gate_b = gate_own[:half], gate_own[half:]
 
     hiddens, d_pres, d_ups = [], [], []
     dgate = 0.0
     for piece in range(hidden_count // step):
         cols = slice(piece * step, piece * step + step)
         pre_gate = jnp.dot(normed, gate_ref[:, cols], preferred_element_type=jnp.float32)
-        pre_up = jnp.dot(normed[:, :split], up_ref[:, cols], preferred_element_type=jnp.float32)
-        pre_up = pre_up + jnp.dot(
-            normed[:, split:], up_rest_ref[:, cols], preferred_element_type=jnp.float32
-        )
+        pre_up, start = 0.0, 0
+        for ref in up_refs:
+            rows = normed[:, start : start + ref.shape[0]]
+            pre_up = pre_up + jnp.dot(rows, ref[:, cols], preferred_element_type=jnp.float32)
+            start += ref.shape[0]
         d_hidden = jnp.dot(grads, down_turned_ref[:, cols], preferred_element_type=jnp.float32)
         sigma = jax.nn.sigmoid(pre_gate)
         silu_val = pre_gate * sigma
         hidden = silu_val * pre_up
-        hiddens.append((forward(hidden) * gate_f).astype(jnp.bfloat16))
-        dgate = dgate + jnp.sum(backward(hidden) * d_hidden, axis=-1, keepdims=True)
+        hiddens.append((hidden[:half] * gate_f).astype(jnp.bfloat16))
+        dgate = dgate + jnp.sum(hidden[half:] * d_hidden, axis=-1, keepdims=True)
         d_hidden = d_hidden * gate_b
-        d_ups.append((d_hidden * backward(silu_val)).astype(jnp.bfloat16))
-        sigma_b = backward(sigma)
-        slope = sigma_b * (1.0 + backward(pre_gate) * (1.0 - sigma_b))
-        d_pres.append((d_hidden * backward(pre_up) * slope).astype(jnp.bfloat16))
+        d_ups.append((d_hidden * silu_val[half:]).astype(jnp.bfloat16))
+        sigma_b = sigma[half:]
+        slope = sigma_b * (1.0 + pre_gate[half:] * (1.0 - sigma_b))
+        d_pres.append((d_hidden * pre_up[half:] * slope).astype(jnp.bfloat16))
 
     hidden = jnp.concatenate(hiddens, axis=1)
     d_pre = jnp.concatenate(d_pres, axis=1)
@@ -467,46 +467,50 @@
     d_normed = jnp.concatenate(
         [
             jnp.dot(d_up, mat[...], preferred_element_type=jnp.float32)
-            for mat in (up_turned_ref, up_rest_turned_ref)
+            for mat in up_turned_refs
         ],
         axis=1,
     )
     d_normed = d_normed + jnp.dot(d_pre, gate_turned_ref[...], preferred_element_type=jnp.float32)
-    spread = gate_b * dgate * (backward(own) - backward(gates))
+    spread = gate_b * dgate * (own[half:] - gates[half:])
     spread_high = spread.astype(jnp.bfloat16)
     spread_low = (spread - spread_high.astype(jnp.float32)).astype(jnp.bfloat16)
     d_normed = d_normed + jnp.dot(spread_high, router, preferred_element_type=jnp.float32)
     d_normed = d_normed + jnp.dot(spread_low, router, preferred_element_type=jnp.float32)
 
-    parts = []
-    for k in range(SQUARE):
-        parts.append(out_f[8 * k : 8 * k + 8])
-        parts.append(d_normed[8 * k : 8 * k + 8])
-    kept_ref[...] = jnp.concatenate(parts[:SQUARE], axis=0).astype(jnp.bfloat16)
-    sent_ref[...] = jnp.concatenate(parts[SQUARE:], axis=0).astype(jnp.bfloat16)
-
-
-def run_experts(near, far, router, *weights):
+    quarter = half // 2
+    for ref, rows in ((kept_ref, slice(0, quarter)), (sent_ref, slice(quarter, half))):
+        ref[...] = jnp.concatenate([out_f[rows], d_normed[rows]], axis=1).astype(jnp.bfloat16)
+
+
+def run_experts(blocks, router, *weights):
     width = router.shape[1]
-    rows = SQUARE // 2 * 16
     return pl.pallas_call(
         expert_kernel,
-        out_shape=[jax.ShapeDtypeStruct((rows, width), jnp.bfloat16)] * 2,
-        in_specs=[VMEM] * (3 + len(weights)),
+        out_shape=[jax.ShapeDtypeStruct((2 * blocks[0].shape[0], 2 * width), jnp.bfloat16)] * 2,
+        in_specs=[VMEM] * (1 + len(blocks) + len(weights)),
         out_specs=[VMEM] * 2,
         compiler_params=pltpu.CompilerParams(vmem_limit_bytes=24 * MIB),
         name="experts",
-    )(near, far, router, *weights)
-
-
-def ending_kernel(across_ref, scale_ref, along_ref, back_ref, rest_ref):
+    )(*blocks, router, *weights)
+
+
+def ending_kernel(across_ref, raw_ref, scale_ref, along_ref, back_ref, rest_ref):
     first_section = in_first_section()
-    packed = across_ref[...].astype(jnp.float32)
-    width = scale_ref.shape[1]
-    grads = packed[8:16, :width]
-    acts = packed[16:24, :width]
-    gain_rows = packed[8:24, width : width + LANES] + packed[0:16, width + LANES :]
-    gain_row = jnp.concatenate([gain_rows[k : k + 1] for k in range(16)], axis=1)
+    count, width = scale_ref.shape
+    grads = across_ref[...].astype(jnp.float32)[:, width : 2 * width]
+    raw = raw_ref[...].astype(jnp.float32)
+    acts, gain_rows = raw[:, :width], raw[:, width:]
+    spread = width // count
+    gain_rows = gain_rows[:, :spread] + gain_rows[:, spread:]
+    gain_row = jnp.concatenate(
+        [
+            gain_rows[row : row + 1, k : k + LANES]
+            for k in range(0, spread, LANES)
+            for row in range(count)
+        ],
+        axis=1,
+    )
     factor = root_factor(acts)
     unit = acts * factor
     scale_ref[...] = jnp.where(first_section, factor * gain_row, 1.0)
@@ -523,36 +527,43 @@
     fwd_act, fwd_routes, bwd_saved, bwd_grad, bwd_routes, norm_gain, router, w_gate, w_up, w_down
 ):
     count, width = fwd_act.shape[1:]
-    used = width + LANES
-    along, acts, gain_row, router_rows = pack_rows(
+    across, along, acts, gain_row, router_rows = pack_rows(
         fwd_act, fwd_routes, bwd_saved, bwd_grad, bwd_routes, norm_gain, router.T
     )
-    wide = jax.ShapeDtypeStruct((3 * count, used + LANES), jnp.bfloat16)
-    across = in_vmem(widen_kernel, "widen", [wide], along, acts, gain_row)[0]
     across = swapped(across, SECTION)
     along = swapped(along, HALF)
-    upper = width // 2
-    gate_mats, up_mats = fetched((w_gate[0], 0, width), (w_up[0], 0, upper))
-    along, gate_mats, up_mats = lax.optimization_barrier((along, gate_mats, up_mats))
-    rows = jax.ShapeDtypeStruct((3 * count, used), jnp.bfloat16)
+    cuts = (width // 2, width)
+    gate_hbm, up_hbm, down_hbm = w_gate[0], w_up[0], w_down[0]
+    gate_mats, *ups = fetched((gate_hbm, 0, width), (up_hbm, 0, cuts[0]))
+    along, gate_mats, ups = lax.optimization_barrier((along, gate_mats, ups))
+    rows = jax.ShapeDtypeStruct((count, 3 * width + LANES), jnp.bfloat16)
     mine = in_vmem(merge_kernel, "merge", [rows], along, across)[0]
-    down_hbm, up_hbm, _ = lax.optimization_barrier((w_down[0], w_up[0], mine))
-    rest_mats, down_mats = fetched((up_hbm, upper, width - upper), (down_hbm, 0, down_hbm.shape[0]))
+    down_hbm, up_hbm, _ = lax.optimization_barrier((down_hbm, up_hbm, mine))
+    down_mats, *more = fetched(
+        (down_hbm, 0, down_hbm.shape[0]), (up_hbm, cuts[0], cuts[1] - cuts[0])
+    )
+    ups = ups + more
+    received = [swapped(mine, *k) for k in SQUARE_CHIPS]
+    early = jnp.concatenate([mine, received[EARLY]], axis=0)
+    late = jnp.concatenate([b for i, b in enumerate(received) if i != EARLY], axis=0)
+    late, ups, down_mats = lax.optimization_barrier((late, ups, down_mats))
+    blocks = [early, late, swapped(early, CORE), swapped(late, CORE)]
+
+    weights = [m for mats in [gate_mats, down_mats] + ups for m in mats]
+    kept, sent = run_experts(blocks, router_rows, *weights)
+
+    chip = added(kept, swapped(sent, CORE))
+    acts, chip = lax.optimization_barrier((acts, chip))
     real = jax.ShapeDtypeStruct((count, width), jnp.float32)
-    ending = in_vmem(ending_kernel, "endings", [real] * 4, across)
-    blocks = [mine] + [swapped(mine, k) for k in (2, 4, 6)]
-    near = jnp.concatenate([b[:16] for b in blocks] + [b[16:] for b in blocks], axis=0)
-    near, rest_mats, down_mats, ending = lax.optimization_barrier(
-        (near, rest_mats, down_mats, ending)
-    )
-    far = swapped(near, CORE)
-
-    kept, sent = run_experts(
-        near, far, router_rows, *gate_mats, *up_mats, *rest_mats, *down_mats
-    )
-
-    chip = added(kept, swapped(sent, CORE))
-    pieces = [chip[0:16]] + [swapped(chip[8 * k : 8 * k + 16], k) for k in (2, 4, 6)]
+    wide = jax.ShapeDtypeStruct((count, width + 2 * (width // count)), jnp.bfloat16)
+    raw = swapped(in_vmem(widen_kernel, "widen", [wide], acts, gain_row)[0], SECTION)
+    pieces = [chip[:count]]
+    order = [EARLY] + [i for i in range(len(SQUARE_CHIPS)) if i != EARLY]
+    places = [order.index(i) + 1 for i in range(len(SQUARE_CHIPS))]
+    pieces += [
+        swapped(chip[i * count : (i + 1) * count], *k) for i, k in zip(places, SQUARE_CHIPS)
+    ]
+    ending = in_vmem(ending_kernel, "endings", [real] * 4, across, raw)
     small = jax.ShapeDtypeStruct((count, width), jnp.bfloat16)
     leaving, staying = in_vmem(leave_kernel, "leave", [small, real], *pieces)
     other = swapped(leaving, SECTION + HALF)

time: 38.4 us -> 37.8 us (0.984)
  waiting for transfers between devices: 11.4 us -> 9 us
  starting transfers between devices: 15.1 us -> 16.8 us
    ppermute x11 -> x13, waiting for transfers between devices: 11.4 us -> 9 us  [swapped(): lax.ppermute(block, AXES, [(i, i ^ distances[i & CORE]) for i in range(co...]
    ppermute x11 -> x13, starting transfers between devices: 15.1 us -> 16.8 us  [swapped(): lax.ppermute(block, AXES, [(i, i ^ distances[i & CORE]) for i in range(co...]
  transfers between devices with their start and end apart: 11 -> 13, of which waited for: 7 -> 9; matrix products, arithmetic and copies ran while one was open for 0% -> 0% of each run, Pallas kernels for 15% -> 16%
where the time goes in v4:
time: 37.8 us; the launch traced here: 37.7 us
  starting transfers between devices  16.8 us (44%)
  Pallas kernels  11 us (29%)
  waiting for transfers between devices  9 us (24%)
  between operations  0.75 us (2%)
    ppermute x13, starting transfers between devices, swapped(): lax.ppermute(block, AXES, [(i, i ^ distances[i & CORE]) for i in range(co...  16.8 us
    ppermute x13, waiting for transfers between devices, swapped(): lax.ppermute(block, AXES, [(i, i ^ distances[i & CORE]) for i in range(co...  9 us
    pallas_call x2, Pallas kernels, fetched(): pl.pallas_call(functools.partial(fetch_kernel, parts=sizes), out_shape=he...  5.99 us
    pallas_call x1, Pallas kernels, run_experts(): pl.pallas_call(expert_kernel, out_shape=[jax.ShapeDtypeStruct((2 * blocks...  3.05 us
    pallas_call x1, Pallas kernels, pack_rows(): pl.pallas_call(pack_kernel, out_shape=[jax.ShapeDtypeStruct((count, 2 * w...  0.97 us
  transfers between devices with their start and end apart: 13, of which 9 were waited for; matrix products, arithmetic and copies ran while one was open for 0% of the time, Pallas kernels for 16%

profile of v4, /device:TPU:0, one launch (start us, length us, event | category | flops | bytes accessed | tf_op | source)
XLA Modules:
  0.0 37.7 jit_solution(15654187134251254529)
XLA Ops:
  0.6 1.0 %pack.1 = (bf16[8,4224]{1,0:T(8,128)(2,1)S(1)}, bf16[8,4352]{1,0:T(8,128)(2,1)S(1)}, bf16[8,2048]{1,0:T(8,128)(2,1)S(1)}, f32[1,2048]{1,0:T(1,128)S(1)}, bf16[16,2048]{1,0:T(8,128)(2,1)S(1)}) custom-call(bf16[1,8,2048]{2,1,0:T(8,128)(2,1)} %fwd_act.1, s32[1,8,8]{2,1,0:T(8,128)} %fwd_routes.1, bf16[1,8,2048]{2,1,0:T(8,128)(2,1)} %bwd_saved.1, ...), custom_call_target="tpu_custom_call" | custom-call | tf_op jit(solution)/shard_map/pack/pallas_call | solution.py:248
  1.6 4.1 %collective-permute-start = (bf16[8,4352]{1,0:T(8,128)(2,1)S(1)}, bf16[8,4352]{1,0:T(8,128)(2,1)S(1)}, u32[]{:S(2)}, u32[]{:S(2)}) collective-permute-start(bf16[8,4352]{1,0:T(8,128)(2,1)S(1)} %get-tuple-element.40), channel_id=1, source_target_pairs={{0,8},{1,9},{2,10},{3,11},{4,12},{5,13},{6,14},{7,15},{8,0},{9,1},... | collective-permute-start | bytes 208904 | tf_op jit(solution)/shard_map/ppermute | solution.py:190
  5.7 1.5 %collective-permute-start.1 = (bf16[8,4224]{1,0:T(8,128)(2,1)S(1)}, bf16[8,4224]{1,0:T(8,128)(2,1)S(1)}, u32[]{:S(2)}, u32[]{:S(2)}) collective-permute-start(bf16[8,4224]{1,0:T(8,128)(2,1)S(1)} %get-tuple-element.46), channel_id=1, source_target_pairs={{0,16},{1,17},{2,18},{3,19},{4,20},{5,21},{6,22},{7,23},{8,24},{9,... | collective-permute-start | bytes 202760 | tf_op jit(solution)/shard_map/ppermute | solution.py:190
  7.2 3.1 %fetch.2 = (bf16[2048,768]{1,0:T(8,128)(2,1)S(1)}, bf16[1024,768]{1,0:T(8,128)(2,1)S(1)}, bf16[768,2048]{1,0:T(8,128)(2,1)S(1)}, bf16[768,1024]{1,0:T(8,128)(2,1)S(1)}) custom-call(bf16[2048,768]{1,0:T(8,128)(2,1)} %bitcast.6, bf16[2048,768]{1,0:T(8,128)(2,1)} %bitcast.4), custom_call_target="tpu_custom_call" | custom-call | bytes 9437184 | tf_op jit(solution)/shard_map/fetch/pallas_call | solution.py:395
  10.3 0.0 collective-permute-done.along_ref
  10.3 0.0 collective-permute-done.1.across_ref
  10.3 0.1 merge.1
  10.4 2.5 %collective-permute-start.2 = (bf16[8,6272]{1,0:T(8,128)(2,1)S(1)}, bf16[8,6272]{1,0:T(8,128)(2,1)S(1)}, u32[]{:S(2)}, u32[]{:S(2)}) collective-permute-start(bf16[8,6272]{1,0:T(8,128)(2,1)S(1)} %merge.1), channel_id=1, source_target_pairs={{0,6},{1,7},{2,4},{3,5},{4,2},{5,3},{6,0},{7,1},{8,14},{9,15},{10,... | collective-permute-start | bytes 301064 | tf_op jit(solution)/shard_map/ppermute | solution.py:190
  12.9 0.4 %collective-permute-start.4 = (bf16[8,6272]{1,0:T(8,128)(2,1)S(1)}, bf16[8,6272]{1,0:T(8,128)(2,1)S(1)}, u32[]{:S(2)}, u32[]{:S(2)}) collective-permute-start(bf16[8,6272]{1,0:T(8,128)(2,1)S(1)} %merge.1), channel_id=1, source_target_pairs={{0,4},{1,5},{2,6},{3,7},{4,0},{5,1},{6,2},{7,3},{8,12},{9,13},{10,... | collective-permute-start | bytes 301064 | tf_op jit(solution)/shard_map/ppermute | solution.py:190
  13.4 0.5 %collective-permute-start.3 = (bf16[8,6272]{1,0:T(8,128)(2,1)S(1)}, bf16[8,6272]{1,0:T(8,128)(2,1)S(1)}, u32[]{:S(2)}, u32[]{:S(2)}) collective-permute-start(bf16[8,6272]{1,0:T(8,128)(2,1)S(1)} %merge.1), channel_id=1, source_target_pairs={{0,2},{1,3},{2,0},{3,1},{4,6},{5,7},{6,4},{7,5},{8,10},{9,11},{10,... | collective-permute-start | bytes 301064 | tf_op jit(solution)/shard_map/ppermute | solution.py:190
  13.9 2.9 %fetch.3 = (bf16[768,2048]{1,0:T(8,128)(2,1)S(1)}, bf16[1024,768]{1,0:T(8,128)(2,1)S(1)}, bf16[2048,768]{1,0:T(8,128)(2,1)S(1)}, bf16[768,1024]{1,0:T(8,128)(2,1)S(1)}) custom-call(bf16[768,2048]{1,0:T(8,128)(2,1)} %bitcast.7, bf16[2048,768]{1,0:T(8,128)(2,1)} %bitcast.5), custom_call_target="tpu_custom_call" | custom-call | bytes 9437184 | tf_op jit(solution)/shard_map/fetch/pallas_call | solution.py:395
  16.9 0.1 collective-permute-start.5
  16.9 0.8 %collective-permute-done.4 = bf16[8,6272]{1,0:T(8,128)(2,1)S(1)} collective-permute-done((bf16[8,6272]{1,0:T(8,128)(2,1)S(1)}, bf16[8,6272]{1,0:T(8,128)(2,1)S(1)}, u32[]{:S(2)}, u32[]{:S(2)}) %collective-permute-start.4) | collective-permute-done | bytes 100384 | tf_op jit(solution)/shard_map/ppermute | solution.py:190
  17.8 0.3 collective-permute-done.3
  18.1 0.1 collective-permute-start.6
  18.1 0.2 collective-permute-done.5.far_ref
  18.4 1.2 %collective-permute-done.6.last_ref = bf16[16,6272]{1,0:T(8,128)(2,1)S(1)} collective-permute-done((bf16[16,6272]{1,0:T(8,128)(2,1)S(1)}, bf16[16,6272]{1,0:T(8,128)(2,1)S(1)}, u32[]{:S(2)}, u32[]{:S(2)}) %collective-permute-start.6) | collective-permute-done | bytes 200736 | tf_op jit(solution)/shard_map/ppermute | solution.py:190
  19.6 3.1 %experts.1 = (bf16[32,4096]{1,0:T(8,128)(2,1)S(1)}, bf16[32,4096]{1,0:T(8,128)(2,1)S(1)}) custom-call(bf16[16,6272]{1,0:T(8,128)(2,1)S(1)} %pad_maximum_fusion.near_ref, bf16[16,6272]{1,0:T(8,128)(2,1)S(1)} %pad_maximum_fusion.1.next_ref, bf16[16,6272]{1,0:T(8,128)(2,1)S(1)} %collective-permute-done.5.far_ref, ...), custom_call_target="tpu_custom_call" | custom-call | tf_op jit(solution)/shard_map/experts/pallas_call | solution.py:488
  22.6 0.2 collective-permute-start.7
  22.8 1.4 %collective-permute-done.7 = bf16[32,4096]{1,0:T(8,128)(2,1)S(1)} collective-permute-done((bf16[32,4096]{1,0:T(8,128)(2,1)S(1)}, bf16[32,4096]{1,0:T(8,128)(2,1)S(1)}, u32[]{:S(2)}, u32[]{:S(2)}) %collective-permute-start.7) | collective-permute-done | bytes 262176 | tf_op jit(solution)/shard_map/ppermute | solution.py:190
  24.2 0.1 add_convert_fusion
  24.3 2.0 %collective-permute-start.10 = (bf16[8,4096]{1,0:T(8,128)(2,1)S(1)}, bf16[8,4096]{1,0:T(8,128)(2,1)S(1)}, u32[]{:S(2)}, u32[]{:S(2)}) collective-permute-start(bf16[8,4096]{1,0:T(8,128)(2,1)S(1)} %get-tuple-element.76), channel_id=1, source_target_pairs={{0,6},{1,7},{2,4},{3,5},{4,2},{5,3},{6,0},{7,1},{8,14},{9,15},{10,... | collective-permute-start | bytes 196616 | tf_op jit(solution)/shard_map/ppermute | solution.py:190
  26.4 0.5 %collective-permute-start.9 = (bf16[8,4096]{1,0:T(8,128)(2,1)S(1)}, bf16[8,4096]{1,0:T(8,128)(2,1)S(1)}, u32[]{:S(2)}, u32[]{:S(2)}) collective-permute-start(bf16[8,4096]{1,0:T(8,128)(2,1)S(1)} %get-tuple-element.77), channel_id=1, source_target_pairs={{0,4},{1,5},{2,6},{3,7},{4,0},{5,1},{6,2},{7,3},{8,12},{9,13},{10,... | collective-permute-start | bytes 196616 | tf_op jit(solution)/shard_map/ppermute | solution.py:190
  26.8 1.0 %collective-permute-start.8 = (bf16[8,4096]{1,0:T(8,128)(2,1)S(1)}, bf16[8,4096]{1,0:T(8,128)(2,1)S(1)}, u32[]{:S(2)}, u32[]{:S(2)}) collective-permute-start(bf16[8,4096]{1,0:T(8,128)(2,1)S(1)} %get-tuple-element.78), channel_id=1, source_target_pairs={{0,2},{1,3},{2,0},{3,1},{4,6},{5,7},{6,4},{7,5},{8,10},{9,11},{10,... | collective-permute-start | bytes 196616 | tf_op jit(solution)/shard_map/ppermute | solution.py:190
  27.9 1.2 %collective-permute-start.12 = (bf16[8,2560]{1,0:T(8,128)(2,1)S(1)}, bf16[8,2560]{1,0:T(8,128)(2,1)S(1)}, u32[]{:S(2)}, u32[]{:S(2)}) collective-permute-start(bf16[8,2560]{1,0:T(8,128)(2,1)S(1)} %widen.1), channel_id=1, source_target_pairs={{0,16},{1,17},{2,18},{3,19},{4,20},{5,21},{6,22},{7,23},{8,24},{9,... | collective-permute-start | bytes 122888 | tf_op jit(solution)/shard_map/ppermute | solution.py:190
  29.1 0.7 %collective-permute-done.10.d_ref = bf16[8,4096]{1,0:T(8,128)(2,1)S(1)} collective-permute-done((bf16[8,4096]{1,0:T(8,128)(2,1)S(1)}, bf16[8,4096]{1,0:T(8,128)(2,1)S(1)}, u32[]{:S(2)}, u32[]{:S(2)}) %collective-permute-start.10) | collective-permute-done | bytes 65568 | tf_op jit(solution)/shard_map/ppermute | solution.py:190
  29.9 0.8 %collective-permute-done.9.c_ref = bf16[8,4096]{1,0:T(8,128)(2,1)S(1)} collective-permute-done((bf16[8,4096]{1,0:T(8,128)(2,1)S(1)}, bf16[8,4096]{1,0:T(8,128)(2,1)S(1)}, u32[]{:S(2)}, u32[]{:S(2)}) %collective-permute-start.9) | collective-permute-done | bytes 65568 | tf_op jit(solution)/shard_map/ppermute | solution.py:190
  30.6 0.5 %collective-permute-done.8.b_ref = bf16[8,4096]{1,0:T(8,128)(2,1)S(1)} collective-permute-done((bf16[8,4096]{1,0:T(8,128)(2,1)S(1)}, bf16[8,4096]{1,0:T(8,128)(2,1)S(1)}, u32[]{:S(2)}, u32[]{:S(2)}) %collective-permute-start.8) | collective-permute-done | bytes 65568 | tf_op jit(solution)/shard_map/ppermute | solution.py:190
  31.1 2.6 %collective-permute-start.11 = (bf16[8,2048]{1,0:T(8,128)(2,1)S(1)}, bf16[8,2048]{1,0:T(8,128)(2,1)S(1)}, u32[]{:S(2)}, u32[]{:S(2)}) collective-permute-start(bf16[8,2048]{1,0:T(8,128)(2,1)S(1)} %get-tuple-element.69), channel_id=1, source_target_pairs={{0,24},{1,25},{2,26},{3,27},{4,28},{5,29},{6,30},{7,31},{8,16},{9,... | collective-permute-start | bytes 98312 | tf_op jit(solution)/shard_map/ppermute | solution.py:190
  33.7 0.1 endings.1
  33.8 3.1 %collective-permute-done.11.other_ref = bf16[8,2048]{1,0:T(8,128)(2,1)S(1)} collective-permute-done((bf16[8,2048]{1,0:T(8,128)(2,1)S(1)}, bf16[8,2048]{1,0:T(8,128)(2,1)S(1)}, u32[]{:S(2)}, u32[]{:S(2)}) %collective-permute-start.11) | collective-permute-done | bytes 32800 | tf_op jit(solution)/shard_map/ppermute | solution.py:190
  36.9 0.7 %finish.1 = (bf16[1,8,2048]{2,1,0:T(8,128)(2,1)}, bf16[1,8,2048]{2,1,0:T(8,128)(2,1)}) custom-call(f32[8,2048]{1,0:T(8,128)S(1)} %get-tuple-element.68.staying_ref, bf16[8,2048]{1,0:T(8,128)(2,1)S(1)} %collective-permute-done.11.other_ref, f32[8,2048]{1,0:T(8,128)S(1)} %get-tuple-element.72.scale_ref, f32[8,2048]{1,0:T(8,128)S(1)} %get-tuple-element.73.towards_ref, ...), custom_call_target="tpu_custom_call" | custom-call | tf_op jit(solution)/shard_map/finish/pallas_call | solution.py:354
  (7 shorter events, 0.1 us)
Async XLA Ops:
  1.6 8.7 %collective-permute-start = (bf16[8,4352]{1,0:T(8,128)(2,1)S(1)}, bf16[8,4352]{1,0:T(8,128)(2,1)S(1)}, u32[]{:S(2)}, u32[]{:S(2)}) collective-permute-start(bf16[8,4352]{1,0:T(8,128)(2,1)S(1)} %get-tuple-element.40), channel_id=1, source_target_pairs={{0,8},{1,9},{2,10},{3,11},{4,12},{5,13},{6,14},{7,15},{8,0},{9,1},... | collective-permute-start | bytes 208904 | tf_op jit(solution)/shard_map/ppermute | solution.py:190
  5.7 4.6 %collective-permute-start.1 = (bf16[8,4224]{1,0:T(8,128)(2,1)S(1)}, bf16[8,4224]{1,0:T(8,128)(2,1)S(1)}, u32[]{:S(2)}, u32[]{:S(2)}) collective-permute-start(bf16[8,4224]{1,0:T(8,128)(2,1)S(1)} %get-tuple-element.46), channel_id=1, source_target_pairs={{0,16},{1,17},{2,18},{3,19},{4,20},{5,21},{6,22},{7,23},{8,24},{9,... | collective-permute-start | bytes 202760 | tf_op jit(solution)/shard_map/ppermute | solution.py:190
  10.4 6.4 %collective-permute-start.2 = (bf16[8,6272]{1,0:T(8,128)(2,1)S(1)}, bf16[8,6272]{1,0:T(8,128)(2,1)S(1)}, u32[]{:S(2)}, u32[]{:S(2)}) collective-permute-start(bf16[8,6272]{1,0:T(8,128)(2,1)S(1)} %merge.1), channel_id=1, source_target_pairs={{0,6},{1,7},{2,4},{3,5},{4,2},{5,3},{6,0},{7,1},{8,14},{9,15},{10,... | collective-permute-start | bytes 301064 | tf_op jit(solution)/shard_map/ppermute | solution.py:190
  12.9 4.8 %collective-permute-start.4 = (bf16[8,6272]{1,0:T(8,128)(2,1)S(1)}, bf16[8,6272]{1,0:T(8,128)(2,1)S(1)}, u32[]{:S(2)}, u32[]{:S(2)}) collective-permute-start(bf16[8,6272]{1,0:T(8,128)(2,1)S(1)} %merge.1), channel_id=1, source_target_pairs={{0,4},{1,5},{2,6},{3,7},{4,0},{5,1},{6,2},{7,3},{8,12},{9,13},{10,... | collective-permute-start | bytes 301064 | tf_op jit(solution)/shard_map/ppermute | solution.py:190
  13.4 4.6 %collective-permute-start.3 = (bf16[8,6272]{1,0:T(8,128)(2,1)S(1)}, bf16[8,6272]{1,0:T(8,128)(2,1)S(1)}, u32[]{:S(2)}, u32[]{:S(2)}) collective-permute-start(bf16[8,6272]{1,0:T(8,128)(2,1)S(1)} %merge.1), channel_id=1, source_target_pairs={{0,2},{1,3},{2,0},{3,1},{4,6},{5,7},{6,4},{7,5},{8,10},{9,11},{10,... | collective-permute-start | bytes 301064 | tf_op jit(solution)/shard_map/ppermute | solution.py:190
  16.9 1.5 %collective-permute-start.5 = (bf16[16,6272]{1,0:T(8,128)(2,1)S(1)}, bf16[16,6272]{1,0:T(8,128)(2,1)S(1)}, u32[]{:S(2)}, u32[]{:S(2)}) collective-permute-start(bf16[16,6272]{1,0:T(8,128)(2,1)S(1)} %pad_maximum_fusion.near_ref), channel_id=1, source_target_pairs={{0,1},{1,0},{2,3},{3,2},{4,5},{5,4},{6,7},{7,6},{8,9},{9,8},{10,11... | collective-permute-start | bytes 602120 | tf_op jit(solution)/shard_map/ppermute | solution.py:190
  18.1 1.5 %collective-permute-start.6 = (bf16[16,6272]{1,0:T(8,128)(2,1)S(1)}, bf16[16,6272]{1,0:T(8,128)(2,1)S(1)}, u32[]{:S(2)}, u32[]{:S(2)}) collective-permute-start(bf16[16,6272]{1,0:T(8,128)(2,1)S(1)} %pad_maximum_fusion.1.next_ref), channel_id=1, source_target_pairs={{0,1},{1,0},{2,3},{3,2},{4,5},{5,4},{6,7},{7,6},{8,9},{9,8},{10,11... | collective-permute-start | bytes 602120 | tf_op jit(solution)/shard_map/ppermute | solution.py:190
  22.6 1.6 %collective-permute-start.7 = (bf16[32,4096]{1,0:T(8,128)(2,1)S(1)}, bf16[32,4096]{1,0:T(8,128)(2,1)S(1)}, u32[]{:S(2)}, u32[]{:S(2)}) collective-permute-start(bf16[32,4096]{1,0:T(8,128)(2,1)S(1)} %get-tuple-element.66), channel_id=1, source_target_pairs={{0,1},{1,0},{2,3},{3,2},{4,5},{5,4},{6,7},{7,6},{8,9},{9,8},{10,11... | collective-permute-start | bytes 786440 | tf_op jit(solution)/shard_map/ppermute | solution.py:190
  24.3 5.5 %collective-permute-start.10 = (bf16[8,4096]{1,0:T(8,128)(2,1)S(1)}, bf16[8,4096]{1,0:T(8,128)(2,1)S(1)}, u32[]{:S(2)}, u32[]{:S(2)}) collective-permute-start(bf16[8,4096]{1,0:T(8,128)(2,1)S(1)} %get-tuple-element.76), channel_id=1, source_target_pairs={{0,6},{1,7},{2,4},{3,5},{4,2},{5,3},{6,0},{7,1},{8,14},{9,15},{10,... | collective-permute-start | bytes 196616 | tf_op jit(solution)/shard_map/ppermute | solution.py:190
  26.4 4.3 %collective-permute-start.9 = (bf16[8,4096]{1,0:T(8,128)(2,1)S(1)}, bf16[8,4096]{1,0:T(8,128)(2,1)S(1)}, u32[]{:S(2)}, u32[]{:S(2)}) collective-permute-start(bf16[8,4096]{1,0:T(8,128)(2,1)S(1)} %get-tuple-element.77), channel_id=1, source_target_pairs={{0,4},{1,5},{2,6},{3,7},{4,0},{5,1},{6,2},{7,3},{8,12},{9,13},{10,... | collective-permute-start | bytes 196616 | tf_op jit(solution)/shard_map/ppermute | solution.py:190
  26.8 4.3 %collective-permute-start.8 = (bf16[8,4096]{1,0:T(8,128)(2,1)S(1)}, bf16[8,4096]{1,0:T(8,128)(2,1)S(1)}, u32[]{:S(2)}, u32[]{:S(2)}) collective-permute-start(bf16[8,4096]{1,0:T(8,128)(2,1)S(1)} %get-tuple-element.78), channel_id=1, source_target_pairs={{0,2},{1,3},{2,0},{3,1},{4,6},{5,7},{6,4},{7,5},{8,10},{9,11},{10,... | collective-permute-start | bytes 196616 | tf_op jit(solution)/shard_map/ppermute | solution.py:190
  27.9 5.8 %collective-permute-start.12 = (bf16[8,2560]{1,0:T(8,128)(2,1)S(1)}, bf16[8,2560]{1,0:T(8,128)(2,1)S(1)}, u32[]{:S(2)}, u32[]{:S(2)}) collective-permute-start(bf16[8,2560]{1,0:T(8,128)(2,1)S(1)} %widen.1), channel_id=1, source_target_pairs={{0,16},{1,17},{2,18},{3,19},{4,20},{5,21},{6,22},{7,23},{8,24},{9,... | collective-permute-start | bytes 122888 | tf_op jit(solution)/shard_map/ppermute | solution.py:190
  31.1 5.8 %collective-permute-start.11 = (bf16[8,2048]{1,0:T(8,128)(2,1)S(1)}, bf16[8,2048]{1,0:T(8,128)(2,1)S(1)}, u32[]{:S(2)}, u32[]{:S(2)}) collective-permute-start(bf16[8,2048]{1,0:T(8,128)(2,1)S(1)} %get-tuple-element.69), channel_id=1, source_target_pairs={{0,24},{1,25},{2,26},{3,27},{4,28},{5,29},{6,30},{7,31},{8,16},{9,... | collective-permute-start | bytes 98312 | tf_op jit(solution)/shard_map/ppermute | solution.py:190

commit v5 on v4

--- a/solution.py
+++ b/solution.py
@@ -409,7 +409,7 @@
     near_ref, next_ref, far_ref, last_ref, router_ref,
     gate_ref, gate_turned_ref, down_ref, down_turned_ref, *refs,
 ):
-    up_refs, up_turned_refs, (kept_ref, sent_ref) = refs[:-2:2], refs[1:-2:2], refs[-2:]
+    up_refs, up_turned_refs, out_refs = refs[:-4:2], refs[1:-4:2], refs[-4:]
     width, hidden_count = gate_ref.shape
     step = 256
     own_expert = lax.axis_index("expert")
@@ -478,8 +478,9 @@
     d_normed = d_normed + jnp.dot(spread_high, router, preferred_element_type=jnp.float32)
     d_normed = d_normed + jnp.dot(spread_low, router, preferred_element_type=jnp.float32)
 
-    quarter = half // 2
-    for ref, rows in ((kept_ref, slice(0, quarter)), (sent_ref, slice(quarter, half))):
+    count = half // len(out_refs)
+    for k, ref in enumerate(out_refs):
+        rows = slice(k * count, (k + 1) * count)
         ref[...] = jnp.concatenate([out_f[rows], d_normed[rows]], axis=1).astype(jnp.bfloat16)
 
 
@@ -487,9 +488,9 @@
     width = router.shape[1]
     return pl.pallas_call(
         expert_kernel,
-        out_shape=[jax.ShapeDtypeStruct((2 * blocks[0].shape[0], 2 * width), jnp.bfloat16)] * 2,
+        out_shape=[jax.ShapeDtypeStruct((b.shape[0], 2 * width), jnp.bfloat16) for b in blocks],
         in_specs=[VMEM] * (1 + len(blocks) + len(weights)),
-        out_specs=[VMEM] * 2,
+        out_specs=[VMEM] * len(blocks),
         compiler_params=pltpu.CompilerParams(vmem_limit_bytes=24 * MIB),
         name="experts",
     )(*blocks, router, *weights)
@@ -550,19 +551,18 @@
     blocks = [early, late, swapped(early, CORE), swapped(late, CORE)]
 
     weights = [m for mats in [gate_mats, down_mats] + ups for m in mats]
-    kept, sent = run_experts(blocks, router_rows, *weights)
-
-    chip = added(kept, swapped(sent, CORE))
-    acts, chip = lax.optimization_barrier((acts, chip))
+    kept = run_experts(blocks, router_rows, *weights)
+    chips = [added(block, swapped(sent, CORE)) for block, sent in zip(kept[:2], kept[2:])]
+    acts, last_chip = lax.optimization_barrier((acts, chips[1]))
+    chips = [chips[0], last_chip]
     real = jax.ShapeDtypeStruct((count, width), jnp.float32)
     wide = jax.ShapeDtypeStruct((count, width + 2 * (width // count)), jnp.bfloat16)
     raw = swapped(in_vmem(widen_kernel, "widen", [wide], acts, gain_row)[0], SECTION)
-    pieces = [chip[:count]]
+    pieces = [chips[0][:count]]
     order = [EARLY] + [i for i in range(len(SQUARE_CHIPS)) if i != EARLY]
-    places = [order.index(i) + 1 for i in range(len(SQUARE_CHIPS))]
-    pieces += [
-        swapped(chip[i * count : (i + 1) * count], *k) for i, k in zip(places, SQUARE_CHIPS)
-    ]
+    for i, distances in enumerate(SQUARE_CHIPS):
+        chip, place = divmod(order.index(i) + 1, 2)
+        pieces.append(swapped(chips[chip][place * count : (place + 1) * count], *distances))
     ending = in_vmem(ending_kernel, "endings", [real] * 4, across, raw)
     small = jax.ShapeDtypeStruct((count, width), jnp.bfloat16)
     leaving, staying = in_vmem(leave_kernel, "leave", [small, real], *pieces)

time: 37.8 us -> 37.7 us (level)
  waiting for transfers between devices: 9 us -> 8.37 us
  starting transfers between devices: 16.8 us -> 17.3 us
    ppermute x13 -> x14, waiting for transfers between devices: 9 us -> 8.37 us  [swapped(): lax.ppermute(block, AXES, [(i, i ^ distances[i & CORE]) for i in range(co...]
    ppermute x13 -> x14, starting transfers between devices: 16.8 us -> 17.3 us  [swapped(): lax.ppermute(block, AXES, [(i, i ^ distances[i & CORE]) for i in range(co...]
  transfers between devices with their start and end apart: 13 -> 14, of which waited for: 9 -> 9; matrix products, arithmetic and copies ran while one was open for 0% -> 0% of each run, Pallas kernels for 16% -> 16%
where the time goes in v5:
time: 37.7 us; the launch traced here: 37.6 us
  starting transfers between devices  17.3 us (46%)
  Pallas kernels  11 us (29%)
  waiting for transfers between devices  8.37 us (22%)
  between operations  0.76 us (2%)
    ppermute x14, starting transfers between devices, swapped(): lax.ppermute(block, AXES, [(i, i ^ distances[i & CORE]) for i in range(co...  17.3 us
    ppermute x14, waiting for transfers between devices, swapped(): lax.ppermute(block, AXES, [(i, i ^ distances[i & CORE]) for i in range(co...  8.37 us
    pallas_call x2, Pallas kernels, fetched(): pl.pallas_call(functools.partial(fetch_kernel, parts=sizes), out_shape=he...  5.99 us
    pallas_call x1, Pallas kernels, run_experts(): pl.pallas_call(expert_kernel, out_shape=[jax.ShapeDtypeStruct((b.shape[0]...  3.04 us
    pallas_call x1, Pallas kernels, pack_rows(): pl.pallas_call(pack_kernel, out_shape=[jax.ShapeDtypeStruct((count, 2 * w...  0.97 us
  transfers between devices with their start and end apart: 14, of which 9 were waited for; matrix products, arithmetic and copies ran while one was open for 0% of the time, Pallas kernels for 16%

profile of v5, /device:TPU:0, one launch (start us, length us, event | category | flops | bytes accessed | tf_op | source)
XLA Modules:
  0.0 37.6 jit_solution(17957939002989423094)
XLA Ops:
  0.6 1.0 %pack.1 = (bf16[8,4224]{1,0:T(8,128)(2,1)S(1)}, bf16[8,4352]{1,0:T(8,128)(2,1)S(1)}, bf16[8,2048]{1,0:T(8,128)(2,1)S(1)}, f32[1,2048]{1,0:T(1,128)S(1)}, bf16[16,2048]{1,0:T(8,128)(2,1)S(1)}) custom-call(bf16[1,8,2048]{2,1,0:T(8,128)(2,1)} %fwd_act.1, s32[1,8,8]{2,1,0:T(8,128)} %fwd_routes.1, bf16[1,8,2048]{2,1,0:T(8,128)(2,1)} %bwd_saved.1, ...), custom_call_target="tpu_custom_call" | custom-call | tf_op jit(solution)/shard_map/pack/pallas_call | solution.py:248
  1.6 4.1 %collective-permute-start = (bf16[8,4352]{1,0:T(8,128)(2,1)S(1)}, bf16[8,4352]{1,0:T(8,128)(2,1)S(1)}, u32[]{:S(2)}, u32[]{:S(2)}) collective-permute-start(bf16[8,4352]{1,0:T(8,128)(2,1)S(1)} %get-tuple-element.41), channel_id=1, source_target_pairs={{0,8},{1,9},{2,10},{3,11},{4,12},{5,13},{6,14},{7,15},{8,0},{9,1},... | collective-permute-start | bytes 208904 | tf_op jit(solution)/shard_map/ppermute | solution.py:190
  5.7 1.5 %collective-permute-start.1 = (bf16[8,4224]{1,0:T(8,128)(2,1)S(1)}, bf16[8,4224]{1,0:T(8,128)(2,1)S(1)}, u32[]{:S(2)}, u32[]{:S(2)}) collective-permute-start(bf16[8,4224]{1,0:T(8,128)(2,1)S(1)} %get-tuple-element.47), channel_id=1, source_target_pairs={{0,16},{1,17},{2,18},{3,19},{4,20},{5,21},{6,22},{7,23},{8,24},{9,... | collective-permute-start | bytes 202760 | tf_op jit(solution)/shard_map/ppermute | solution.py:190
  7.2 3.1 %fetch.2 = (bf16[2048,768]{1,0:T(8,128)(2,1)S(1)}, bf16[1024,768]{1,0:T(8,128)(2,1)S(1)}, bf16[768,2048]{1,0:T(8,128)(2,1)S(1)}, bf16[768,1024]{1,0:T(8,128)(2,1)S(1)}) custom-call(bf16[2048,768]{1,0:T(8,128)(2,1)} %bitcast.6, bf16[2048,768]{1,0:T(8,128)(2,1)} %bitcast.4), custom_call_target="tpu_custom_call" | custom-call | bytes 9437184 | tf_op jit(solution)/shard_map/fetch/pallas_call | solution.py:395
  10.3 0.0 collective-permute-done.1.across_ref
  10.3 0.1 merge.1
  10.4 2.5 %collective-permute-start.2 = (bf16[8,6272]{1,0:T(8,128)(2,1)S(1)}, bf16[8,6272]{1,0:T(8,128)(2,1)S(1)}, u32[]{:S(2)}, u32[]{:S(2)}) collective-permute-start(bf16[8,6272]{1,0:T(8,128)(2,1)S(1)} %merge.1), channel_id=1, source_target_pairs={{0,6},{1,7},{2,4},{3,5},{4,2},{5,3},{6,0},{7,1},{8,14},{9,15},{10,... | collective-permute-start | bytes 301064 | tf_op jit(solution)/shard_map/ppermute | solution.py:190
  12.9 0.4 %collective-permute-start.4 = (bf16[8,6272]{1,0:T(8,128)(2,1)S(1)}, bf16[8,6272]{1,0:T(8,128)(2,1)S(1)}, u32[]{:S(2)}, u32[]{:S(2)}) collective-permute-start(bf16[8,6272]{1,0:T(8,128)(2,1)S(1)} %merge.1), channel_id=1, source_target_pairs={{0,4},{1,5},{2,6},{3,7},{4,0},{5,1},{6,2},{7,3},{8,12},{9,13},{10,... | collective-permute-start | bytes 301064 | tf_op jit(solution)/shard_map/ppermute | solution.py:190
  13.4 0.5 %collective-permute-start.3 = (bf16[8,6272]{1,0:T(8,128)(2,1)S(1)}, bf16[8,6272]{1,0:T(8,128)(2,1)S(1)}, u32[]{:S(2)}, u32[]{:S(2)}) collective-permute-start(bf16[8,6272]{1,0:T(8,128)(2,1)S(1)} %merge.1), channel_id=1, source_target_pairs={{0,2},{1,3},{2,0},{3,1},{4,6},{5,7},{6,4},{7,5},{8,10},{9,11},{10,... | collective-permute-start | bytes 301064 | tf_op jit(solution)/shard_map/ppermute | solution.py:190
  13.9 2.9 %fetch.3 = (bf16[768,2048]{1,0:T(8,128)(2,1)S(1)}, bf16[1024,768]{1,0:T(8,128)(2,1)S(1)}, bf16[2048,768]{1,0:T(8,128)(2,1)S(1)}, bf16[768,1024]{1,0:T(8,128)(2,1)S(1)}) custom-call(bf16[768,2048]{1,0:T(8,128)(2,1)} %bitcast.7, bf16[2048,768]{1,0:T(8,128)(2,1)} %bitcast.5), custom_call_target="tpu_custom_call" | custom-call | bytes 9437184 | tf_op jit(solution)/shard_map/fetch/pallas_call | solution.py:395
  16.8 0.0 collective-permute-done.2
  16.9 0.1 collective-permute-start.5
  16.9 0.8 %collective-permute-done.4 = bf16[8,6272]{1,0:T(8,128)(2,1)S(1)} collective-permute-done((bf16[8,6272]{1,0:T(8,128)(2,1)S(1)}, bf16[8,6272]{1,0:T(8,128)(2,1)S(1)}, u32[]{:S(2)}, u32[]{:S(2)}) %collective-permute-start.4) | collective-permute-done | bytes 100384 | tf_op jit(solution)/shard_map/ppermute | solution.py:190
  17.8 0.3 collective-permute-done.3
  18.1 0.1 collective-permute-start.6
  18.1 0.2 collective-permute-done.5.far_ref
  18.4 1.2 %collective-permute-done.6.last_ref = bf16[16,6272]{1,0:T(8,128)(2,1)S(1)} collective-permute-done((bf16[16,6272]{1,0:T(8,128)(2,1)S(1)}, bf16[16,6272]{1,0:T(8,128)(2,1)S(1)}, u32[]{:S(2)}, u32[]{:S(2)}) %collective-permute-start.6) | collective-permute-done | bytes 200736 | tf_op jit(solution)/shard_map/ppermute | solution.py:190
  19.6 3.0 %experts.1 = (bf16[16,4096]{1,0:T(8,128)(2,1)S(1)}, bf16[16,4096]{1,0:T(8,128)(2,1)S(1)}, bf16[16,4096]{1,0:T(8,128)(2,1)S(1)}, bf16[16,4096]{1,0:T(8,128)(2,1)S(1)}) custom-call(bf16[16,6272]{1,0:T(8,128)(2,1)S(1)} %pad_maximum_fusion.near_ref, bf16[16,6272]{1,0:T(8,128)(2,1)S(1)} %pad_maximum_fusion.1.next_ref, ...), custom_call_target="tpu_custom_call" | custom-call | tf_op jit(solution)/shard_map/experts/pallas_call | solution.py:489
  22.6 0.2 collective-permute-start.7
  22.8 0.4 collective-permute-start.8
  23.2 0.8 %collective-permute-done.7 = bf16[16,4096]{1,0:T(8,128)(2,1)S(1)} collective-permute-done((bf16[16,4096]{1,0:T(8,128)(2,1)S(1)}, bf16[16,4096]{1,0:T(8,128)(2,1)S(1)}, u32[]{:S(2)}, u32[]{:S(2)}) %collective-permute-start.7) | collective-permute-done | bytes 131104 | tf_op jit(solution)/shard_map/ppermute | solution.py:190
  24.1 2.1 %collective-permute-start.11 = (bf16[8,4096]{1,0:T(8,128)(2,1)S(1)}, bf16[8,4096]{1,0:T(8,128)(2,1)S(1)}, u32[]{:S(2)}, u32[]{:S(2)}) collective-permute-start(bf16[8,4096]{1,0:T(8,128)(2,1)S(1)} %get-tuple-element.80), channel_id=1, source_target_pairs={{0,6},{1,7},{2,4},{3,5},{4,2},{5,3},{6,0},{7,1},{8,14},{9,15},{10,... | collective-permute-start | bytes 196616 | tf_op jit(solution)/shard_map/ppermute | solution.py:190
  26.2 0.5 %collective-permute-start.10 = (bf16[8,4096]{1,0:T(8,128)(2,1)S(1)}, bf16[8,4096]{1,0:T(8,128)(2,1)S(1)}, u32[]{:S(2)}, u32[]{:S(2)}) collective-permute-start(bf16[8,4096]{1,0:T(8,128)(2,1)S(1)} %get-tuple-element.82), channel_id=1, source_target_pairs={{0,4},{1,5},{2,6},{3,7},{4,0},{5,1},{6,2},{7,3},{8,12},{9,13},{10,... | collective-permute-start | bytes 196616 | tf_op jit(solution)/shard_map/ppermute | solution.py:190
  26.7 1.0 %collective-permute-start.9 = (bf16[8,4096]{1,0:T(8,128)(2,1)S(1)}, bf16[8,4096]{1,0:T(8,128)(2,1)S(1)}, u32[]{:S(2)}, u32[]{:S(2)}) collective-permute-start(bf16[8,4096]{1,0:T(8,128)(2,1)S(1)} %get-tuple-element.83), channel_id=1, source_target_pairs={{0,2},{1,3},{2,0},{3,1},{4,6},{5,7},{6,4},{7,5},{8,10},{9,11},{10,... | collective-permute-start | bytes 196616 | tf_op jit(solution)/shard_map/ppermute | solution.py:190
  27.8 1.3 %collective-permute-start.13 = (bf16[8,2560]{1,0:T(8,128)(2,1)S(1)}, bf16[8,2560]{1,0:T(8,128)(2,1)S(1)}, u32[]{:S(2)}, u32[]{:S(2)}) collective-permute-start(bf16[8,2560]{1,0:T(8,128)(2,1)S(1)} %widen.1), channel_id=1, source_target_pairs={{0,16},{1,17},{2,18},{3,19},{4,20},{5,21},{6,22},{7,23},{8,24},{9,... | collective-permute-start | bytes 122888 | tf_op jit(solution)/shard_map/ppermute | solution.py:190
  29.0 0.4 %collective-permute-done.11.d_ref = bf16[8,4096]{1,0:T(8,128)(2,1)S(1)} collective-permute-done((bf16[8,4096]{1,0:T(8,128)(2,1)S(1)}, bf16[8,4096]{1,0:T(8,128)(2,1)S(1)}, u32[]{:S(2)}, u32[]{:S(2)}) %collective-permute-start.11) | collective-permute-done | bytes 65568 | tf_op jit(solution)/shard_map/ppermute | solution.py:190
  29.5 1.1 %collective-permute-done.10.c_ref = bf16[8,4096]{1,0:T(8,128)(2,1)S(1)} collective-permute-done((bf16[8,4096]{1,0:T(8,128)(2,1)S(1)}, bf16[8,4096]{1,0:T(8,128)(2,1)S(1)}, u32[]{:S(2)}, u32[]{:S(2)}) %collective-permute-start.10) | collective-permute-done | bytes 65568 | tf_op jit(solution)/shard_map/ppermute | solution.py:190
  30.5 0.5 %collective-permute-done.9.b_ref = bf16[8,4096]{1,0:T(8,128)(2,1)S(1)} collective-permute-done((bf16[8,4096]{1,0:T(8,128)(2,1)S(1)}, bf16[8,4096]{1,0:T(8,128)(2,1)S(1)}, u32[]{:S(2)}, u32[]{:S(2)}) %collective-permute-start.9) | collective-permute-done | bytes 65568 | tf_op jit(solution)/shard_map/ppermute | solution.py:190
  31.1 2.6 %collective-permute-start.12 = (bf16[8,2048]{1,0:T(8,128)(2,1)S(1)}, bf16[8,2048]{1,0:T(8,128)(2,1)S(1)}, u32[]{:S(2)}, u32[]{:S(2)}) collective-permute-start(bf16[8,2048]{1,0:T(8,128)(2,1)S(1)} %get-tuple-element.73), channel_id=1, source_target_pairs={{0,24},{1,25},{2,26},{3,27},{4,28},{5,29},{6,30},{7,31},{8,16},{9,... | collective-permute-start | bytes 98312 | tf_op jit(solution)/shard_map/ppermute | solution.py:190
  33.7 0.1 endings.1
  33.8 3.0 %collective-permute-done.12.other_ref = bf16[8,2048]{1,0:T(8,128)(2,1)S(1)} collective-permute-done((bf16[8,2048]{1,0:T(8,128)(2,1)S(1)}, bf16[8,2048]{1,0:T(8,128)(2,1)S(1)}, u32[]{:S(2)}, u32[]{:S(2)}) %collective-permute-start.12) | collective-permute-done | bytes 32800 | tf_op jit(solution)/shard_map/ppermute | solution.py:190
  36.8 0.7 %finish.1 = (bf16[1,8,2048]{2,1,0:T(8,128)(2,1)}, bf16[1,8,2048]{2,1,0:T(8,128)(2,1)}) custom-call(f32[8,2048]{1,0:T(8,128)S(1)} %get-tuple-element.72.staying_ref, bf16[8,2048]{1,0:T(8,128)(2,1)S(1)} %collective-permute-done.12.other_ref, f32[8,2048]{1,0:T(8,128)S(1)} %get-tuple-element.76.scale_ref, f32[8,2048]{1,0:T(8,128)S(1)} %get-tuple-element.77.towards_ref, ...), custom_call_target="tpu_custom_call" | custom-call | tf_op jit(solution)/shard_map/finish/pallas_call | solution.py:354
  (11 shorter events, 0.2 us)
Async XLA Ops:
  1.6 8.7 %collective-permute-start = (bf16[8,4352]{1,0:T(8,128)(2,1)S(1)}, bf16[8,4352]{1,0:T(8,128)(2,1)S(1)}, u32[]{:S(2)}, u32[]{:S(2)}) collective-permute-start(bf16[8,4352]{1,0:T(8,128)(2,1)S(1)} %get-tuple-element.41), channel_id=1, source_target_pairs={{0,8},{1,9},{2,10},{3,11},{4,12},{5,13},{6,14},{7,15},{8,0},{9,1},... | collective-permute-start | bytes 208904 | tf_op jit(solution)/shard_map/ppermute | solution.py:190
  5.7 4.6 %collective-permute-start.1 = (bf16[8,4224]{1,0:T(8,128)(2,1)S(1)}, bf16[8,4224]{1,0:T(8,128)(2,1)S(1)}, u32[]{:S(2)}, u32[]{:S(2)}) collective-permute-start(bf16[8,4224]{1,0:T(8,128)(2,1)S(1)} %get-tuple-element.47), channel_id=1, source_target_pairs={{0,16},{1,17},{2,18},{3,19},{4,20},{5,21},{6,22},{7,23},{8,24},{9,... | collective-permute-start | bytes 202760 | tf_op jit(solution)/shard_map/ppermute | solution.py:190
  10.4 6.4 %collective-permute-start.2 = (bf16[8,6272]{1,0:T(8,128)(2,1)S(1)}, bf16[8,6272]{1,0:T(8,128)(2,1)S(1)}, u32[]{:S(2)}, u32[]{:S(2)}) collective-permute-start(bf16[8,6272]{1,0:T(8,128)(2,1)S(1)} %merge.1), channel_id=1, source_target_pairs={{0,6},{1,7},{2,4},{3,5},{4,2},{5,3},{6,0},{7,1},{8,14},{9,15},{10,... | collective-permute-start | bytes 301064 | tf_op jit(solution)/shard_map/ppermute | solution.py:190
  12.9 4.8 %collective-permute-start.4 = (bf16[8,6272]{1,0:T(8,128)(2,1)S(1)}, bf16[8,6272]{1,0:T(8,128)(2,1)S(1)}, u32[]{:S(2)}, u32[]{:S(2)}) collective-permute-start(bf16[8,6272]{1,0:T(8,128)(2,1)S(1)} %merge.1), channel_id=1, source_target_pairs={{0,4},{1,5},{2,6},{3,7},{4,0},{5,1},{6,2},{7,3},{8,12},{9,13},{10,... | collective-permute-start | bytes 301064 | tf_op jit(solution)/shard_map/ppermute | solution.py:190
  13.4 4.6 %collective-permute-start.3 = (bf16[8,6272]{1,0:T(8,128)(2,1)S(1)}, bf16[8,6272]{1,0:T(8,128)(2,1)S(1)}, u32[]{:S(2)}, u32[]{:S(2)}) collective-permute-start(bf16[8,6272]{1,0:T(8,128)(2,1)S(1)} %merge.1), channel_id=1, source_target_pairs={{0,2},{1,3},{2,0},{3,1},{4,6},{5,7},{6,4},{7,5},{8,10},{9,11},{10,... | collective-permute-start | bytes 301064 | tf_op jit(solution)/shard_map/ppermute | solution.py:190
  16.9 1.5 %collective-permute-start.5 = (bf16[16,6272]{1,0:T(8,128)(2,1)S(1)}, bf16[16,6272]{1,0:T(8,128)(2,1)S(1)}, u32[]{:S(2)}, u32[]{:S(2)}) collective-permute-start(bf16[16,6272]{1,0:T(8,128)(2,1)S(1)} %pad_maximum_fusion.near_ref), channel_id=1, source_target_pairs={{0,1},{1,0},{2,3},{3,2},{4,5},{5,4},{6,7},{7,6},{8,9},{9,8},{10,11... | collective-permute-start | bytes 602120 | tf_op jit(solution)/shard_map/ppermute | solution.py:190
  18.1 1.5 %collective-permute-start.6 = (bf16[16,6272]{1,0:T(8,128)(2,1)S(1)}, bf16[16,6272]{1,0:T(8,128)(2,1)S(1)}, u32[]{:S(2)}, u32[]{:S(2)}) collective-permute-start(bf16[16,6272]{1,0:T(8,128)(2,1)S(1)} %pad_maximum_fusion.1.next_ref), channel_id=1, source_target_pairs={{0,1},{1,0},{2,3},{3,2},{4,5},{5,4},{6,7},{7,6},{8,9},{9,8},{10,11... | collective-permute-start | bytes 602120 | tf_op jit(solution)/shard_map/ppermute | solution.py:190
  22.6 1.4 %collective-permute-start.7 = (bf16[16,4096]{1,0:T(8,128)(2,1)S(1)}, bf16[16,4096]{1,0:T(8,128)(2,1)S(1)}, u32[]{:S(2)}, u32[]{:S(2)}) collective-permute-start(bf16[16,4096]{1,0:T(8,128)(2,1)S(1)} %get-tuple-element.67), channel_id=1, source_target_pairs={{0,1},{1,0},{2,3},{3,2},{4,5},{5,4},{6,7},{7,6},{8,9},{9,8},{10,11... | collective-permute-start | bytes 393224 | tf_op jit(solution)/shard_map/ppermute | solution.py:190
  22.8 3.3 %collective-permute-start.8 = (bf16[16,4096]{1,0:T(8,128)(2,1)S(1)}, bf16[16,4096]{1,0:T(8,128)(2,1)S(1)}, u32[]{:S(2)}, u32[]{:S(2)}) collective-permute-start(bf16[16,4096]{1,0:T(8,128)(2,1)S(1)} %get-tuple-element.70), channel_id=1, source_target_pairs={{0,1},{1,0},{2,3},{3,2},{4,5},{5,4},{6,7},{7,6},{8,9},{9,8},{10,11... | collective-permute-start | bytes 393224 | tf_op jit(solution)/shard_map/ppermute | solution.py:190
  24.1 5.4 %collective-permute-start.11 = (bf16[8,4096]{1,0:T(8,128)(2,1)S(1)}, bf16[8,4096]{1,0:T(8,128)(2,1)S(1)}, u32[]{:S(2)}, u32[]{:S(2)}) collective-permute-start(bf16[8,4096]{1,0:T(8,128)(2,1)S(1)} %get-tuple-element.80), channel_id=1, source_target_pairs={{0,6},{1,7},{2,4},{3,5},{4,2},{5,3},{6,0},{7,1},{8,14},{9,15},{10,... | collective-permute-start | bytes 196616 | tf_op jit(solution)/shard_map/ppermute | solution.py:190
  26.2 4.3 %collective-permute-start.10 = (bf16[8,4096]{1,0:T(8,128)(2,1)S(1)}, bf16[8,4096]{1,0:T(8,128)(2,1)S(1)}, u32[]{:S(2)}, u32[]{:S(2)}) collective-permute-start(bf16[8,4096]{1,0:T(8,128)(2,1)S(1)} %get-tuple-element.82), channel_id=1, source_target_pairs={{0,4},{1,5},{2,6},{3,7},{4,0},{5,1},{6,2},{7,3},{8,12},{9,13},{10,... | collective-permute-start | bytes 196616 | tf_op jit(solution)/shard_map/ppermute | solution.py:190
  26.7 4.3 %collective-permute-start.9 = (bf16[8,4096]{1,0:T(8,128)(2,1)S(1)}, bf16[8,4096]{1,0:T(8,128)(2,1)S(1)}, u32[]{:S(2)}, u32[]{:S(2)}) collective-permute-start(bf16[8,4096]{1,0:T(8,128)(2,1)S(1)} %get-tuple-element.83), channel_id=1, source_target_pairs={{0,2},{1,3},{2,0},{3,1},{4,6},{5,7},{6,4},{7,5},{8,10},{9,11},{10,... | collective-permute-start | bytes 196616 | tf_op jit(solution)/shard_map/ppermute | solution.py:190
  27.8 5.9 %collective-permute-start.13 = (bf16[8,2560]{1,0:T(8,128)(2,1)S(1)}, bf16[8,2560]{1,0:T(8,128)(2,1)S(1)}, u32[]{:S(2)}, u32[]{:S(2)}) collective-permute-start(bf16[8,2560]{1,0:T(8,128)(2,1)S(1)} %widen.1), channel_id=1, source_target_pairs={{0,16},{1,17},{2,18},{3,19},{4,20},{5,21},{6,22},{7,23},{8,24},{9,... | collective-permute-start | bytes 122888 | tf_op jit(solution)/shard_map/ppermute | solution.py:190
  31.1 5.8 %collective-permute-start.12 = (bf16[8,2048]{1,0:T(8,128)(2,1)S(1)}, bf16[8,2048]{1,0:T(8,128)(2,1)S(1)}, u32[]{:S(2)}, u32[]{:S(2)}) collective-permute-start(bf16[8,2048]{1,0:T(8,128)(2,1)S(1)} %get-tuple-element.73), channel_id=1, source_target_pairs={{0,24},{1,25},{2,26},{3,27},{4,28},{5,29},{6,30},{7,31},{8,16},{9,... | collective-permute-start | bytes 98312 | tf_op jit(solution)/shard_map/ppermute | solution.py:190

commit v6 on v5

--- a/solution.py
+++ b/solution.py
@@ -173,10 +173,10 @@
 
 AXES = ("section", "expert")
 SQUARE = 8
-CORE, HALF, SECTION = 1, 8, 16
+CORE, HALF, SECTION = 1, 9, 16
 EARLY = 2
 LANES = 128
-SQUARE_CHIPS = ((2, 2), (4, 4), (6, 6))
+SQUARE_CHIPS = (3, 5, 7)
 TOP_COUNT = 8
 VMEM = pl.BlockSpec(memory_space=pltpu.VMEM)
 SMEM = pl.BlockSpec(memory_space=pltpu.SMEM)
@@ -184,10 +184,9 @@
 MIB = 1024 * 1024
 
 
-def swapped(block, even, odd=None):
-    distances = (even, even if odd is None else odd)
+def swapped(block, distance):
     count = lax.axis_size(AXES)
-    return lax.ppermute(block, AXES, [(i, i ^ distances[i & CORE]) for i in range(count)])
+    return lax.ppermute(block, AXES, [(i, i ^ distance) for i in range(count)])
 
 
 def in_hbm(array):
@@ -231,8 +230,14 @@
     pltpu.make_async_copy(fwd_routes.at[0], routes_ref, sems.at[3]).wait()
     grad_copy.wait()
     routes = routes_ref[...].astype(jnp.float32)
+    blank = jnp.zeros_like(routes)
     routes = jnp.concatenate(
-        [routes, jnp.zeros((routes.shape[0], LANES - TOP_COUNT), jnp.float32)], axis=1
+        [
+            jnp.where(first_section, routes, blank),
+            jnp.where(first_section, blank, routes),
+            jnp.zeros((routes.shape[0], LANES - 2 * TOP_COUNT), jnp.float32),
+        ],
+        axis=1,
     )
     rows = jnp.concatenate(
         [normed, grads_ref[...].astype(jnp.float32), routes], axis=1
@@ -292,19 +297,23 @@
 
 
 def merge_kernel(along_ref, across_ref, mine_ref):
+    width = (across_ref.shape[1] - LANES) // 2
     first_section = in_first_section()
-    used = across_ref.shape[1]
-    width = (used - LANES) // 2
-    along = along_ref[...].astype(jnp.float32)[:, :used]
-    across = across_ref[...].astype(jnp.float32)
-    forward = jnp.where(first_section, along, across)
-    backward = jnp.where(first_section, across, along)
-    routes = jnp.concatenate(
-        [forward[:, 2 * width : 2 * width + TOP_COUNT], backward[:, 2 * width : -TOP_COUNT]], axis=1
-    )
-    mine_ref[...] = jnp.concatenate(
-        [forward[:, :width], backward[:, : 2 * width], routes], axis=1
-    ).astype(jnp.bfloat16)
+
+    def merge(forward_ref, backward_ref):
+        mine_ref[:, :width] = forward_ref[:, :width]
+        mine_ref[:, width : 3 * width] = backward_ref[:, : 2 * width]
+
+    @pl.when(first_section)
+    def _():
+        merge(along_ref, across_ref)
+
+    @pl.when(jnp.logical_not(first_section))
+    def _():
+        merge(across_ref, along_ref)
+
+    tail = slice(2 * width, 2 * width + LANES)
+    mine_ref[:, 3 * width :] = along_ref[:, tail] + across_ref[:, tail]
 
 
 def leave_kernel(a_ref, b_ref, c_ref, d_ref, leaving_ref, staying_ref):
@@ -475,8 +484,11 @@
     spread = gate_b * dgate * (own[half:] - gates[half:])
     spread_high = spread.astype(jnp.bfloat16)
     spread_low = (spread - spread_high.astype(jnp.float32)).astype(jnp.bfloat16)
-    d_normed = d_normed + jnp.dot(spread_high, router, preferred_element_type=jnp.float32)
-    d_normed = d_normed + jnp.dot(spread_low, router, preferred_element_type=jnp.float32)
+    d_normed = d_normed + jnp.dot(
+        jnp.concatenate([spread_high, spread_low], axis=1),
+        jnp.concatenate([router, router], axis=0),
+        preferred_element_type=jnp.float32,
+    )
 
     count = half // len(out_refs)
     for k, ref in enumerate(out_refs):
@@ -544,7 +556,7 @@
         (down_hbm, 0, down_hbm.shape[0]), (up_hbm, cuts[0], cuts[1] - cuts[0])
     )
     ups = ups + more
-    received = [swapped(mine, *k) for k in SQUARE_CHIPS]
+    received = [swapped(mine, k) for k in SQUARE_CHIPS]
     early = jnp.concatenate([mine, received[EARLY]], axis=0)
     late = jnp.concatenate([b for i, b in enumerate(received) if i != EARLY], axis=0)
     late, ups, down_mats = lax.optimization_barrier((late, ups, down_mats))
@@ -560,9 +572,9 @@
     raw = swapped(in_vmem(widen_kernel, "widen", [wide], acts, gain_row)[0], SECTION)
     pieces = [chips[0][:count]]
     order = [EARLY] + [i for i in range(len(SQUARE_CHIPS)) if i != EARLY]
-    for i, distances in enumerate(SQUARE_CHIPS):
+    for i, distance in enumerate(SQUARE_CHIPS):
         chip, place = divmod(order.index(i) + 1, 2)
-        pieces.append(swapped(chips[chip][place * count : (place + 1) * count], *distances))
+        pieces.append(swapped(chips[chip][place * count : (place + 1) * count], distance))
     ending = in_vmem(ending_kernel, "endings", [real] * 4, across, raw)
     small = jax.ShapeDtypeStruct((count, width), jnp.bfloat16)
     leaving, staying = in_vmem(leave_kernel, "leave", [small, real], *pieces)

time: 37.7 us -> 37.2 us (0.987)
  waiting for transfers between devices: 8.37 us -> 7.81 us
    ppermute x14, waiting for transfers between devices: 8.37 us -> 7.81 us  [swapped(): return lax.ppermute(block, AXES, [(i, i ^ distance) for i in range(count)])]
  transfers between devices with their start and end apart: 14 -> 14, of which waited for: 9 -> 9; matrix products, arithmetic and copies ran while one was open for 0% -> 0% of each run, Pallas kernels for 16% -> 17%
where the time goes in v6:
time: 37.2 us; the launch traced here: 37 us
  starting transfers between devices  17.5 us (47%)
  Pallas kernels  10.9 us (29%)
  waiting for transfers between devices  7.81 us (21%)
  between operations  0.74 us (2%)
    ppermute x14, starting transfers between devices, swapped(): return lax.ppermute(block, AXES, [(i, i ^ distance) for i in range(count)])  17.5 us
    ppermute x14, waiting for transfers between devices, swapped(): return lax.ppermute(block, AXES, [(i, i ^ distance) for i in range(count)])  7.81 us
    pallas_call x2, Pallas kernels, fetched(): pl.pallas_call(functools.partial(fetch_kernel, parts=sizes), out_shape=he...  5.99 us
    pallas_call x1, Pallas kernels, run_experts(): pl.pallas_call(expert_kernel, out_shape=[jax.ShapeDtypeStruct((b.shape[0]...  2.98 us
    pallas_call x1, Pallas kernels, pack_rows(): pl.pallas_call(pack_kernel, out_shape=[jax.ShapeDtypeStruct((count, 2 * w...  1 us
  transfers between devices with their start and end apart: 14, of which 9 were waited for; matrix products, arithmetic and copies ran while one was open for 0% of the time, Pallas kernels for 17%

profile of v6, /device:TPU:0, one launch (start us, length us, event | category | flops | bytes accessed | tf_op | source)
XLA Modules:
  0.0 37.0 jit_solution(10323246471963619098)
XLA Ops:
  0.6 1.0 %pack.1 = (bf16[8,4224]{1,0:T(8,128)(2,1)S(1)}, bf16[8,4352]{1,0:T(8,128)(2,1)S(1)}, bf16[8,2048]{1,0:T(8,128)(2,1)S(1)}, f32[1,2048]{1,0:T(1,128)S(1)}, bf16[16,2048]{1,0:T(8,128)(2,1)S(1)}) custom-call(bf16[1,8,2048]{2,1,0:T(8,128)(2,1)} %fwd_act.1, s32[1,8,8]{2,1,0:T(8,128)} %fwd_routes.1, bf16[1,8,2048]{2,1,0:T(8,128)(2,1)} %bwd_saved.1, ...), custom_call_target="tpu_custom_call" | custom-call | tf_op jit(solution)/shard_map/pack/pallas_call | solution.py:253
  1.6 3.5 %collective-permute-start = (bf16[8,4352]{1,0:T(8,128)(2,1)S(1)}, bf16[8,4352]{1,0:T(8,128)(2,1)S(1)}, u32[]{:S(2)}, u32[]{:S(2)}) collective-permute-start(bf16[8,4352]{1,0:T(8,128)(2,1)S(1)} %get-tuple-element.41), channel_id=1, source_target_pairs={{0,9},{1,8},{2,11},{3,10},{4,13},{5,12},{6,15},{7,14},{8,1},{9,0},... | collective-permute-start | bytes 208904 | tf_op jit(solution)/shard_map/ppermute | solution.py:189
  5.2 1.5 %collective-permute-start.1 = (bf16[8,4224]{1,0:T(8,128)(2,1)S(1)}, bf16[8,4224]{1,0:T(8,128)(2,1)S(1)}, u32[]{:S(2)}, u32[]{:S(2)}) collective-permute-start(bf16[8,4224]{1,0:T(8,128)(2,1)S(1)} %get-tuple-element.47), channel_id=1, source_target_pairs={{0,16},{1,17},{2,18},{3,19},{4,20},{5,21},{6,22},{7,23},{8,24},{9,... | collective-permute-start | bytes 202760 | tf_op jit(solution)/shard_map/ppermute | solution.py:189
  6.7 3.1 %fetch.2 = (bf16[2048,768]{1,0:T(8,128)(2,1)S(1)}, bf16[1024,768]{1,0:T(8,128)(2,1)S(1)}, bf16[768,2048]{1,0:T(8,128)(2,1)S(1)}, bf16[768,1024]{1,0:T(8,128)(2,1)S(1)}) custom-call(bf16[2048,768]{1,0:T(8,128)(2,1)} %bitcast.6, bf16[2048,768]{1,0:T(8,128)(2,1)} %bitcast.4), custom_call_target="tpu_custom_call" | custom-call | bytes 9437184 | tf_op jit(solution)/shard_map/fetch/pallas_call | solution.py:404
  9.8 0.0 collective-permute-done.along_ref
  9.8 0.1 collective-permute-done.1.across_ref
  9.9 2.5 %collective-permute-start.2 = (bf16[8,6272]{1,0:T(8,128)(2,1)S(1)}, bf16[8,6272]{1,0:T(8,128)(2,1)S(1)}, u32[]{:S(2)}, u32[]{:S(2)}) collective-permute-start(bf16[8,6272]{1,0:T(8,128)(2,1)S(1)} %merge.1), channel_id=1, source_target_pairs={{0,7},{1,6},{2,5},{3,4},{4,3},{5,2},{6,1},{7,0},{8,15},{9,14},{10,... | collective-permute-start | bytes 301064 | tf_op jit(solution)/shard_map/ppermute | solution.py:189
  12.4 0.3 collective-permute-start.4
  12.7 0.4 %collective-permute-start.3 = (bf16[8,6272]{1,0:T(8,128)(2,1)S(1)}, bf16[8,6272]{1,0:T(8,128)(2,1)S(1)}, u32[]{:S(2)}, u32[]{:S(2)}) collective-permute-start(bf16[8,6272]{1,0:T(8,128)(2,1)S(1)} %merge.1), channel_id=1, source_target_pairs={{0,3},{1,2},{2,1},{3,0},{4,7},{5,6},{6,5},{7,4},{8,11},{9,10},{10,... | collective-permute-start | bytes 301064 | tf_op jit(solution)/shard_map/ppermute | solution.py:189
  13.1 2.9 %fetch.3 = (bf16[768,2048]{1,0:T(8,128)(2,1)S(1)}, bf16[1024,768]{1,0:T(8,128)(2,1)S(1)}, bf16[2048,768]{1,0:T(8,128)(2,1)S(1)}, bf16[768,1024]{1,0:T(8,128)(2,1)S(1)}) custom-call(bf16[768,2048]{1,0:T(8,128)(2,1)} %bitcast.7, bf16[2048,768]{1,0:T(8,128)(2,1)} %bitcast.5), custom_call_target="tpu_custom_call" | custom-call | bytes 9437184 | tf_op jit(solution)/shard_map/fetch/pallas_call | solution.py:404
  16.0 0.0 collective-permute-done.2
  16.0 0.3 collective-permute-start.5
  16.3 1.5 %collective-permute-done.4 = bf16[8,6272]{1,0:T(8,128)(2,1)S(1)} collective-permute-done((bf16[8,6272]{1,0:T(8,128)(2,1)S(1)}, bf16[8,6272]{1,0:T(8,128)(2,1)S(1)}, u32[]{:S(2)}, u32[]{:S(2)}) %collective-permute-start.4) | collective-permute-done | bytes 100384 | tf_op jit(solution)/shard_map/ppermute | solution.py:189
  17.8 0.1 collective-permute-done.3
  18.0 0.2 collective-permute-start.6
  18.2 0.0 collective-permute-done.5.far_ref
  18.2 1.3 %collective-permute-done.6.last_ref = bf16[16,6272]{1,0:T(8,128)(2,1)S(1)} collective-permute-done((bf16[16,6272]{1,0:T(8,128)(2,1)S(1)}, bf16[16,6272]{1,0:T(8,128)(2,1)S(1)}, u32[]{:S(2)}, u32[]{:S(2)}) %collective-permute-start.6) | collective-permute-done | bytes 200736 | tf_op jit(solution)/shard_map/ppermute | solution.py:189
  19.5 3.0 %experts.1 = (bf16[16,4096]{1,0:T(8,128)(2,1)S(1)}, bf16[16,4096]{1,0:T(8,128)(2,1)S(1)}, bf16[16,4096]{1,0:T(8,128)(2,1)S(1)}, bf16[16,4096]{1,0:T(8,128)(2,1)S(1)}) custom-call(bf16[16,6272]{1,0:T(8,128)(2,1)S(1)} %pad_maximum_fusion.near_ref, bf16[16,6272]{1,0:T(8,128)(2,1)S(1)} %pad_maximum_fusion.1.next_ref, ...), custom_call_target="tpu_custom_call" | custom-call | tf_op jit(solution)/shard_map/experts/pallas_call | solution.py:501
  22.5 0.2 collective-permute-start.7
  22.7 0.4 collective-permute-start.8
  23.0 0.8 %collective-permute-done.7 = bf16[16,4096]{1,0:T(8,128)(2,1)S(1)} collective-permute-done((bf16[16,4096]{1,0:T(8,128)(2,1)S(1)}, bf16[16,4096]{1,0:T(8,128)(2,1)S(1)}, u32[]{:S(2)}, u32[]{:S(2)}) %collective-permute-start.7) | collective-permute-done | bytes 131104 | tf_op jit(solution)/shard_map/ppermute | solution.py:189
  23.9 2.5 %collective-permute-start.11 = (bf16[8,4096]{1,0:T(8,128)(2,1)S(1)}, bf16[8,4096]{1,0:T(8,128)(2,1)S(1)}, u32[]{:S(2)}, u32[]{:S(2)}) collective-permute-start(bf16[8,4096]{1,0:T(8,128)(2,1)S(1)} %get-tuple-element.80), channel_id=1, source_target_pairs={{0,7},{1,6},{2,5},{3,4},{4,3},{5,2},{6,1},{7,0},{8,15},{9,14},{10,... | collective-permute-start | bytes 196616 | tf_op jit(solution)/shard_map/ppermute | solution.py:189
  26.5 0.5 %collective-permute-start.10 = (bf16[8,4096]{1,0:T(8,128)(2,1)S(1)}, bf16[8,4096]{1,0:T(8,128)(2,1)S(1)}, u32[]{:S(2)}, u32[]{:S(2)}) collective-permute-start(bf16[8,4096]{1,0:T(8,128)(2,1)S(1)} %get-tuple-element.82), channel_id=1, source_target_pairs={{0,5},{1,4},{2,7},{3,6},{4,1},{5,0},{6,3},{7,2},{8,13},{9,12},{10,... | collective-permute-start | bytes 196616 | tf_op jit(solution)/shard_map/ppermute | solution.py:189
  27.0 0.2 collective-permute-start.9
  27.2 1.7 %collective-permute-start.13 = (bf16[8,2560]{1,0:T(8,128)(2,1)S(1)}, bf16[8,2560]{1,0:T(8,128)(2,1)S(1)}, u32[]{:S(2)}, u32[]{:S(2)}) collective-permute-start(bf16[8,2560]{1,0:T(8,128)(2,1)S(1)} %widen.1), channel_id=1, source_target_pairs={{0,16},{1,17},{2,18},{3,19},{4,20},{5,21},{6,22},{7,23},{8,24},{9,... | collective-permute-start | bytes 122888 | tf_op jit(solution)/shard_map/ppermute | solution.py:189
  28.9 0.1 collective-permute-done.11.d_ref
  29.0 1.5 %collective-permute-done.10.c_ref = bf16[8,4096]{1,0:T(8,128)(2,1)S(1)} collective-permute-done((bf16[8,4096]{1,0:T(8,128)(2,1)S(1)}, bf16[8,4096]{1,0:T(8,128)(2,1)S(1)}, u32[]{:S(2)}, u32[]{:S(2)}) %collective-permute-start.10) | collective-permute-done | bytes 65568 | tf_op jit(solution)/shard_map/ppermute | solution.py:189
  30.5 0.5 %collective-permute-done.9.b_ref = bf16[8,4096]{1,0:T(8,128)(2,1)S(1)} collective-permute-done((bf16[8,4096]{1,0:T(8,128)(2,1)S(1)}, bf16[8,4096]{1,0:T(8,128)(2,1)S(1)}, u32[]{:S(2)}, u32[]{:S(2)}) %collective-permute-start.9) | collective-permute-done | bytes 65568 | tf_op jit(solution)/shard_map/ppermute | solution.py:189
  31.1 3.4 %collective-permute-start.12 = (bf16[8,2048]{1,0:T(8,128)(2,1)S(1)}, bf16[8,2048]{1,0:T(8,128)(2,1)S(1)}, u32[]{:S(2)}, u32[]{:S(2)}) collective-permute-start(bf16[8,2048]{1,0:T(8,128)(2,1)S(1)} %get-tuple-element.73), channel_id=1, source_target_pairs={{0,25},{1,24},{2,27},{3,26},{4,29},{5,28},{6,31},{7,30},{8,17},{9,... | collective-permute-start | bytes 98312 | tf_op jit(solution)/shard_map/ppermute | solution.py:189
  34.5 0.1 endings.1
  34.6 1.7 %collective-permute-done.12.other_ref = bf16[8,2048]{1,0:T(8,128)(2,1)S(1)} collective-permute-done((bf16[8,2048]{1,0:T(8,128)(2,1)S(1)}, bf16[8,2048]{1,0:T(8,128)(2,1)S(1)}, u32[]{:S(2)}, u32[]{:S(2)}) %collective-permute-start.12) | collective-permute-done | bytes 32800 | tf_op jit(solution)/shard_map/ppermute | solution.py:189
  36.3 0.7 %finish.1 = (bf16[1,8,2048]{2,1,0:T(8,128)(2,1)}, bf16[1,8,2048]{2,1,0:T(8,128)(2,1)}) custom-call(f32[8,2048]{1,0:T(8,128)S(1)} %get-tuple-element.72.staying_ref, bf16[8,2048]{1,0:T(8,128)(2,1)S(1)} %collective-permute-done.12.other_ref, f32[8,2048]{1,0:T(8,128)S(1)} %get-tuple-element.76.scale_ref, f32[8,2048]{1,0:T(8,128)S(1)} %get-tuple-element.77.towards_ref, ...), custom_call_target="tpu_custom_call" | custom-call | tf_op jit(solution)/shard_map/finish/pallas_call | solution.py:363
  (11 shorter events, 0.2 us)
Async XLA Ops:
  1.6 8.1 %collective-permute-start = (bf16[8,4352]{1,0:T(8,128)(2,1)S(1)}, bf16[8,4352]{1,0:T(8,128)(2,1)S(1)}, u32[]{:S(2)}, u32[]{:S(2)}) collective-permute-start(bf16[8,4352]{1,0:T(8,128)(2,1)S(1)} %get-tuple-element.41), channel_id=1, source_target_pairs={{0,9},{1,8},{2,11},{3,10},{4,13},{5,12},{6,15},{7,14},{8,1},{9,0},... | collective-permute-start | bytes 208904 | tf_op jit(solution)/shard_map/ppermute | solution.py:189
  5.2 4.7 %collective-permute-start.1 = (bf16[8,4224]{1,0:T(8,128)(2,1)S(1)}, bf16[8,4224]{1,0:T(8,128)(2,1)S(1)}, u32[]{:S(2)}, u32[]{:S(2)}) collective-permute-start(bf16[8,4224]{1,0:T(8,128)(2,1)S(1)} %get-tuple-element.47), channel_id=1, source_target_pairs={{0,16},{1,17},{2,18},{3,19},{4,20},{5,21},{6,22},{7,23},{8,24},{9,... | collective-permute-start | bytes 202760 | tf_op jit(solution)/shard_map/ppermute | solution.py:189
  9.9 6.1 %collective-permute-start.2 = (bf16[8,6272]{1,0:T(8,128)(2,1)S(1)}, bf16[8,6272]{1,0:T(8,128)(2,1)S(1)}, u32[]{:S(2)}, u32[]{:S(2)}) collective-permute-start(bf16[8,6272]{1,0:T(8,128)(2,1)S(1)} %merge.1), channel_id=1, source_target_pairs={{0,7},{1,6},{2,5},{3,4},{4,3},{5,2},{6,1},{7,0},{8,15},{9,14},{10,... | collective-permute-start | bytes 301064 | tf_op jit(solution)/shard_map/ppermute | solution.py:189
  12.4 5.4 %collective-permute-start.4 = (bf16[8,6272]{1,0:T(8,128)(2,1)S(1)}, bf16[8,6272]{1,0:T(8,128)(2,1)S(1)}, u32[]{:S(2)}, u32[]{:S(2)}) collective-permute-start(bf16[8,6272]{1,0:T(8,128)(2,1)S(1)} %merge.1), channel_id=1, source_target_pairs={{0,5},{1,4},{2,7},{3,6},{4,1},{5,0},{6,3},{7,2},{8,13},{9,12},{10,... | collective-permute-start | bytes 301064 | tf_op jit(solution)/shard_map/ppermute | solution.py:189
  12.7 5.3 %collective-permute-start.3 = (bf16[8,6272]{1,0:T(8,128)(2,1)S(1)}, bf16[8,6272]{1,0:T(8,128)(2,1)S(1)}, u32[]{:S(2)}, u32[]{:S(2)}) collective-permute-start(bf16[8,6272]{1,0:T(8,128)(2,1)S(1)} %merge.1), channel_id=1, source_target_pairs={{0,3},{1,2},{2,1},{3,0},{4,7},{5,6},{6,5},{7,4},{8,11},{9,10},{10,... | collective-permute-start | bytes 301064 | tf_op jit(solution)/shard_map/ppermute | solution.py:189
  16.0 2.1 %collective-permute-start.5 = (bf16[16,6272]{1,0:T(8,128)(2,1)S(1)}, bf16[16,6272]{1,0:T(8,128)(2,1)S(1)}, u32[]{:S(2)}, u32[]{:S(2)}) collective-permute-start(bf16[16,6272]{1,0:T(8,128)(2,1)S(1)} %pad_maximum_fusion.near_ref), channel_id=1, source_target_pairs={{0,1},{1,0},{2,3},{3,2},{4,5},{5,4},{6,7},{7,6},{8,9},{9,8},{10,11... | collective-permute-start | bytes 602120 | tf_op jit(solution)/shard_map/ppermute | solution.py:189
  18.0 1.5 %collective-permute-start.6 = (bf16[16,6272]{1,0:T(8,128)(2,1)S(1)}, bf16[16,6272]{1,0:T(8,128)(2,1)S(1)}, u32[]{:S(2)}, u32[]{:S(2)}) collective-permute-start(bf16[16,6272]{1,0:T(8,128)(2,1)S(1)} %pad_maximum_fusion.1.next_ref), channel_id=1, source_target_pairs={{0,1},{1,0},{2,3},{3,2},{4,5},{5,4},{6,7},{7,6},{8,9},{9,8},{10,11... | collective-permute-start | bytes 602120 | tf_op jit(solution)/shard_map/ppermute | solution.py:189
  22.5 1.4 %collective-permute-start.7 = (bf16[16,4096]{1,0:T(8,128)(2,1)S(1)}, bf16[16,4096]{1,0:T(8,128)(2,1)S(1)}, u32[]{:S(2)}, u32[]{:S(2)}) collective-permute-start(bf16[16,4096]{1,0:T(8,128)(2,1)S(1)} %get-tuple-element.67), channel_id=1, source_target_pairs={{0,1},{1,0},{2,3},{3,2},{4,5},{5,4},{6,7},{7,6},{8,9},{9,8},{10,11... | collective-permute-start | bytes 393224 | tf_op jit(solution)/shard_map/ppermute | solution.py:189
  22.7 3.8 %collective-permute-start.8 = (bf16[16,4096]{1,0:T(8,128)(2,1)S(1)}, bf16[16,4096]{1,0:T(8,128)(2,1)S(1)}, u32[]{:S(2)}, u32[]{:S(2)}) collective-permute-start(bf16[16,4096]{1,0:T(8,128)(2,1)S(1)} %get-tuple-element.70), channel_id=1, source_target_pairs={{0,1},{1,0},{2,3},{3,2},{4,5},{5,4},{6,7},{7,6},{8,9},{9,8},{10,11... | collective-permute-start | bytes 393224 | tf_op jit(solution)/shard_map/ppermute | solution.py:189
  23.9 5.1 %collective-permute-start.11 = (bf16[8,4096]{1,0:T(8,128)(2,1)S(1)}, bf16[8,4096]{1,0:T(8,128)(2,1)S(1)}, u32[]{:S(2)}, u32[]{:S(2)}) collective-permute-start(bf16[8,4096]{1,0:T(8,128)(2,1)S(1)} %get-tuple-element.80), channel_id=1, source_target_pairs={{0,7},{1,6},{2,5},{3,4},{4,3},{5,2},{6,1},{7,0},{8,15},{9,14},{10,... | collective-permute-start | bytes 196616 | tf_op jit(solution)/shard_map/ppermute | solution.py:189
  26.5 4.0 %collective-permute-start.10 = (bf16[8,4096]{1,0:T(8,128)(2,1)S(1)}, bf16[8,4096]{1,0:T(8,128)(2,1)S(1)}, u32[]{:S(2)}, u32[]{:S(2)}) collective-permute-start(bf16[8,4096]{1,0:T(8,128)(2,1)S(1)} %get-tuple-element.82), channel_id=1, source_target_pairs={{0,5},{1,4},{2,7},{3,6},{4,1},{5,0},{6,3},{7,2},{8,13},{9,12},{10,... | collective-permute-start | bytes 196616 | tf_op jit(solution)/shard_map/ppermute | solution.py:189
  27.0 4.0 %collective-permute-start.9 = (bf16[8,4096]{1,0:T(8,128)(2,1)S(1)}, bf16[8,4096]{1,0:T(8,128)(2,1)S(1)}, u32[]{:S(2)}, u32[]{:S(2)}) collective-permute-start(bf16[8,4096]{1,0:T(8,128)(2,1)S(1)} %get-tuple-element.83), channel_id=1, source_target_pairs={{0,3},{1,2},{2,1},{3,0},{4,7},{5,6},{6,5},{7,4},{8,11},{9,10},{10,... | collective-permute-start | bytes 196616 | tf_op jit(solution)/shard_map/ppermute | solution.py:189
  27.2 7.3 %collective-permute-start.13 = (bf16[8,2560]{1,0:T(8,128)(2,1)S(1)}, bf16[8,2560]{1,0:T(8,128)(2,1)S(1)}, u32[]{:S(2)}, u32[]{:S(2)}) collective-permute-start(bf16[8,2560]{1,0:T(8,128)(2,1)S(1)} %widen.1), channel_id=1, source_target_pairs={{0,16},{1,17},{2,18},{3,19},{4,20},{5,21},{6,22},{7,23},{8,24},{9,... | collective-permute-start | bytes 122888 | tf_op jit(solution)/shard_map/ppermute | solution.py:189
  31.1 5.2 %collective-permute-start.12 = (bf16[8,2048]{1,0:T(8,128)(2,1)S(1)}, bf16[8,2048]{1,0:T(8,128)(2,1)S(1)}, u32[]{:S(2)}, u32[]{:S(2)}) collective-permute-start(bf16[8,2048]{1,0:T(8,128)(2,1)S(1)} %get-tuple-element.73), channel_id=1, source_target_pairs={{0,25},{1,24},{2,27},{3,26},{4,29},{5,28},{6,31},{7,30},{8,17},{9,... | collective-permute-start | bytes 98312 | tf_op jit(solution)/shard_map/ppermute | solution.py:189

commit v7 on v6

--- a/solution.py
+++ b/solution.py
@@ -203,7 +203,7 @@
 
 def pack_kernel(
     fwd_act, fwd_routes, bwd_saved, bwd_grad, bwd_routes, gain, router,
-    across_ref, along_ref, acts_ref, gain_ref, router_ref, grads_ref, routes_ref, sems,
+    rows_ref, acts_ref, gain_ref, router_ref, grads_ref, routes_ref, sems,
 ):
     first_section = in_first_section()
     grad_copy = pltpu.make_async_copy(bwd_grad.at[0], grads_ref, sems.at[0])
@@ -239,11 +239,9 @@
         ],
         axis=1,
     )
-    rows = jnp.concatenate(
+    rows_ref[...] = jnp.concatenate(
         [normed, grads_ref[...].astype(jnp.float32), routes], axis=1
     ).astype(jnp.bfloat16)
-    across_ref[...] = rows
-    along_ref[...] = jnp.concatenate([rows, rows[:, -LANES:]], axis=1)
     router_copy.wait()
 
 
@@ -254,13 +252,12 @@
         pack_kernel,
         out_shape=[
             jax.ShapeDtypeStruct((count, 2 * width + LANES), jnp.bfloat16),
-            jax.ShapeDtypeStruct((count, 2 * width + 2 * LANES), jnp.bfloat16),
             jax.ShapeDtypeStruct((count, width), jnp.bfloat16),
             jax.ShapeDtypeStruct(gain.shape, gain.dtype),
             jax.ShapeDtypeStruct(router.shape, router.dtype),
         ],
         in_specs=[HBM] * 7,
-        out_specs=[VMEM] * 5,
+        out_specs=[VMEM] * 4,
         scratch_shapes=[
             pltpu.VMEM((count, width), jnp.bfloat16),
             pltpu.VMEM(fwd_routes.shape[1:], jnp.int32),
@@ -540,11 +537,11 @@
     fwd_act, fwd_routes, bwd_saved, bwd_grad, bwd_routes, norm_gain, router, w_gate, w_up, w_down
 ):
     count, width = fwd_act.shape[1:]
-    across, along, acts, gain_row, router_rows = pack_rows(
+    own, acts, gain_row, router_rows = pack_rows(
         fwd_act, fwd_routes, bwd_saved, bwd_grad, bwd_routes, norm_gain, router.T
     )
-    across = swapped(across, SECTION)
-    along = swapped(along, HALF)
+    across = swapped(own, SECTION)
+    along = swapped(own, HALF)
     cuts = (width // 2, width)
     gate_hbm, up_hbm, down_hbm = w_gate[0], w_up[0], w_down[0]
     gate_mats, *ups = fetched((gate_hbm, 0, width), (up_hbm, 0, cuts[0]))
@@ -559,8 +556,9 @@
     received = [swapped(mine, k) for k in SQUARE_CHIPS]
     early = jnp.concatenate([mine, received[EARLY]], axis=0)
     late = jnp.concatenate([b for i, b in enumerate(received) if i != EARLY], axis=0)
-    late, ups, down_mats = lax.optimization_barrier((late, ups, down_mats))
-    blocks = [early, late, swapped(early, CORE), swapped(late, CORE)]
+    early, ups, down_mats = lax.optimization_barrier((early, ups, down_mats))
+    last = [swapped(b, CORE) for i, b in enumerate(received) if i != EARLY]
+    blocks = [early, late, swapped(early, CORE), jnp.concatenate(last, axis=0)]
 
     weights = [m for mats in [gate_mats, down_mats] + ups for m in mats]
     kept = run_experts(blocks, router_rows, *weights)

time: 37.2 us -> 37 us (level)
  waiting for transfers between devices: 7.81 us -> 7.15 us
  starting transfers between devices: 17.5 us -> 17.9 us
    ppermute x14 -> x15, waiting for transfers between devices: 7.81 us -> 7.15 us  [swapped(): return lax.ppermute(block, AXES, [(i, i ^ distance) for i in range(count)])]
    ppermute x14 -> x15, starting transfers between devices: 17.5 us -> 17.9 us  [swapped(): return lax.ppermute(block, AXES, [(i, i ^ distance) for i in range(count)])]
  transfers between devices with their start and end apart: 14 -> 15, of which waited for: 9 -> 8; matrix products, arithmetic and copies ran while one was open for 0% -> 0% of each run, Pallas kernels for 17% -> 17%
where the time goes in v7:
time: 37 us; the launch traced here: 36.8 us
  starting transfers between devices  17.9 us (48%)
  Pallas kernels  10.9 us (29%)
  waiting for transfers between devices  7.15 us (19%)
  between operations  0.75 us (2%)
    ppermute x15, starting transfers between devices, swapped(): return lax.ppermute(block, AXES, [(i, i ^ distance) for i in range(count)])  17.9 us
    ppermute x15, waiting for transfers between devices, swapped(): return lax.ppermute(block, AXES, [(i, i ^ distance) for i in range(count)])  7.15 us
    pallas_call x2, Pallas kernels, fetched(): pl.pallas_call(functools.partial(fetch_kernel, parts=sizes), out_shape=he...  5.99 us
    pallas_call x1, Pallas kernels, run_experts(): pl.pallas_call(expert_kernel, out_shape=[jax.ShapeDtypeStruct((b.shape[0]...  2.98 us
    pallas_call x1, Pallas kernels, pack_rows(): pl.pallas_call(pack_kernel, out_shape=[jax.ShapeDtypeStruct((count, 2 * w...  1 us
  transfers between devices with their start and end apart: 15, of which 8 were waited for; matrix products, arithmetic and copies ran while one was open for 0% of the time, Pallas kernels for 17%

profile of v7, /device:TPU:0, one launch (start us, length us, event | category | flops | bytes accessed | tf_op | source)
XLA Modules:
  0.0 36.8 jit_solution(5828569676388196839)
XLA Ops:
  0.6 1.0 %pack.1 = (bf16[8,4224]{1,0:T(8,128)(2,1)S(1)}, bf16[8,2048]{1,0:T(8,128)(2,1)S(1)}, f32[1,2048]{1,0:T(1,128)S(1)}, bf16[16,2048]{1,0:T(8,128)(2,1)S(1)}) custom-call(bf16[1,8,2048]{2,1,0:T(8,128)(2,1)} %fwd_act.1, s32[1,8,8]{2,1,0:T(8,128)} %fwd_routes.1, bf16[1,8,2048]{2,1,0:T(8,128)(2,1)} %bwd_saved.1, bf16[1,8,2048]{2,1,0:T(8,128)(2,1)} %bwd_grad.1, ...), custom_call_target="tpu_custom_call" | custom-call | tf_op jit(solution)/shard_map/pack/pallas_call | solution.py:251
  1.6 3.5 %collective-permute-start = (bf16[8,4224]{1,0:T(8,128)(2,1)S(1)}, bf16[8,4224]{1,0:T(8,128)(2,1)S(1)}, u32[]{:S(2)}, u32[]{:S(2)}) collective-permute-start(bf16[8,4224]{1,0:T(8,128)(2,1)S(1)} %get-tuple-element.40), channel_id=1, source_target_pairs={{0,9},{1,8},{2,11},{3,10},{4,13},{5,12},{6,15},{7,14},{8,1},{9,0},... | collective-permute-start | bytes 202760 | tf_op jit(solution)/shard_map/ppermute | solution.py:189
  5.2 1.5 %collective-permute-start.1 = (bf16[8,4224]{1,0:T(8,128)(2,1)S(1)}, bf16[8,4224]{1,0:T(8,128)(2,1)S(1)}, u32[]{:S(2)}, u32[]{:S(2)}) collective-permute-start(bf16[8,4224]{1,0:T(8,128)(2,1)S(1)} %get-tuple-element.40), channel_id=1, source_target_pairs={{0,16},{1,17},{2,18},{3,19},{4,20},{5,21},{6,22},{7,23},{8,24},{9,... | collective-permute-start | bytes 202760 | tf_op jit(solution)/shard_map/ppermute | solution.py:189
  6.7 3.1 %fetch.2 = (bf16[2048,768]{1,0:T(8,128)(2,1)S(1)}, bf16[1024,768]{1,0:T(8,128)(2,1)S(1)}, bf16[768,2048]{1,0:T(8,128)(2,1)S(1)}, bf16[768,1024]{1,0:T(8,128)(2,1)S(1)}) custom-call(bf16[2048,768]{1,0:T(8,128)(2,1)} %bitcast.6, bf16[2048,768]{1,0:T(8,128)(2,1)} %bitcast.4), custom_call_target="tpu_custom_call" | custom-call | bytes 9437184 | tf_op jit(solution)/shard_map/fetch/pallas_call | solution.py:401
  9.8 0.1 collective-permute-done.1.across_ref
  9.9 2.5 %collective-permute-start.2 = (bf16[8,6272]{1,0:T(8,128)(2,1)S(1)}, bf16[8,6272]{1,0:T(8,128)(2,1)S(1)}, u32[]{:S(2)}, u32[]{:S(2)}) collective-permute-start(bf16[8,6272]{1,0:T(8,128)(2,1)S(1)} %merge.1), channel_id=1, source_target_pairs={{0,7},{1,6},{2,5},{3,4},{4,3},{5,2},{6,1},{7,0},{8,15},{9,14},{10,... | collective-permute-start | bytes 301064 | tf_op jit(solution)/shard_map/ppermute | solution.py:189
  12.4 0.3 collective-permute-start.4
  12.7 0.4 %collective-permute-start.3 = (bf16[8,6272]{1,0:T(8,128)(2,1)S(1)}, bf16[8,6272]{1,0:T(8,128)(2,1)S(1)}, u32[]{:S(2)}, u32[]{:S(2)}) collective-permute-start(bf16[8,6272]{1,0:T(8,128)(2,1)S(1)} %merge.1), channel_id=1, source_target_pairs={{0,3},{1,2},{2,1},{3,0},{4,7},{5,6},{6,5},{7,4},{8,11},{9,10},{10,... | collective-permute-start | bytes 301064 | tf_op jit(solution)/shard_map/ppermute | solution.py:189
  13.1 2.9 %fetch.3 = (bf16[768,2048]{1,0:T(8,128)(2,1)S(1)}, bf16[1024,768]{1,0:T(8,128)(2,1)S(1)}, bf16[2048,768]{1,0:T(8,128)(2,1)S(1)}, bf16[768,1024]{1,0:T(8,128)(2,1)S(1)}) custom-call(bf16[768,2048]{1,0:T(8,128)(2,1)} %bitcast.7, bf16[2048,768]{1,0:T(8,128)(2,1)} %bitcast.5), custom_call_target="tpu_custom_call" | custom-call | bytes 9437184 | tf_op jit(solution)/shard_map/fetch/pallas_call | solution.py:401
  16.0 0.0 collective-permute-done.2
  16.0 0.3 collective-permute-start.5
  16.3 1.5 %collective-permute-done.4 = bf16[8,6272]{1,0:T(8,128)(2,1)S(1)} collective-permute-done((bf16[8,6272]{1,0:T(8,128)(2,1)S(1)}, bf16[8,6272]{1,0:T(8,128)(2,1)S(1)}, u32[]{:S(2)}, u32[]{:S(2)}) %collective-permute-start.4) | collective-permute-done | bytes 100384 | tf_op jit(solution)/shard_map/ppermute | solution.py:189
  17.8 0.2 collective-permute-start.7
  18.1 0.3 collective-permute-start.6
  18.4 0.8 %collective-permute-done.7 = bf16[8,6272]{1,0:T(8,128)(2,1)S(1)} collective-permute-done((bf16[8,6272]{1,0:T(8,128)(2,1)S(1)}, bf16[8,6272]{1,0:T(8,128)(2,1)S(1)}, u32[]{:S(2)}, u32[]{:S(2)}) %collective-permute-start.7) | collective-permute-done | bytes 100384 | tf_op jit(solution)/shard_map/ppermute | solution.py:189
  19.1 0.2 collective-permute-done.6
  19.4 0.0 collective-permute-done.5.far_ref
  19.4 3.0 %experts.1 = (bf16[16,4096]{1,0:T(8,128)(2,1)S(1)}, bf16[16,4096]{1,0:T(8,128)(2,1)S(1)}, bf16[16,4096]{1,0:T(8,128)(2,1)S(1)}, bf16[16,4096]{1,0:T(8,128)(2,1)S(1)}) custom-call(bf16[16,6272]{1,0:T(8,128)(2,1)S(1)} %pad_maximum_fusion.near_ref, bf16[16,6272]{1,0:T(8,128)(2,1)S(1)} %pad_maximum_fusion.1.next_ref, ...), custom_call_target="tpu_custom_call" | custom-call | tf_op jit(solution)/shard_map/experts/pallas_call | solution.py:498
  22.4 0.3 collective-permute-start.8
  22.7 0.2 collective-permute-start.9
  23.0 0.8 %collective-permute-done.8 = bf16[16,4096]{1,0:T(8,128)(2,1)S(1)} collective-permute-done((bf16[16,4096]{1,0:T(8,128)(2,1)S(1)}, bf16[16,4096]{1,0:T(8,128)(2,1)S(1)}, u32[]{:S(2)}, u32[]{:S(2)}) %collective-permute-start.8) | collective-permute-done | bytes 131104 | tf_op jit(solution)/shard_map/ppermute | solution.py:189
  23.9 2.4 %collective-permute-start.12 = (bf16[8,4096]{1,0:T(8,128)(2,1)S(1)}, bf16[8,4096]{1,0:T(8,128)(2,1)S(1)}, u32[]{:S(2)}, u32[]{:S(2)}) collective-permute-start(bf16[8,4096]{1,0:T(8,128)(2,1)S(1)} %get-tuple-element.78), channel_id=1, source_target_pairs={{0,7},{1,6},{2,5},{3,4},{4,3},{5,2},{6,1},{7,0},{8,15},{9,14},{10,... | collective-permute-start | bytes 196616 | tf_op jit(solution)/shard_map/ppermute | solution.py:189
  26.3 0.0 collective-permute-done.9
  26.3 0.5 %collective-permute-start.11 = (bf16[8,4096]{1,0:T(8,128)(2,1)S(1)}, bf16[8,4096]{1,0:T(8,128)(2,1)S(1)}, u32[]{:S(2)}, u32[]{:S(2)}) collective-permute-start(bf16[8,4096]{1,0:T(8,128)(2,1)S(1)} %get-tuple-element.80), channel_id=1, source_target_pairs={{0,5},{1,4},{2,7},{3,6},{4,1},{5,0},{6,3},{7,2},{8,13},{9,12},{10,... | collective-permute-start | bytes 196616 | tf_op jit(solution)/shard_map/ppermute | solution.py:189
  26.8 0.3 collective-permute-start.10
  27.1 1.9 %collective-permute-start.14 = (bf16[8,2560]{1,0:T(8,128)(2,1)S(1)}, bf16[8,2560]{1,0:T(8,128)(2,1)S(1)}, u32[]{:S(2)}, u32[]{:S(2)}) collective-permute-start(bf16[8,2560]{1,0:T(8,128)(2,1)S(1)} %widen.1), channel_id=1, source_target_pairs={{0,16},{1,17},{2,18},{3,19},{4,20},{5,21},{6,22},{7,23},{8,24},{9,... | collective-permute-start | bytes 122888 | tf_op jit(solution)/shard_map/ppermute | solution.py:189
  29.0 1.3 %collective-permute-done.11.c_ref = bf16[8,4096]{1,0:T(8,128)(2,1)S(1)} collective-permute-done((bf16[8,4096]{1,0:T(8,128)(2,1)S(1)}, bf16[8,4096]{1,0:T(8,128)(2,1)S(1)}, u32[]{:S(2)}, u32[]{:S(2)}) %collective-permute-start.11) | collective-permute-done | bytes 65568 | tf_op jit(solution)/shard_map/ppermute | solution.py:189
  30.3 0.5 %collective-permute-done.10.b_ref = bf16[8,4096]{1,0:T(8,128)(2,1)S(1)} collective-permute-done((bf16[8,4096]{1,0:T(8,128)(2,1)S(1)}, bf16[8,4096]{1,0:T(8,128)(2,1)S(1)}, u32[]{:S(2)}, u32[]{:S(2)}) %collective-permute-start.10) | collective-permute-done | bytes 65568 | tf_op jit(solution)/shard_map/ppermute | solution.py:189
  30.9 3.3 %collective-permute-start.13 = (bf16[8,2048]{1,0:T(8,128)(2,1)S(1)}, bf16[8,2048]{1,0:T(8,128)(2,1)S(1)}, u32[]{:S(2)}, u32[]{:S(2)}) collective-permute-start(bf16[8,2048]{1,0:T(8,128)(2,1)S(1)} %get-tuple-element.71), channel_id=1, source_target_pairs={{0,25},{1,24},{2,27},{3,26},{4,29},{5,28},{6,31},{7,30},{8,17},{9,... | collective-permute-start | bytes 98312 | tf_op jit(solution)/shard_map/ppermute | solution.py:189
  34.2 0.1 endings.1
  34.3 1.8 %collective-permute-done.13.other_ref = bf16[8,2048]{1,0:T(8,128)(2,1)S(1)} collective-permute-done((bf16[8,2048]{1,0:T(8,128)(2,1)S(1)}, bf16[8,2048]{1,0:T(8,128)(2,1)S(1)}, u32[]{:S(2)}, u32[]{:S(2)}) %collective-permute-start.13) | collective-permute-done | bytes 32800 | tf_op jit(solution)/shard_map/ppermute | solution.py:189
  36.1 0.7 %finish.1 = (bf16[1,8,2048]{2,1,0:T(8,128)(2,1)}, bf16[1,8,2048]{2,1,0:T(8,128)(2,1)}) custom-call(f32[8,2048]{1,0:T(8,128)S(1)} %get-tuple-element.70.staying_ref, bf16[8,2048]{1,0:T(8,128)(2,1)S(1)} %collective-permute-done.13.other_ref, f32[8,2048]{1,0:T(8,128)S(1)} %get-tuple-element.74.scale_ref, f32[8,2048]{1,0:T(8,128)S(1)} %get-tuple-element.75.towards_ref, ...), custom_call_target="tpu_custom_call" | custom-call | tf_op jit(solution)/shard_map/finish/pallas_call | solution.py:360
  (14 shorter events, 0.2 us)
Async XLA Ops:
  1.6 8.1 %collective-permute-start = (bf16[8,4224]{1,0:T(8,128)(2,1)S(1)}, bf16[8,4224]{1,0:T(8,128)(2,1)S(1)}, u32[]{:S(2)}, u32[]{:S(2)}) collective-permute-start(bf16[8,4224]{1,0:T(8,128)(2,1)S(1)} %get-tuple-element.40), channel_id=1, source_target_pairs={{0,9},{1,8},{2,11},{3,10},{4,13},{5,12},{6,15},{7,14},{8,1},{9,0},... | collective-permute-start | bytes 202760 | tf_op jit(solution)/shard_map/ppermute | solution.py:189
  5.2 4.7 %collective-permute-start.1 = (bf16[8,4224]{1,0:T(8,128)(2,1)S(1)}, bf16[8,4224]{1,0:T(8,128)(2,1)S(1)}, u32[]{:S(2)}, u32[]{:S(2)}) collective-permute-start(bf16[8,4224]{1,0:T(8,128)(2,1)S(1)} %get-tuple-element.40), channel_id=1, source_target_pairs={{0,16},{1,17},{2,18},{3,19},{4,20},{5,21},{6,22},{7,23},{8,24},{9,... | collective-permute-start | bytes 202760 | tf_op jit(solution)/shard_map/ppermute | solution.py:189
  9.9 6.1 %collective-permute-start.2 = (bf16[8,6272]{1,0:T(8,128)(2,1)S(1)}, bf16[8,6272]{1,0:T(8,128)(2,1)S(1)}, u32[]{:S(2)}, u32[]{:S(2)}) collective-permute-start(bf16[8,6272]{1,0:T(8,128)(2,1)S(1)} %merge.1), channel_id=1, source_target_pairs={{0,7},{1,6},{2,5},{3,4},{4,3},{5,2},{6,1},{7,0},{8,15},{9,14},{10,... | collective-permute-start | bytes 301064 | tf_op jit(solution)/shard_map/ppermute | solution.py:189
  12.4 5.4 %collective-permute-start.4 = (bf16[8,6272]{1,0:T(8,128)(2,1)S(1)}, bf16[8,6272]{1,0:T(8,128)(2,1)S(1)}, u32[]{:S(2)}, u32[]{:S(2)}) collective-permute-start(bf16[8,6272]{1,0:T(8,128)(2,1)S(1)} %merge.1), channel_id=1, source_target_pairs={{0,5},{1,4},{2,7},{3,6},{4,1},{5,0},{6,3},{7,2},{8,13},{9,12},{10,... | collective-permute-start | bytes 301064 | tf_op jit(solution)/shard_map/ppermute | solution.py:189
  12.7 5.4 %collective-permute-start.3 = (bf16[8,6272]{1,0:T(8,128)(2,1)S(1)}, bf16[8,6272]{1,0:T(8,128)(2,1)S(1)}, u32[]{:S(2)}, u32[]{:S(2)}) collective-permute-start(bf16[8,6272]{1,0:T(8,128)(2,1)S(1)} %merge.1), channel_id=1, source_target_pairs={{0,3},{1,2},{2,1},{3,0},{4,7},{5,6},{6,5},{7,4},{8,11},{9,10},{10,... | collective-permute-start | bytes 301064 | tf_op jit(solution)/shard_map/ppermute | solution.py:189
  16.0 3.4 %collective-permute-start.5 = (bf16[16,6272]{1,0:T(8,128)(2,1)S(1)}, bf16[16,6272]{1,0:T(8,128)(2,1)S(1)}, u32[]{:S(2)}, u32[]{:S(2)}) collective-permute-start(bf16[16,6272]{1,0:T(8,128)(2,1)S(1)} %pad_maximum_fusion.near_ref), channel_id=1, source_target_pairs={{0,1},{1,0},{2,3},{3,2},{4,5},{5,4},{6,7},{7,6},{8,9},{9,8},{10,11... | collective-permute-start | bytes 602120 | tf_op jit(solution)/shard_map/ppermute | solution.py:189
  17.8 1.3 %collective-permute-start.7 = (bf16[8,6272]{1,0:T(8,128)(2,1)S(1)}, bf16[8,6272]{1,0:T(8,128)(2,1)S(1)}, u32[]{:S(2)}, u32[]{:S(2)}) collective-permute-start(bf16[8,6272]{1,0:T(8,128)(2,1)S(1)} %collective-permute-done.4), channel_id=1, source_target_pairs={{0,1},{1,0},{2,3},{3,2},{4,5},{5,4},{6,7},{7,6},{8,9},{9,8},{10,11... | collective-permute-start | bytes 301064 | tf_op jit(solution)/shard_map/ppermute | solution.py:189
  18.1 1.3 %collective-permute-start.6 = (bf16[8,6272]{1,0:T(8,128)(2,1)S(1)}, bf16[8,6272]{1,0:T(8,128)(2,1)S(1)}, u32[]{:S(2)}, u32[]{:S(2)}) collective-permute-start(bf16[8,6272]{1,0:T(8,128)(2,1)S(1)} %collective-permute-done.3), channel_id=1, source_target_pairs={{0,1},{1,0},{2,3},{3,2},{4,5},{5,4},{6,7},{7,6},{8,9},{9,8},{10,11... | collective-permute-start | bytes 301064 | tf_op jit(solution)/shard_map/ppermute | solution.py:189
  22.4 1.4 %collective-permute-start.8 = (bf16[16,4096]{1,0:T(8,128)(2,1)S(1)}, bf16[16,4096]{1,0:T(8,128)(2,1)S(1)}, u32[]{:S(2)}, u32[]{:S(2)}) collective-permute-start(bf16[16,4096]{1,0:T(8,128)(2,1)S(1)} %get-tuple-element.65), channel_id=1, source_target_pairs={{0,1},{1,0},{2,3},{3,2},{4,5},{5,4},{6,7},{7,6},{8,9},{9,8},{10,11... | collective-permute-start | bytes 393224 | tf_op jit(solution)/shard_map/ppermute | solution.py:189
  22.7 3.5 %collective-permute-start.9 = (bf16[16,4096]{1,0:T(8,128)(2,1)S(1)}, bf16[16,4096]{1,0:T(8,128)(2,1)S(1)}, u32[]{:S(2)}, u32[]{:S(2)}) collective-permute-start(bf16[16,4096]{1,0:T(8,128)(2,1)S(1)} %get-tuple-element.68), channel_id=1, source_target_pairs={{0,1},{1,0},{2,3},{3,2},{4,5},{5,4},{6,7},{7,6},{8,9},{9,8},{10,11... | collective-permute-start | bytes 393224 | tf_op jit(solution)/shard_map/ppermute | solution.py:189
  23.9 5.2 %collective-permute-start.12 = (bf16[8,4096]{1,0:T(8,128)(2,1)S(1)}, bf16[8,4096]{1,0:T(8,128)(2,1)S(1)}, u32[]{:S(2)}, u32[]{:S(2)}) collective-permute-start(bf16[8,4096]{1,0:T(8,128)(2,1)S(1)} %get-tuple-element.78), channel_id=1, source_target_pairs={{0,7},{1,6},{2,5},{3,4},{4,3},{5,2},{6,1},{7,0},{8,15},{9,14},{10,... | collective-permute-start | bytes 196616 | tf_op jit(solution)/shard_map/ppermute | solution.py:189
  26.3 4.0 %collective-permute-start.11 = (bf16[8,4096]{1,0:T(8,128)(2,1)S(1)}, bf16[8,4096]{1,0:T(8,128)(2,1)S(1)}, u32[]{:S(2)}, u32[]{:S(2)}) collective-permute-start(bf16[8,4096]{1,0:T(8,128)(2,1)S(1)} %get-tuple-element.80), channel_id=1, source_target_pairs={{0,5},{1,4},{2,7},{3,6},{4,1},{5,0},{6,3},{7,2},{8,13},{9,12},{10,... | collective-permute-start | bytes 196616 | tf_op jit(solution)/shard_map/ppermute | solution.py:189
  26.8 4.0 %collective-permute-start.10 = (bf16[8,4096]{1,0:T(8,128)(2,1)S(1)}, bf16[8,4096]{1,0:T(8,128)(2,1)S(1)}, u32[]{:S(2)}, u32[]{:S(2)}) collective-permute-start(bf16[8,4096]{1,0:T(8,128)(2,1)S(1)} %get-tuple-element.81), channel_id=1, source_target_pairs={{0,3},{1,2},{2,1},{3,0},{4,7},{5,6},{6,5},{7,4},{8,11},{9,10},{10,... | collective-permute-start | bytes 196616 | tf_op jit(solution)/shard_map/ppermute | solution.py:189
  27.1 7.0 %collective-permute-start.14 = (bf16[8,2560]{1,0:T(8,128)(2,1)S(1)}, bf16[8,2560]{1,0:T(8,128)(2,1)S(1)}, u32[]{:S(2)}, u32[]{:S(2)}) collective-permute-start(bf16[8,2560]{1,0:T(8,128)(2,1)S(1)} %widen.1), channel_id=1, source_target_pairs={{0,16},{1,17},{2,18},{3,19},{4,20},{5,21},{6,22},{7,23},{8,24},{9,... | collective-permute-start | bytes 122888 | tf_op jit(solution)/shard_map/ppermute | solution.py:189
  30.9 5.2 %collective-permute-start.13 = (bf16[8,2048]{1,0:T(8,128)(2,1)S(1)}, bf16[8,2048]{1,0:T(8,128)(2,1)S(1)}, u32[]{:S(2)}, u32[]{:S(2)}) collective-permute-start(bf16[8,2048]{1,0:T(8,128)(2,1)S(1)} %get-tuple-element.71), channel_id=1, source_target_pairs={{0,25},{1,24},{2,27},{3,26},{4,29},{5,28},{6,31},{7,30},{8,17},{9,... | collective-permute-start | bytes 98312 | tf_op jit(solution)/shard_map/ppermute | solution.py:189

commit v8 on v7

--- a/solution.py
+++ b/solution.py
@@ -469,28 +469,29 @@
     hidden = jnp.concatenate(hiddens, axis=1)
     d_pre = jnp.concatenate(d_pres, axis=1)
     d_up = jnp.concatenate(d_ups, axis=1)
-    out_f = jnp.dot(hidden, down_ref[...], preferred_element_type=jnp.float32)
-    d_normed = jnp.concatenate(
-        [
-            jnp.dot(d_up, mat[...], preferred_element_type=jnp.float32)
-            for mat in up_turned_refs
-        ],
-        axis=1,
-    )
-    d_normed = d_normed + jnp.dot(d_pre, gate_turned_ref[...], preferred_element_type=jnp.float32)
     spread = gate_b * dgate * (own[half:] - gates[half:])
     spread_high = spread.astype(jnp.bfloat16)
     spread_low = (spread - spread_high.astype(jnp.float32)).astype(jnp.bfloat16)
-    d_normed = d_normed + jnp.dot(
-        jnp.concatenate([spread_high, spread_low], axis=1),
-        jnp.concatenate([router, router], axis=0),
-        preferred_element_type=jnp.float32,
-    )
-
+    spread = jnp.concatenate([spread_high, spread_low], axis=1)
+    routers = jnp.concatenate([router, router], axis=0)
     count = half // len(out_refs)
-    for k, ref in enumerate(out_refs):
-        rows = slice(k * count, (k + 1) * count)
-        ref[...] = jnp.concatenate([out_f[rows], d_normed[rows]], axis=1).astype(jnp.bfloat16)
+    start = 0
+    for turned in up_turned_refs:
+        span = turned.shape[1]
+        cols = slice(start, start + span)
+        out_f = jnp.dot(hidden, down_ref[:, cols], preferred_element_type=jnp.float32)
+        d_normed = jnp.dot(d_up, turned[...], preferred_element_type=jnp.float32)
+        d_normed = d_normed + jnp.dot(
+            d_pre, gate_turned_ref[:, cols], preferred_element_type=jnp.float32
+        )
+        d_normed = d_normed + jnp.dot(
+            spread, routers[:, cols], preferred_element_type=jnp.float32
+        )
+        for k, ref in enumerate(out_refs):
+            rows = slice(k * count, (k + 1) * count)
+            ref[:, cols] = out_f[rows].astype(jnp.bfloat16)
+            ref[:, width + start : width + start + span] = d_normed[rows].astype(jnp.bfloat16)
+        start += span
 
 
 def run_experts(blocks, router, *weights):

time: 37 us -> 37 us (level)
  no operation moved by 1% of the time
where the time goes in v8:
time: 37 us; the launch traced here: 36.8 us
  starting transfers between devices  17.9 us (48%)
  Pallas kernels  10.9 us (29%)
  waiting for transfers between devices  7.15 us (19%)
  between operations  0.75 us (2%)
    ppermute x15, starting transfers between devices, swapped(): return lax.ppermute(block, AXES, [(i, i ^ distance) for i in range(count)])  17.9 us
    ppermute x15, waiting for transfers between devices, swapped(): return lax.ppermute(block, AXES, [(i, i ^ distance) for i in range(count)])  7.15 us
    pallas_call x2, Pallas kernels, fetched(): pl.pallas_call(functools.partial(fetch_kernel, parts=sizes), out_shape=he...  5.99 us
    pallas_call x1, Pallas kernels, run_experts(): pl.pallas_call(expert_kernel, out_shape=[jax.ShapeDtypeStruct((b.shape[0]...  2.99 us
    pallas_call x1, Pallas kernels, pack_rows(): pl.pallas_call(pack_kernel, out_shape=[jax.ShapeDtypeStruct((count, 2 * w...  1 us
  transfers between devices with their start and end apart: 15, of which 8 were waited for; matrix products, arithmetic and copies ran while one was open for 0% of the time, Pallas kernels for 17%

profile of v8, /device:TPU:0, one launch (start us, length us, event | category | flops | bytes accessed | tf_op | source)
XLA Modules:
  0.0 36.8 jit_solution(14027590307572962171)
XLA Ops:
  0.6 1.0 %pack.1 = (bf16[8,4224]{1,0:T(8,128)(2,1)S(1)}, bf16[8,2048]{1,0:T(8,128)(2,1)S(1)}, f32[1,2048]{1,0:T(1,128)S(1)}, bf16[16,2048]{1,0:T(8,128)(2,1)S(1)}) custom-call(bf16[1,8,2048]{2,1,0:T(8,128)(2,1)} %fwd_act.1, s32[1,8,8]{2,1,0:T(8,128)} %fwd_routes.1, bf16[1,8,2048]{2,1,0:T(8,128)(2,1)} %bwd_saved.1, bf16[1,8,2048]{2,1,0:T(8,128)(2,1)} %bwd_grad.1, ...), custom_call_target="tpu_custom_call" | custom-call | tf_op jit(solution)/shard_map/pack/pallas_call | solution.py:251
  1.6 3.5 %collective-permute-start = (bf16[8,4224]{1,0:T(8,128)(2,1)S(1)}, bf16[8,4224]{1,0:T(8,128)(2,1)S(1)}, u32[]{:S(2)}, u32[]{:S(2)}) collective-permute-start(bf16[8,4224]{1,0:T(8,128)(2,1)S(1)} %get-tuple-element.40), channel_id=1, source_target_pairs={{0,9},{1,8},{2,11},{3,10},{4,13},{5,12},{6,15},{7,14},{8,1},{9,0},... | collective-permute-start | bytes 202760 | tf_op jit(solution)/shard_map/ppermute | solution.py:189
  5.2 1.5 %collective-permute-start.1 = (bf16[8,4224]{1,0:T(8,128)(2,1)S(1)}, bf16[8,4224]{1,0:T(8,128)(2,1)S(1)}, u32[]{:S(2)}, u32[]{:S(2)}) collective-permute-start(bf16[8,4224]{1,0:T(8,128)(2,1)S(1)} %get-tuple-element.40), channel_id=1, source_target_pairs={{0,16},{1,17},{2,18},{3,19},{4,20},{5,21},{6,22},{7,23},{8,24},{9,... | collective-permute-start | bytes 202760 | tf_op jit(solution)/shard_map/ppermute | solution.py:189
  6.7 3.1 %fetch.2 = (bf16[2048,768]{1,0:T(8,128)(2,1)S(1)}, bf16[1024,768]{1,0:T(8,128)(2,1)S(1)}, bf16[768,2048]{1,0:T(8,128)(2,1)S(1)}, bf16[768,1024]{1,0:T(8,128)(2,1)S(1)}) custom-call(bf16[2048,768]{1,0:T(8,128)(2,1)} %bitcast.6, bf16[2048,768]{1,0:T(8,128)(2,1)} %bitcast.4), custom_call_target="tpu_custom_call" | custom-call | bytes 9437184 | tf_op jit(solution)/shard_map/fetch/pallas_call | solution.py:401
  9.8 0.1 collective-permute-done.1.across_ref
  9.9 2.5 %collective-permute-start.2 = (bf16[8,6272]{1,0:T(8,128)(2,1)S(1)}, bf16[8,6272]{1,0:T(8,128)(2,1)S(1)}, u32[]{:S(2)}, u32[]{:S(2)}) collective-permute-start(bf16[8,6272]{1,0:T(8,128)(2,1)S(1)} %merge.1), channel_id=1, source_target_pairs={{0,7},{1,6},{2,5},{3,4},{4,3},{5,2},{6,1},{7,0},{8,15},{9,14},{10,... | collective-permute-start | bytes 301064 | tf_op jit(solution)/shard_map/ppermute | solution.py:189
  12.4 0.3 collective-permute-start.4
  12.7 0.4 %collective-permute-start.3 = (bf16[8,6272]{1,0:T(8,128)(2,1)S(1)}, bf16[8,6272]{1,0:T(8,128)(2,1)S(1)}, u32[]{:S(2)}, u32[]{:S(2)}) collective-permute-start(bf16[8,6272]{1,0:T(8,128)(2,1)S(1)} %merge.1), channel_id=1, source_target_pairs={{0,3},{1,2},{2,1},{3,0},{4,7},{5,6},{6,5},{7,4},{8,11},{9,10},{10,... | collective-permute-start | bytes 301064 | tf_op jit(solution)/shard_map/ppermute | solution.py:189
  13.1 2.9 %fetch.3 = (bf16[768,2048]{1,0:T(8,128)(2,1)S(1)}, bf16[1024,768]{1,0:T(8,128)(2,1)S(1)}, bf16[2048,768]{1,0:T(8,128)(2,1)S(1)}, bf16[768,1024]{1,0:T(8,128)(2,1)S(1)}) custom-call(bf16[768,2048]{1,0:T(8,128)(2,1)} %bitcast.7, bf16[2048,768]{1,0:T(8,128)(2,1)} %bitcast.5), custom_call_target="tpu_custom_call" | custom-call | bytes 9437184 | tf_op jit(solution)/shard_map/fetch/pallas_call | solution.py:401
  16.0 0.0 collective-permute-done.2
  16.0 0.3 collective-permute-start.5
  16.3 1.5 %collective-permute-done.4 = bf16[8,6272]{1,0:T(8,128)(2,1)S(1)} collective-permute-done((bf16[8,6272]{1,0:T(8,128)(2,1)S(1)}, bf16[8,6272]{1,0:T(8,128)(2,1)S(1)}, u32[]{:S(2)}, u32[]{:S(2)}) %collective-permute-start.4) | collective-permute-done | bytes 100384 | tf_op jit(solution)/shard_map/ppermute | solution.py:189
  17.8 0.2 collective-permute-start.7
  18.1 0.0 collective-permute-done.3
  18.1 0.3 collective-permute-start.6
  18.4 0.8 %collective-permute-done.7 = bf16[8,6272]{1,0:T(8,128)(2,1)S(1)} collective-permute-done((bf16[8,6272]{1,0:T(8,128)(2,1)S(1)}, bf16[8,6272]{1,0:T(8,128)(2,1)S(1)}, u32[]{:S(2)}, u32[]{:S(2)}) %collective-permute-start.7) | collective-permute-done | bytes 100384 | tf_op jit(solution)/shard_map/ppermute | solution.py:189
  19.1 0.2 collective-permute-done.6
  19.4 0.0 collective-permute-done.5.far_ref
  19.4 3.0 %experts.1 = (bf16[16,4096]{1,0:T(8,128)(2,1)S(1)}, bf16[16,4096]{1,0:T(8,128)(2,1)S(1)}, bf16[16,4096]{1,0:T(8,128)(2,1)S(1)}, bf16[16,4096]{1,0:T(8,128)(2,1)S(1)}) custom-call(bf16[16,6272]{1,0:T(8,128)(2,1)S(1)} %pad_maximum_fusion.near_ref, bf16[16,6272]{1,0:T(8,128)(2,1)S(1)} %pad_maximum_fusion.1.next_ref, ...), custom_call_target="tpu_custom_call" | custom-call | tf_op jit(solution)/shard_map/experts/pallas_call | solution.py:499
  22.4 0.3 collective-permute-start.8
  22.7 0.2 collective-permute-start.9
  23.0 0.8 %collective-permute-done.8 = bf16[16,4096]{1,0:T(8,128)(2,1)S(1)} collective-permute-done((bf16[16,4096]{1,0:T(8,128)(2,1)S(1)}, bf16[16,4096]{1,0:T(8,128)(2,1)S(1)}, u32[]{:S(2)}, u32[]{:S(2)}) %collective-permute-start.8) | collective-permute-done | bytes 131104 | tf_op jit(solution)/shard_map/ppermute | solution.py:189
  23.9 2.4 %collective-permute-start.12 = (bf16[8,4096]{1,0:T(8,128)(2,1)S(1)}, bf16[8,4096]{1,0:T(8,128)(2,1)S(1)}, u32[]{:S(2)}, u32[]{:S(2)}) collective-permute-start(bf16[8,4096]{1,0:T(8,128)(2,1)S(1)} %get-tuple-element.78), channel_id=1, source_target_pairs={{0,7},{1,6},{2,5},{3,4},{4,3},{5,2},{6,1},{7,0},{8,15},{9,14},{10,... | collective-permute-start | bytes 196616 | tf_op jit(solution)/shard_map/ppermute | solution.py:189
  26.3 0.5 %collective-permute-start.11 = (bf16[8,4096]{1,0:T(8,128)(2,1)S(1)}, bf16[8,4096]{1,0:T(8,128)(2,1)S(1)}, u32[]{:S(2)}, u32[]{:S(2)}) collective-permute-start(bf16[8,4096]{1,0:T(8,128)(2,1)S(1)} %get-tuple-element.80), channel_id=1, source_target_pairs={{0,5},{1,4},{2,7},{3,6},{4,1},{5,0},{6,3},{7,2},{8,13},{9,12},{10,... | collective-permute-start | bytes 196616 | tf_op jit(solution)/shard_map/ppermute | solution.py:189
  26.8 0.3 collective-permute-start.10
  27.1 1.9 %collective-permute-start.14 = (bf16[8,2560]{1,0:T(8,128)(2,1)S(1)}, bf16[8,2560]{1,0:T(8,128)(2,1)S(1)}, u32[]{:S(2)}, u32[]{:S(2)}) collective-permute-start(bf16[8,2560]{1,0:T(8,128)(2,1)S(1)} %widen.1), channel_id=1, source_target_pairs={{0,16},{1,17},{2,18},{3,19},{4,20},{5,21},{6,22},{7,23},{8,24},{9,... | collective-permute-start | bytes 122888 | tf_op jit(solution)/shard_map/ppermute | solution.py:189
  29.0 1.3 %collective-permute-done.11.c_ref = bf16[8,4096]{1,0:T(8,128)(2,1)S(1)} collective-permute-done((bf16[8,4096]{1,0:T(8,128)(2,1)S(1)}, bf16[8,4096]{1,0:T(8,128)(2,1)S(1)}, u32[]{:S(2)}, u32[]{:S(2)}) %collective-permute-start.11) | collective-permute-done | bytes 65568 | tf_op jit(solution)/shard_map/ppermute | solution.py:189
  30.3 0.5 %collective-permute-done.10.b_ref = bf16[8,4096]{1,0:T(8,128)(2,1)S(1)} collective-permute-done((bf16[8,4096]{1,0:T(8,128)(2,1)S(1)}, bf16[8,4096]{1,0:T(8,128)(2,1)S(1)}, u32[]{:S(2)}, u32[]{:S(2)}) %collective-permute-start.10) | collective-permute-done | bytes 65568 | tf_op jit(solution)/shard_map/ppermute | solution.py:189
  30.9 3.3 %collective-permute-start.13 = (bf16[8,2048]{1,0:T(8,128)(2,1)S(1)}, bf16[8,2048]{1,0:T(8,128)(2,1)S(1)}, u32[]{:S(2)}, u32[]{:S(2)}) collective-permute-start(bf16[8,2048]{1,0:T(8,128)(2,1)S(1)} %get-tuple-element.71), channel_id=1, source_target_pairs={{0,25},{1,24},{2,27},{3,26},{4,29},{5,28},{6,31},{7,30},{8,17},{9,... | collective-permute-start | bytes 98312 | tf_op jit(solution)/shard_map/ppermute | solution.py:189
  34.2 0.1 endings.1
  34.3 1.8 %collective-permute-done.13.other_ref = bf16[8,2048]{1,0:T(8,128)(2,1)S(1)} collective-permute-done((bf16[8,2048]{1,0:T(8,128)(2,1)S(1)}, bf16[8,2048]{1,0:T(8,128)(2,1)S(1)}, u32[]{:S(2)}, u32[]{:S(2)}) %collective-permute-start.13) | collective-permute-done | bytes 32800 | tf_op jit(solution)/shard_map/ppermute | solution.py:189
  36.1 0.7 %finish.1 = (bf16[1,8,2048]{2,1,0:T(8,128)(2,1)}, bf16[1,8,2048]{2,1,0:T(8,128)(2,1)}) custom-call(f32[8,2048]{1,0:T(8,128)S(1)} %get-tuple-element.70.staying_ref, bf16[8,2048]{1,0:T(8,128)(2,1)S(1)} %collective-permute-done.13.other_ref, f32[8,2048]{1,0:T(8,128)S(1)} %get-tuple-element.74.scale_ref, f32[8,2048]{1,0:T(8,128)S(1)} %get-tuple-element.75.towards_ref, ...), custom_call_target="tpu_custom_call" | custom-call | tf_op jit(solution)/shard_map/finish/pallas_call | solution.py:360
  (14 shorter events, 0.2 us)
Async XLA Ops:
  1.6 8.1 %collective-permute-start = (bf16[8,4224]{1,0:T(8,128)(2,1)S(1)}, bf16[8,4224]{1,0:T(8,128)(2,1)S(1)}, u32[]{:S(2)}, u32[]{:S(2)}) collective-permute-start(bf16[8,4224]{1,0:T(8,128)(2,1)S(1)} %get-tuple-element.40), channel_id=1, source_target_pairs={{0,9},{1,8},{2,11},{3,10},{4,13},{5,12},{6,15},{7,14},{8,1},{9,0},... | collective-permute-start | bytes 202760 | tf_op jit(solution)/shard_map/ppermute | solution.py:189
  5.2 4.7 %collective-permute-start.1 = (bf16[8,4224]{1,0:T(8,128)(2,1)S(1)}, bf16[8,4224]{1,0:T(8,128)(2,1)S(1)}, u32[]{:S(2)}, u32[]{:S(2)}) collective-permute-start(bf16[8,4224]{1,0:T(8,128)(2,1)S(1)} %get-tuple-element.40), channel_id=1, source_target_pairs={{0,16},{1,17},{2,18},{3,19},{4,20},{5,21},{6,22},{7,23},{8,24},{9,... | collective-permute-start | bytes 202760 | tf_op jit(solution)/shard_map/ppermute | solution.py:189
  9.9 6.1 %collective-permute-start.2 = (bf16[8,6272]{1,0:T(8,128)(2,1)S(1)}, bf16[8,6272]{1,0:T(8,128)(2,1)S(1)}, u32[]{:S(2)}, u32[]{:S(2)}) collective-permute-start(bf16[8,6272]{1,0:T(8,128)(2,1)S(1)} %merge.1), channel_id=1, source_target_pairs={{0,7},{1,6},{2,5},{3,4},{4,3},{5,2},{6,1},{7,0},{8,15},{9,14},{10,... | collective-permute-start | bytes 301064 | tf_op jit(solution)/shard_map/ppermute | solution.py:189
  12.4 5.4 %collective-permute-start.4 = (bf16[8,6272]{1,0:T(8,128)(2,1)S(1)}, bf16[8,6272]{1,0:T(8,128)(2,1)S(1)}, u32[]{:S(2)}, u32[]{:S(2)}) collective-permute-start(bf16[8,6272]{1,0:T(8,128)(2,1)S(1)} %merge.1), channel_id=1, source_target_pairs={{0,5},{1,4},{2,7},{3,6},{4,1},{5,0},{6,3},{7,2},{8,13},{9,12},{10,... | collective-permute-start | bytes 301064 | tf_op jit(solution)/shard_map/ppermute | solution.py:189
  12.7 5.4 %collective-permute-start.3 = (bf16[8,6272]{1,0:T(8,128)(2,1)S(1)}, bf16[8,6272]{1,0:T(8,128)(2,1)S(1)}, u32[]{:S(2)}, u32[]{:S(2)}) collective-permute-start(bf16[8,6272]{1,0:T(8,128)(2,1)S(1)} %merge.1), channel_id=1, source_target_pairs={{0,3},{1,2},{2,1},{3,0},{4,7},{5,6},{6,5},{7,4},{8,11},{9,10},{10,... | collective-permute-start | bytes 301064 | tf_op jit(solution)/shard_map/ppermute | solution.py:189
  16.0 3.4 %collective-permute-start.5 = (bf16[16,6272]{1,0:T(8,128)(2,1)S(1)}, bf16[16,6272]{1,0:T(8,128)(2,1)S(1)}, u32[]{:S(2)}, u32[]{:S(2)}) collective-permute-start(bf16[16,6272]{1,0:T(8,128)(2,1)S(1)} %pad_maximum_fusion.near_ref), channel_id=1, source_target_pairs={{0,1},{1,0},{2,3},{3,2},{4,5},{5,4},{6,7},{7,6},{8,9},{9,8},{10,11... | collective-permute-start | bytes 602120 | tf_op jit(solution)/shard_map/ppermute | solution.py:189
  17.8 1.3 %collective-permute-start.7 = (bf16[8,6272]{1,0:T(8,128)(2,1)S(1)}, bf16[8,6272]{1,0:T(8,128)(2,1)S(1)}, u32[]{:S(2)}, u32[]{:S(2)}) collective-permute-start(bf16[8,6272]{1,0:T(8,128)(2,1)S(1)} %collective-permute-done.4), channel_id=1, source_target_pairs={{0,1},{1,0},{2,3},{3,2},{4,5},{5,4},{6,7},{7,6},{8,9},{9,8},{10,11... | collective-permute-start | bytes 301064 | tf_op jit(solution)/shard_map/ppermute | solution.py:189
  18.1 1.3 %collective-permute-start.6 = (bf16[8,6272]{1,0:T(8,128)(2,1)S(1)}, bf16[8,6272]{1,0:T(8,128)(2,1)S(1)}, u32[]{:S(2)}, u32[]{:S(2)}) collective-permute-start(bf16[8,6272]{1,0:T(8,128)(2,1)S(1)} %collective-permute-done.3), channel_id=1, source_target_pairs={{0,1},{1,0},{2,3},{3,2},{4,5},{5,4},{6,7},{7,6},{8,9},{9,8},{10,11... | collective-permute-start | bytes 301064 | tf_op jit(solution)/shard_map/ppermute | solution.py:189
  22.4 1.4 %collective-permute-start.8 = (bf16[16,4096]{1,0:T(8,128)(2,1)S(1)}, bf16[16,4096]{1,0:T(8,128)(2,1)S(1)}, u32[]{:S(2)}, u32[]{:S(2)}) collective-permute-start(bf16[16,4096]{1,0:T(8,128)(2,1)S(1)} %get-tuple-element.65), channel_id=1, source_target_pairs={{0,1},{1,0},{2,3},{3,2},{4,5},{5,4},{6,7},{7,6},{8,9},{9,8},{10,11... | collective-permute-start | bytes 393224 | tf_op jit(solution)/shard_map/ppermute | solution.py:189
  22.7 3.5 %collective-permute-start.9 = (bf16[16,4096]{1,0:T(8,128)(2,1)S(1)}, bf16[16,4096]{1,0:T(8,128)(2,1)S(1)}, u32[]{:S(2)}, u32[]{:S(2)}) collective-permute-start(bf16[16,4096]{1,0:T(8,128)(2,1)S(1)} %get-tuple-element.68), channel_id=1, source_target_pairs={{0,1},{1,0},{2,3},{3,2},{4,5},{5,4},{6,7},{7,6},{8,9},{9,8},{10,11... | collective-permute-start | bytes 393224 | tf_op jit(solution)/shard_map/ppermute | solution.py:189
  23.9 5.2 %collective-permute-start.12 = (bf16[8,4096]{1,0:T(8,128)(2,1)S(1)}, bf16[8,4096]{1,0:T(8,128)(2,1)S(1)}, u32[]{:S(2)}, u32[]{:S(2)}) collective-permute-start(bf16[8,4096]{1,0:T(8,128)(2,1)S(1)} %get-tuple-element.78), channel_id=1, source_target_pairs={{0,7},{1,6},{2,5},{3,4},{4,3},{5,2},{6,1},{7,0},{8,15},{9,14},{10,... | collective-permute-start | bytes 196616 | tf_op jit(solution)/shard_map/ppermute | solution.py:189
  26.3 4.0 %collective-permute-start.11 = (bf16[8,4096]{1,0:T(8,128)(2,1)S(1)}, bf16[8,4096]{1,0:T(8,128)(2,1)S(1)}, u32[]{:S(2)}, u32[]{:S(2)}) collective-permute-start(bf16[8,4096]{1,0:T(8,128)(2,1)S(1)} %get-tuple-element.80), channel_id=1, source_target_pairs={{0,5},{1,4},{2,7},{3,6},{4,1},{5,0},{6,3},{7,2},{8,13},{9,12},{10,... | collective-permute-start | bytes 196616 | tf_op jit(solution)/shard_map/ppermute | solution.py:189
  26.8 4.0 %collective-permute-start.10 = (bf16[8,4096]{1,0:T(8,128)(2,1)S(1)}, bf16[8,4096]{1,0:T(8,128)(2,1)S(1)}, u32[]{:S(2)}, u32[]{:S(2)}) collective-permute-start(bf16[8,4096]{1,0:T(8,128)(2,1)S(1)} %get-tuple-element.81), channel_id=1, source_target_pairs={{0,3},{1,2},{2,1},{3,0},{4,7},{5,6},{6,5},{7,4},{8,11},{9,10},{10,... | collective-permute-start | bytes 196616 | tf_op jit(solution)/shard_map/ppermute | solution.py:189
  27.1 7.0 %collective-permute-start.14 = (bf16[8,2560]{1,0:T(8,128)(2,1)S(1)}, bf16[8,2560]{1,0:T(8,128)(2,1)S(1)}, u32[]{:S(2)}, u32[]{:S(2)}) collective-permute-start(bf16[8,2560]{1,0:T(8,128)(2,1)S(1)} %widen.1), channel_id=1, source_target_pairs={{0,16},{1,17},{2,18},{3,19},{4,20},{5,21},{6,22},{7,23},{8,24},{9,... | collective-permute-start | bytes 122888 | tf_op jit(solution)/shard_map/ppermute | solution.py:189
  30.9 5.2 %collective-permute-start.13 = (bf16[8,2048]{1,0:T(8,128)(2,1)S(1)}, bf16[8,2048]{1,0:T(8,128)(2,1)S(1)}, u32[]{:S(2)}, u32[]{:S(2)}) collective-permute-start(bf16[8,2048]{1,0:T(8,128)(2,1)S(1)} %get-tuple-element.71), channel_id=1, source_target_pairs={{0,25},{1,24},{2,27},{3,26},{4,29},{5,28},{6,31},{7,30},{8,17},{9,... | collective-permute-start | bytes 98312 | tf_op jit(solution)/shard_map/ppermute | solution.py:189

commit v9 on v8

--- a/solution.py
+++ b/solution.py
@@ -543,7 +543,7 @@
     )
     across = swapped(own, SECTION)
     along = swapped(own, HALF)
-    cuts = (width // 2, width)
+    cuts = (3 * width // 8, width)
     gate_hbm, up_hbm, down_hbm = w_gate[0], w_up[0], w_down[0]
     gate_mats, *ups = fetched((gate_hbm, 0, width), (up_hbm, 0, cuts[0]))
     along, gate_mats, ups = lax.optimization_barrier((along, gate_mats, ups))

time: 37 us -> 37.3 us (level)
  transfers between devices with their start and end apart: 15 -> 15, of which waited for: 8 -> 8; matrix products, arithmetic and copies ran while one was open for 0% -> 0% of each run, Pallas kernels for 17% -> 16%
where the time goes in v9:
time: 37.3 us; the launch traced here: 37.1 us
  starting transfers between devices  17.8 us (48%)
  Pallas kernels  11.1 us (30%)
  waiting for transfers between devices  7.35 us (20%)
  between operations  0.75 us (2%)
    ppermute x15, starting transfers between devices, swapped(): return lax.ppermute(block, AXES, [(i, i ^ distance) for i in range(count)])  17.8 us
    ppermute x15, waiting for transfers between devices, swapped(): return lax.ppermute(block, AXES, [(i, i ^ distance) for i in range(count)])  7.35 us
    pallas_call x2, Pallas kernels, fetched(): pl.pallas_call(functools.partial(fetch_kernel, parts=sizes), out_shape=he...  5.93 us
    pallas_call x1, Pallas kernels, run_experts(): pl.pallas_call(expert_kernel, out_shape=[jax.ShapeDtypeStruct((b.shape[0]...  3.25 us
    pallas_call x1, Pallas kernels, pack_rows(): pl.pallas_call(pack_kernel, out_shape=[jax.ShapeDtypeStruct((count, 2 * w...  1 us
  transfers between devices with their start and end apart: 15, of which 8 were waited for; matrix products, arithmetic and copies ran while one was open for 0% of the time, Pallas kernels for 16%

profile of v9, /device:TPU:0, one launch (start us, length us, event | category | flops | bytes accessed | tf_op | source)
XLA Modules:
  0.0 37.1 jit_solution(16467830638158244941)
XLA Ops:
  0.6 1.0 %pack.1 = (bf16[8,4224]{1,0:T(8,128)(2,1)S(1)}, bf16[8,2048]{1,0:T(8,128)(2,1)S(1)}, f32[1,2048]{1,0:T(1,128)S(1)}, bf16[16,2048]{1,0:T(8,128)(2,1)S(1)}) custom-call(bf16[1,8,2048]{2,1,0:T(8,128)(2,1)} %fwd_act.1, s32[1,8,8]{2,1,0:T(8,128)} %fwd_routes.1, bf16[1,8,2048]{2,1,0:T(8,128)(2,1)} %bwd_saved.1, bf16[1,8,2048]{2,1,0:T(8,128)(2,1)} %bwd_grad.1, ...), custom_call_target="tpu_custom_call" | custom-call | tf_op jit(solution)/shard_map/pack/pallas_call | solution.py:251
  1.6 3.5 %collective-permute-start = (bf16[8,4224]{1,0:T(8,128)(2,1)S(1)}, bf16[8,4224]{1,0:T(8,128)(2,1)S(1)}, u32[]{:S(2)}, u32[]{:S(2)}) collective-permute-start(bf16[8,4224]{1,0:T(8,128)(2,1)S(1)} %get-tuple-element.40), channel_id=1, source_target_pairs={{0,9},{1,8},{2,11},{3,10},{4,13},{5,12},{6,15},{7,14},{8,1},{9,0},... | collective-permute-start | bytes 202760 | tf_op jit(solution)/shard_map/ppermute | solution.py:189
  5.2 1.5 %collective-permute-start.1 = (bf16[8,4224]{1,0:T(8,128)(2,1)S(1)}, bf16[8,4224]{1,0:T(8,128)(2,1)S(1)}, u32[]{:S(2)}, u32[]{:S(2)}) collective-permute-start(bf16[8,4224]{1,0:T(8,128)(2,1)S(1)} %get-tuple-element.40), channel_id=1, source_target_pairs={{0,16},{1,17},{2,18},{3,19},{4,20},{5,21},{6,22},{7,23},{8,24},{9,... | collective-permute-start | bytes 202760 | tf_op jit(solution)/shard_map/ppermute | solution.py:189
  6.7 2.9 %fetch.2 = (bf16[2048,768]{1,0:T(8,128)(2,1)S(1)}, bf16[768,768]{1,0:T(8,128)(2,1)S(1)}, bf16[768,2048]{1,0:T(8,128)(2,1)S(1)}, bf16[768,768]{1,0:T(8,128)(2,1)S(1)}) custom-call(bf16[2048,768]{1,0:T(8,128)(2,1)} %bitcast.6, bf16[2048,768]{1,0:T(8,128)(2,1)} %bitcast.4), custom_call_target="tpu_custom_call" | custom-call | bytes 8650752 | tf_op jit(solution)/shard_map/fetch/pallas_call | solution.py:401
  9.6 0.0 collective-permute-done.along_ref
  9.6 0.3 collective-permute-done.1.across_ref
  9.9 2.3 %collective-permute-start.2 = (bf16[8,6272]{1,0:T(8,128)(2,1)S(1)}, bf16[8,6272]{1,0:T(8,128)(2,1)S(1)}, u32[]{:S(2)}, u32[]{:S(2)}) collective-permute-start(bf16[8,6272]{1,0:T(8,128)(2,1)S(1)} %merge.1), channel_id=1, source_target_pairs={{0,7},{1,6},{2,5},{3,4},{4,3},{5,2},{6,1},{7,0},{8,15},{9,14},{10,... | collective-permute-start | bytes 301064 | tf_op jit(solution)/shard_map/ppermute | solution.py:189
  12.2 0.5 %collective-permute-start.4 = (bf16[8,6272]{1,0:T(8,128)(2,1)S(1)}, bf16[8,6272]{1,0:T(8,128)(2,1)S(1)}, u32[]{:S(2)}, u32[]{:S(2)}) collective-permute-start(bf16[8,6272]{1,0:T(8,128)(2,1)S(1)} %merge.1), channel_id=1, source_target_pairs={{0,5},{1,4},{2,7},{3,6},{4,1},{5,0},{6,3},{7,2},{8,13},{9,12},{10,... | collective-permute-start | bytes 301064 | tf_op jit(solution)/shard_map/ppermute | solution.py:189
  12.7 0.2 collective-permute-start.3
  12.9 3.1 %fetch.3 = (bf16[768,2048]{1,0:T(8,128)(2,1)S(1)}, bf16[1280,768]{1,0:T(8,128)(2,1)S(1)}, bf16[2048,768]{1,0:T(8,128)(2,1)S(1)}, bf16[768,1280]{1,0:T(8,128)(2,1)S(1)}) custom-call(bf16[768,2048]{1,0:T(8,128)(2,1)} %bitcast.7, bf16[2048,768]{1,0:T(8,128)(2,1)} %bitcast.5), custom_call_target="tpu_custom_call" | custom-call | bytes 10223616 | tf_op jit(solution)/shard_map/fetch/pallas_call | solution.py:401
  15.9 0.0 collective-permute-done.2
  16.0 0.5 %collective-permute-start.5 = (bf16[16,6272]{1,0:T(8,128)(2,1)S(1)}, bf16[16,6272]{1,0:T(8,128)(2,1)S(1)}, u32[]{:S(2)}, u32[]{:S(2)}) collective-permute-start(bf16[16,6272]{1,0:T(8,128)(2,1)S(1)} %pad_maximum_fusion.near_ref), channel_id=1, source_target_pairs={{0,1},{1,0},{2,3},{3,2},{4,5},{5,4},{6,7},{7,6},{8,9},{9,8},{10,11... | collective-permute-start | bytes 602120 | tf_op jit(solution)/shard_map/ppermute | solution.py:189
  16.5 1.5 %collective-permute-done.4 = bf16[8,6272]{1,0:T(8,128)(2,1)S(1)} collective-permute-done((bf16[8,6272]{1,0:T(8,128)(2,1)S(1)}, bf16[8,6272]{1,0:T(8,128)(2,1)S(1)}, u32[]{:S(2)}, u32[]{:S(2)}) %collective-permute-start.4) | collective-permute-done | bytes 100384 | tf_op jit(solution)/shard_map/ppermute | solution.py:189
  17.9 0.2 collective-permute-start.7
  18.2 0.3 collective-permute-start.6
  18.5 0.8 %collective-permute-done.7 = bf16[8,6272]{1,0:T(8,128)(2,1)S(1)} collective-permute-done((bf16[8,6272]{1,0:T(8,128)(2,1)S(1)}, bf16[8,6272]{1,0:T(8,128)(2,1)S(1)}, u32[]{:S(2)}, u32[]{:S(2)}) %collective-permute-start.7) | collective-permute-done | bytes 100384 | tf_op jit(solution)/shard_map/ppermute | solution.py:189
  19.3 0.2 collective-permute-done.6
  19.5 3.3 %experts.1 = (bf16[16,4096]{1,0:T(8,128)(2,1)S(1)}, bf16[16,4096]{1,0:T(8,128)(2,1)S(1)}, bf16[16,4096]{1,0:T(8,128)(2,1)S(1)}, bf16[16,4096]{1,0:T(8,128)(2,1)S(1)}) custom-call(bf16[16,6272]{1,0:T(8,128)(2,1)S(1)} %pad_maximum_fusion.near_ref, bf16[16,6272]{1,0:T(8,128)(2,1)S(1)} %pad_maximum_fusion.1.next_ref, ...), custom_call_target="tpu_custom_call" | custom-call | tf_op jit(solution)/shard_map/experts/pallas_call | solution.py:499
  22.8 0.3 collective-permute-start.8
  23.1 0.2 collective-permute-start.9
  23.4 0.8 %collective-permute-done.8 = bf16[16,4096]{1,0:T(8,128)(2,1)S(1)} collective-permute-done((bf16[16,4096]{1,0:T(8,128)(2,1)S(1)}, bf16[16,4096]{1,0:T(8,128)(2,1)S(1)}, u32[]{:S(2)}, u32[]{:S(2)}) %collective-permute-start.8) | collective-permute-done | bytes 131104 | tf_op jit(solution)/shard_map/ppermute | solution.py:189
  24.2 2.3 %collective-permute-start.12 = (bf16[8,4096]{1,0:T(8,128)(2,1)S(1)}, bf16[8,4096]{1,0:T(8,128)(2,1)S(1)}, u32[]{:S(2)}, u32[]{:S(2)}) collective-permute-start(bf16[8,4096]{1,0:T(8,128)(2,1)S(1)} %get-tuple-element.78), channel_id=1, source_target_pairs={{0,7},{1,6},{2,5},{3,4},{4,3},{5,2},{6,1},{7,0},{8,15},{9,14},{10,... | collective-permute-start | bytes 196616 | tf_op jit(solution)/shard_map/ppermute | solution.py:189
  26.6 0.5 %collective-permute-start.11 = (bf16[8,4096]{1,0:T(8,128)(2,1)S(1)}, bf16[8,4096]{1,0:T(8,128)(2,1)S(1)}, u32[]{:S(2)}, u32[]{:S(2)}) collective-permute-start(bf16[8,4096]{1,0:T(8,128)(2,1)S(1)} %get-tuple-element.80), channel_id=1, source_target_pairs={{0,5},{1,4},{2,7},{3,6},{4,1},{5,0},{6,3},{7,2},{8,13},{9,12},{10,... | collective-permute-start | bytes 196616 | tf_op jit(solution)/shard_map/ppermute | solution.py:189
  27.1 0.4 %collective-permute-start.10 = (bf16[8,4096]{1,0:T(8,128)(2,1)S(1)}, bf16[8,4096]{1,0:T(8,128)(2,1)S(1)}, u32[]{:S(2)}, u32[]{:S(2)}) collective-permute-start(bf16[8,4096]{1,0:T(8,128)(2,1)S(1)} %get-tuple-element.81), channel_id=1, source_target_pairs={{0,3},{1,2},{2,1},{3,0},{4,7},{5,6},{6,5},{7,4},{8,11},{9,10},{10,... | collective-permute-start | bytes 196616 | tf_op jit(solution)/shard_map/ppermute | solution.py:189
  27.5 1.7 %collective-permute-start.14 = (bf16[8,2560]{1,0:T(8,128)(2,1)S(1)}, bf16[8,2560]{1,0:T(8,128)(2,1)S(1)}, u32[]{:S(2)}, u32[]{:S(2)}) collective-permute-start(bf16[8,2560]{1,0:T(8,128)(2,1)S(1)} %widen.1), channel_id=1, source_target_pairs={{0,16},{1,17},{2,18},{3,19},{4,20},{5,21},{6,22},{7,23},{8,24},{9,... | collective-permute-start | bytes 122888 | tf_op jit(solution)/shard_map/ppermute | solution.py:189
  29.3 1.3 %collective-permute-done.11.c_ref = bf16[8,4096]{1,0:T(8,128)(2,1)S(1)} collective-permute-done((bf16[8,4096]{1,0:T(8,128)(2,1)S(1)}, bf16[8,4096]{1,0:T(8,128)(2,1)S(1)}, u32[]{:S(2)}, u32[]{:S(2)}) %collective-permute-start.11) | collective-permute-done | bytes 65568 | tf_op jit(solution)/shard_map/ppermute | solution.py:189
  30.6 0.5 %collective-permute-done.10.b_ref = bf16[8,4096]{1,0:T(8,128)(2,1)S(1)} collective-permute-done((bf16[8,4096]{1,0:T(8,128)(2,1)S(1)}, bf16[8,4096]{1,0:T(8,128)(2,1)S(1)}, u32[]{:S(2)}, u32[]{:S(2)}) %collective-permute-start.10) | collective-permute-done | bytes 65568 | tf_op jit(solution)/shard_map/ppermute | solution.py:189
  31.2 3.3 %collective-permute-start.13 = (bf16[8,2048]{1,0:T(8,128)(2,1)S(1)}, bf16[8,2048]{1,0:T(8,128)(2,1)S(1)}, u32[]{:S(2)}, u32[]{:S(2)}) collective-permute-start(bf16[8,2048]{1,0:T(8,128)(2,1)S(1)} %get-tuple-element.71), channel_id=1, source_target_pairs={{0,25},{1,24},{2,27},{3,26},{4,29},{5,28},{6,31},{7,30},{8,17},{9,... | collective-permute-start | bytes 98312 | tf_op jit(solution)/shard_map/ppermute | solution.py:189
  34.4 0.0 collective-permute-done.14.raw_ref
  34.5 0.1 endings.1
  34.6 1.8 %collective-permute-done.13.other_ref = bf16[8,2048]{1,0:T(8,128)(2,1)S(1)} collective-permute-done((bf16[8,2048]{1,0:T(8,128)(2,1)S(1)}, bf16[8,2048]{1,0:T(8,128)(2,1)S(1)}, u32[]{:S(2)}, u32[]{:S(2)}) %collective-permute-start.13) | collective-permute-done | bytes 32800 | tf_op jit(solution)/shard_map/ppermute | solution.py:189
  36.4 0.7 %finish.1 = (bf16[1,8,2048]{2,1,0:T(8,128)(2,1)}, bf16[1,8,2048]{2,1,0:T(8,128)(2,1)}) custom-call(f32[8,2048]{1,0:T(8,128)S(1)} %get-tuple-element.70.staying_ref, bf16[8,2048]{1,0:T(8,128)(2,1)S(1)} %collective-permute-done.13.other_ref, f32[8,2048]{1,0:T(8,128)S(1)} %get-tuple-element.74.scale_ref, f32[8,2048]{1,0:T(8,128)S(1)} %get-tuple-element.75.towards_ref, ...), custom_call_target="tpu_custom_call" | custom-call | tf_op jit(solution)/shard_map/finish/pallas_call | solution.py:360
  (14 shorter events, 0.2 us)
Async XLA Ops:
  1.6 7.9 %collective-permute-start = (bf16[8,4224]{1,0:T(8,128)(2,1)S(1)}, bf16[8,4224]{1,0:T(8,128)(2,1)S(1)}, u32[]{:S(2)}, u32[]{:S(2)}) collective-permute-start(bf16[8,4224]{1,0:T(8,128)(2,1)S(1)} %get-tuple-element.40), channel_id=1, source_target_pairs={{0,9},{1,8},{2,11},{3,10},{4,13},{5,12},{6,15},{7,14},{8,1},{9,0},... | collective-permute-start | bytes 202760 | tf_op jit(solution)/shard_map/ppermute | solution.py:189
  5.2 4.7 %collective-permute-start.1 = (bf16[8,4224]{1,0:T(8,128)(2,1)S(1)}, bf16[8,4224]{1,0:T(8,128)(2,1)S(1)}, u32[]{:S(2)}, u32[]{:S(2)}) collective-permute-start(bf16[8,4224]{1,0:T(8,128)(2,1)S(1)} %get-tuple-element.40), channel_id=1, source_target_pairs={{0,16},{1,17},{2,18},{3,19},{4,20},{5,21},{6,22},{7,23},{8,24},{9,... | collective-permute-start | bytes 202760 | tf_op jit(solution)/shard_map/ppermute | solution.py:189
  9.9 6.0 %collective-permute-start.2 = (bf16[8,6272]{1,0:T(8,128)(2,1)S(1)}, bf16[8,6272]{1,0:T(8,128)(2,1)S(1)}, u32[]{:S(2)}, u32[]{:S(2)}) collective-permute-start(bf16[8,6272]{1,0:T(8,128)(2,1)S(1)} %merge.1), channel_id=1, source_target_pairs={{0,7},{1,6},{2,5},{3,4},{4,3},{5,2},{6,1},{7,0},{8,15},{9,14},{10,... | collective-permute-start | bytes 301064 | tf_op jit(solution)/shard_map/ppermute | solution.py:189
  12.2 5.7 %collective-permute-start.4 = (bf16[8,6272]{1,0:T(8,128)(2,1)S(1)}, bf16[8,6272]{1,0:T(8,128)(2,1)S(1)}, u32[]{:S(2)}, u32[]{:S(2)}) collective-permute-start(bf16[8,6272]{1,0:T(8,128)(2,1)S(1)} %merge.1), channel_id=1, source_target_pairs={{0,5},{1,4},{2,7},{3,6},{4,1},{5,0},{6,3},{7,2},{8,13},{9,12},{10,... | collective-permute-start | bytes 301064 | tf_op jit(solution)/shard_map/ppermute | solution.py:189
  12.7 5.5 %collective-permute-start.3 = (bf16[8,6272]{1,0:T(8,128)(2,1)S(1)}, bf16[8,6272]{1,0:T(8,128)(2,1)S(1)}, u32[]{:S(2)}, u32[]{:S(2)}) collective-permute-start(bf16[8,6272]{1,0:T(8,128)(2,1)S(1)} %merge.1), channel_id=1, source_target_pairs={{0,3},{1,2},{2,1},{3,0},{4,7},{5,6},{6,5},{7,4},{8,11},{9,10},{10,... | collective-permute-start | bytes 301064 | tf_op jit(solution)/shard_map/ppermute | solution.py:189
  16.0 3.5 %collective-permute-start.5 = (bf16[16,6272]{1,0:T(8,128)(2,1)S(1)}, bf16[16,6272]{1,0:T(8,128)(2,1)S(1)}, u32[]{:S(2)}, u32[]{:S(2)}) collective-permute-start(bf16[16,6272]{1,0:T(8,128)(2,1)S(1)} %pad_maximum_fusion.near_ref), channel_id=1, source_target_pairs={{0,1},{1,0},{2,3},{3,2},{4,5},{5,4},{6,7},{7,6},{8,9},{9,8},{10,11... | collective-permute-start | bytes 602120 | tf_op jit(solution)/shard_map/ppermute | solution.py:189
  17.9 1.3 %collective-permute-start.7 = (bf16[8,6272]{1,0:T(8,128)(2,1)S(1)}, bf16[8,6272]{1,0:T(8,128)(2,1)S(1)}, u32[]{:S(2)}, u32[]{:S(2)}) collective-permute-start(bf16[8,6272]{1,0:T(8,128)(2,1)S(1)} %collective-permute-done.4), channel_id=1, source_target_pairs={{0,1},{1,0},{2,3},{3,2},{4,5},{5,4},{6,7},{7,6},{8,9},{9,8},{10,11... | collective-permute-start | bytes 301064 | tf_op jit(solution)/shard_map/ppermute | solution.py:189
  18.2 1.3 %collective-permute-start.6 = (bf16[8,6272]{1,0:T(8,128)(2,1)S(1)}, bf16[8,6272]{1,0:T(8,128)(2,1)S(1)}, u32[]{:S(2)}, u32[]{:S(2)}) collective-permute-start(bf16[8,6272]{1,0:T(8,128)(2,1)S(1)} %collective-permute-done.3), channel_id=1, source_target_pairs={{0,1},{1,0},{2,3},{3,2},{4,5},{5,4},{6,7},{7,6},{8,9},{9,8},{10,11... | collective-permute-start | bytes 301064 | tf_op jit(solution)/shard_map/ppermute | solution.py:189
  22.8 1.4 %collective-permute-start.8 = (bf16[16,4096]{1,0:T(8,128)(2,1)S(1)}, bf16[16,4096]{1,0:T(8,128)(2,1)S(1)}, u32[]{:S(2)}, u32[]{:S(2)}) collective-permute-start(bf16[16,4096]{1,0:T(8,128)(2,1)S(1)} %get-tuple-element.65), channel_id=1, source_target_pairs={{0,1},{1,0},{2,3},{3,2},{4,5},{5,4},{6,7},{7,6},{8,9},{9,8},{10,11... | collective-permute-start | bytes 393224 | tf_op jit(solution)/shard_map/ppermute | solution.py:189
  23.1 3.5 %collective-permute-start.9 = (bf16[16,4096]{1,0:T(8,128)(2,1)S(1)}, bf16[16,4096]{1,0:T(8,128)(2,1)S(1)}, u32[]{:S(2)}, u32[]{:S(2)}) collective-permute-start(bf16[16,4096]{1,0:T(8,128)(2,1)S(1)} %get-tuple-element.68), channel_id=1, source_target_pairs={{0,1},{1,0},{2,3},{3,2},{4,5},{5,4},{6,7},{7,6},{8,9},{9,8},{10,11... | collective-permute-start | bytes 393224 | tf_op jit(solution)/shard_map/ppermute | solution.py:189
  24.2 5.0 %collective-permute-start.12 = (bf16[8,4096]{1,0:T(8,128)(2,1)S(1)}, bf16[8,4096]{1,0:T(8,128)(2,1)S(1)}, u32[]{:S(2)}, u32[]{:S(2)}) collective-permute-start(bf16[8,4096]{1,0:T(8,128)(2,1)S(1)} %get-tuple-element.78), channel_id=1, source_target_pairs={{0,7},{1,6},{2,5},{3,4},{4,3},{5,2},{6,1},{7,0},{8,15},{9,14},{10,... | collective-permute-start | bytes 196616 | tf_op jit(solution)/shard_map/ppermute | solution.py:189
  26.6 4.0 %collective-permute-start.11 = (bf16[8,4096]{1,0:T(8,128)(2,1)S(1)}, bf16[8,4096]{1,0:T(8,128)(2,1)S(1)}, u32[]{:S(2)}, u32[]{:S(2)}) collective-permute-start(bf16[8,4096]{1,0:T(8,128)(2,1)S(1)} %get-tuple-element.80), channel_id=1, source_target_pairs={{0,5},{1,4},{2,7},{3,6},{4,1},{5,0},{6,3},{7,2},{8,13},{9,12},{10,... | collective-permute-start | bytes 196616 | tf_op jit(solution)/shard_map/ppermute | solution.py:189
  27.1 4.1 %collective-permute-start.10 = (bf16[8,4096]{1,0:T(8,128)(2,1)S(1)}, bf16[8,4096]{1,0:T(8,128)(2,1)S(1)}, u32[]{:S(2)}, u32[]{:S(2)}) collective-permute-start(bf16[8,4096]{1,0:T(8,128)(2,1)S(1)} %get-tuple-element.81), channel_id=1, source_target_pairs={{0,3},{1,2},{2,1},{3,0},{4,7},{5,6},{6,5},{7,4},{8,11},{9,10},{10,... | collective-permute-start | bytes 196616 | tf_op jit(solution)/shard_map/ppermute | solution.py:189
  27.5 6.9 %collective-permute-start.14 = (bf16[8,2560]{1,0:T(8,128)(2,1)S(1)}, bf16[8,2560]{1,0:T(8,128)(2,1)S(1)}, u32[]{:S(2)}, u32[]{:S(2)}) collective-permute-start(bf16[8,2560]{1,0:T(8,128)(2,1)S(1)} %widen.1), channel_id=1, source_target_pairs={{0,16},{1,17},{2,18},{3,19},{4,20},{5,21},{6,22},{7,23},{8,24},{9,... | collective-permute-start | bytes 122888 | tf_op jit(solution)/shard_map/ppermute | solution.py:189
  31.2 5.2 %collective-permute-start.13 = (bf16[8,2048]{1,0:T(8,128)(2,1)S(1)}, bf16[8,2048]{1,0:T(8,128)(2,1)S(1)}, u32[]{:S(2)}, u32[]{:S(2)}) collective-permute-start(bf16[8,2048]{1,0:T(8,128)(2,1)S(1)} %get-tuple-element.71), channel_id=1, source_target_pairs={{0,25},{1,24},{2,27},{3,26},{4,29},{5,28},{6,31},{7,30},{8,17},{9,... | collective-permute-start | bytes 98312 | tf_op jit(solution)/shard_map/ppermute | solution.py:189
